TPU v7x, 256 devices: a whole 4x4x8 slice. The times are simulated.
256 devices in a mesh: row: 8 (over z), col: 32 (over x, y, core).
Axes of the slice: x: 4, y: 4, z: 8, core: 2. Of those that a mesh axis runs over, the one named last changes fastest.
Arguments:
- embeddings: bfloat16 [49152, 256], P(('row', 'col')), may hold values from -256 to 256
- start_vectors: float32 [49152, 64], P(('row', 'col')), may hold values from -6 to 6
Outputs:
- spectral: float32 [49152, 64], P(('row', 'col'))
All inputs are finite; a program needn't handle non-finite values.
Results may differ from a plain program's by a relative error of at most 0.0068.
Values may be sent and summed in bfloat16 or wider, within the bound.
No kernel may reach another device: no remote copies, remote signals or barrier semaphores. Data moves between devices by JAX's collectives and lax.ppermute only.
A program may use at most 64 MiB of HBM per device.

v0:
```python
import math

import jax
import jax.numpy as jnp
from jax import lax
from jax.sharding import PartitionSpec as P

sharpness = 16.0
threshold = 0.3


def local(embeddings, start_vectors):
    local_docs = embeddings.shape[0]
    all_docs = local_docs * lax.axis_size("row") * lax.axis_size("col")
    widened = embeddings.astype(jnp.float32)
    unit_rows = (
        widened * lax.rsqrt(jnp.sum(widened * widened, axis=1, keepdims=True) + 1e-06)
    ).astype(jnp.bfloat16)
    column_set = lax.all_gather(unit_rows, "row", axis=0, tiled=True)
    scores = lax.dot_general(
        lax.all_gather(unit_rows, "col", axis=0, tiled=True),
        column_set,
        (((1,), (1,)), ((), ())),
        preferred_element_type=jnp.float32,
    )
    adjacency = jax.nn.sigmoid(sharpness * (scores - threshold)).astype(jnp.bfloat16)
    row_sums = jnp.sum(adjacency, axis=1, dtype=jnp.float32)
    degree_set = lax.psum(row_sums, "col")
    own_first = lax.axis_index("col") * local_docs
    degree = lax.dynamic_slice_in_dim(degree_set, own_first, local_docs, 0)
    inv_root = lax.rsqrt(degree)
    root_degree = jnp.sqrt(degree)

    def products(weighted):
        gathered = lax.all_gather(weighted, "row", axis=0, tiled=True)
        return (adjacency, gathered)

    def own_sums(weighted):
        tiles, gathered = products(weighted)
        return lax.psum_scatter(
            jnp.dot(tiles, gathered, preferred_element_type=jnp.float32),
            "col",
            scatter_dimension=0,
            tiled=True,
        )

    def deflation(vectors):
        return lax.psum(
            (jnp.sum(root_degree[:, None] * vectors, axis=0), jnp.sum(degree)), ("row", "col")
        )

    vectors = start_vectors
    weighted = (inv_root[:, None] * vectors).astype(jnp.bfloat16)
    correlation, degree_total = deflation(vectors)
    partial_sums = own_sums(weighted)
    vectors = (
        inv_root[:, None] * partial_sums
        - root_degree[:, None] * (correlation / degree_total)[None, :]
    )
    weighted = (inv_root[:, None] * vectors).astype(jnp.bfloat16)
    correlation, degree_total = deflation(vectors)
    partial_sums = own_sums(weighted)
    vectors = (
        inv_root[:, None] * partial_sums
        - root_degree[:, None] * (correlation / degree_total)[None, :]
    )
    gram_matrix = lax.psum(
        jnp.dot(vectors.T, vectors, precision=lax.Precision.HIGHEST), ("row", "col")
    )
    cholesky_factor = jnp.linalg.cholesky(gram_matrix)
    solved = lax.linalg.triangular_solve(cholesky_factor, vectors.T, left_side=True, lower=True)
    return solved.T * math.sqrt(all_docs)


def solution(mesh):
    return jax.shard_map(
        local,
        mesh=mesh,
        in_specs=(P(("row", "col"), None), P(("row", "col"), None)),
        out_specs=P(("row", "col"), None),
        check_vma=False,
    )
```

profile of v0, /device:TPU:1, one launch (start us, length us, event | category | flops | bytes accessed | tf_op | source)
XLA Modules:
  0.0 554.0 jit_solution(9075832216609413625)
XLA Ops:
  6.5 1.0 fusion
  7.6 1.6 fusion.1
  9.2 24.6 %all_gather.13 = bf16[1536,256]{1,0:T(8,128)(2,1)S(1)} all-gather(bf16[192,256]{1,0:T(8,128)(2,1)} %fusion.1), channel_id=1, replica_groups=mesh['row'=8,'col'=32] {'row'}, dimensions={0}, use_global_device_ids=true | all-gather | bytes 884736 | tf_op jit(solution)/shard_map/all_gather | solution.py:19
  33.9 30.4 %all-gather.4.cloned.1.call-done = bf16[6144,256]{1,0:T(8,128)(2,1)} async-done(((bf16[192,256]{1,0:T(8,128)(2,1)}), bf16[6144,256]{1,0:T(8,128)(2,1)}) %all-gather.4.cloned.1.call-update) | async-done | bytes 3145744 | tf_op jit(solution)/shard_map/all_gather | solution.py:21
  64.2 16.3 %convert_reduce_fusion = (f32[6144]{0:T(1024)S(1)}, bf16[6144,1536]{0,1:T(8,128)(2,1)}) fusion(bf16[6144,256]{1,0:T(8,128)(2,1)} %all-gather.4.cloned.1.call-done, bf16[1536,256]{1,0:T(8,128)(2,1)S(1)} %all_gather.13), kind=kOutput, calls=%fused_computation | convolution fusion | flops 4907329536 | bytes 22831104 | tf_op jit(solution)/shard_map/dot_general | solution.py:20
  80.5 120.9 %psum.38 = f32[6144]{0:T(1024)S(1)} all-reduce(f32[6144]{0:T(1024)S(1)} %get-tuple-element.14), channel_id=1, replica_groups=mesh['row'=8,'col'=32] {'col'}, use_global_device_ids=true, to_apply=%region_2.0 | all-reduce | flops 6144 | bytes 49152 | tf_op jit(solution)/shard_map/psum | solution.py:28
  201.4 0.7 dynamic-slice_reduce_fusion
  202.1 0.1 multiply_reduce_fusion.1
  202.2 19.9 %all-gather = bf16[8,192,64]{1,2,0:T(8,128)(2,1)S(1)} all-gather(bf16[1,192,64]{1,2,0:T(8,128)(2,1)S(1)} %get-tuple-element.10), channel_id=1, replica_groups=mesh['row'=8,'col'=32] {'row'}, dimensions={0}, use_global_device_ids=true | all-gather | bytes 221184 | tf_op jit(solution)/shard_map/all_gather | solution.py:35
  222.1 0.1 copy.9
  222.2 0.2 reshape.20
  222.4 12.9 %fusion.14 = f32[6144,64]{1,0:T(8,128)} fusion(bf16[1536,64]{0,1:T(8,128)(2,1)S(1)} %reshape.20, bf16[6144,1536]{0,1:T(8,128)(2,1)} %get-tuple-element.15), kind=kOutput, calls=%fused_computation.37 | convolution fusion | flops 1207959552 | bytes 20643840
  235.5 83.2 %all-reduce = (f32[64]{0:T(128)S(1)}, f32[]{:T(128)}) all-reduce(f32[64]{0:T(128)S(1)} %get-tuple-element.9, f32[]{:T(128)} %get-tuple-element.11), channel_id=1, replica_groups=mesh['row'=8,'col'=32] {'row','col'}, use_global_device_ids=true, to_apply=%region_5.0 | all-reduce | flops 65 | bytes 520 | tf_op jit(solution)/shard_map/psum | solution.py:48
  318.7 0.6 broadcast_divide_fusion.1
  319.3 9.1 %reduce-scatter.7.cloned.1.call-done = f32[192,64]{1,0:T(8,128)} async-done(((f32[6144,64]{1,0:T(8,128)}), f32[192,64]{1,0:T(8,128)}) %reduce-scatter.7.cloned.1.call-update) | async-done | bytes 49168
  328.4 1.0 copy.15
  329.4 0.2 multiply_reduce_fusion
  329.5 20.3 %all-gather.1 = bf16[8,192,64]{1,2,0:T(8,128)(2,1)S(1)} all-gather(bf16[1,192,64]{1,2,0:T(8,128)(2,1)S(1)} %get-tuple-element.8), channel_id=1, replica_groups=mesh['row'=8,'col'=32] {'row'}, dimensions={0}, use_global_device_ids=true | all-gather | bytes 221184 | tf_op jit(solution)/shard_map/all_gather | solution.py:35
  349.8 0.1 copy.10
  350.0 0.2 reshape.22
  350.2 12.9 %fusion.15 = f32[6144,64]{1,0:T(8,128)} fusion(bf16[1536,64]{0,1:T(8,128)(2,1)S(1)} %reshape.22, bf16[6144,1536]{0,1:T(8,128)(2,1)} %get-tuple-element.15), kind=kOutput, calls=%fused_computation.38 | convolution fusion | flops 1207959552 | bytes 20643840
  363.2 81.8 %psum.41 = f32[64]{0:T(128)S(1)} all-reduce(f32[64]{0:T(128)S(1)} %get-tuple-element.7), channel_id=1, replica_groups=mesh['row'=8,'col'=32] {'row','col'}, use_global_device_ids=true, to_apply=%region_10.0 | all-reduce | flops 64 | bytes 512 | tf_op jit(solution)/shard_map/psum | solution.py:48
  445.0 0.6 broadcast_divide_fusion
  445.7 10.1 %reduce-scatter.9.cloned.1.call-done = f32[192,64]{1,0:T(8,128)} async-done(((f32[6144,64]{1,0:T(8,128)}), f32[192,64]{1,0:T(8,128)}) %reduce-scatter.9.cloned.1.call-update) | async-done | bytes 49168
  455.8 1.0 copy.17
  456.8 0.3 fusion.2
  457.0 77.3 %psum.42 = f32[64,64]{0,1:T(8,128)S(1)} all-reduce(f32[64,64]{0,1:T(8,128)S(1)} %fusion.2), channel_id=1, replica_groups=mesh['row'=8,'col'=32] {'row','col'}, use_global_device_ids=true, to_apply=%region_11.0 | all-reduce | flops 4096 | bytes 32768 | tf_op jit(solution)/shard_map/psum | solution.py:67
  534.4 5.8 %cholesky.16 = f32[64,64]{1,0:T(8,128)S(1)} custom-call(f32[64,64]{1,0:T(8,128)S(1)} %fusion.7), custom_call_target="Cholesky" | custom-call | tf_op jit(solution)/shard_map/jit(cholesky)/cholesky | solution.py:70
  540.3 0.6 compare_reduce_fusion
  540.9 0.7 fusion.3
  541.6 4.9 custom-call.6
  546.5 0.9 convolution_multiply_fusion
  (12 shorter events, 0.3 us)
Async XLA Ops:
  6.5 57.7 %all-gather.4.cloned.1.call-start = ((), (), s32[]{:S(2)}) async-start(), calls=%async_computation.2 | async-start | bytes 3244032 | tf_op jit(solution)/shard_map/all_gather | solution.py:21
  9.2 319.2 %reduce-scatter.7.cloned.1.call-start = ((), (), s32[]{:S(2)}) async-start(), calls=%async_computation.3 | async-start | bytes 3244032
  33.9 168.2 %copy-start = (f32[192,64]{0,1:T(8,128)S(1)}, f32[192,64]{0,1:T(8,128)}, u32[]{:S(2)}) copy-start(f32[192,64]{0,1:T(8,128)} %param.3) | copy-start | bytes 147460
  235.4 220.4 %reduce-scatter.9.cloned.1.call-start = ((), (), s32[]{:S(2)}) async-start(), calls=%async_computation.4 | async-start | bytes 3244032
Sparse Core Ops, SparseCore 0:
  9.9 54.2 all-gather.3
  235.5 92.8 reduce-scatter.6
  363.3 92.4 reduce-scatter.8
where the time goes:
time: 555 us; the launch traced here: 554 us
  blocking collectives  428 us (77%)
  waiting for transfers between devices  49.6 us (9%)
  matrix products  43.3 us (8%)
  other arithmetic  17 us (3%)
  between operations  13.2 us (2%)
    psum x2, blocking collectives, deflation(): lax.psum((jnp.sum(root_degree[:, None] * vectors, axis=0), jnp.sum(degree...  165 us
    psum x1, blocking collectives, local(): degree_set = lax.psum(row_sums, 'col')  121 us
    psum x1, blocking collectives, local(): lax.psum(jnp.dot(vectors.T, vectors, precision=lax.Precision.HIGHEST), ('...  77.3 us
    all_gather x2, blocking collectives, products(): gathered = lax.all_gather(weighted, 'row', axis=0, tiled=True)  40.2 us
    all_gather x1, waiting for transfers between devices, local(): lax.all_gather(unit_rows, 'col', axis=0, tiled=True)  30.4 us
    unnamed x2, matrix products  25.9 us
    all_gather x1, blocking collectives, local(): column_set = lax.all_gather(unit_rows, 'row', axis=0, tiled=True)  24.6 us
    unnamed x5, waiting for transfers between devices  19.2 us
  transfers between devices with their start and end apart: 3, of which 3 were waited for; matrix products, arithmetic and copies ran while one was open for 0% of the time, Pallas kernels for 0%

commit v1 on v0

v1 whole, which is shorter than its diff:
```python
import math

import jax
import jax.numpy as jnp
from jax import lax
from jax.sharding import Mesh
from jax.sharding import PartitionSpec as P

sharpness = 16.0
threshold = 0.3

AXES = ("z", "x", "y", "core")
PLANE = ("x", "y")
SIZES = {"z": 8, "x": 4, "y": 4, "core": 2}


def spread(value, axes):
    peers = math.prod(SIZES[a] for a in axes)
    return lax.all_to_all(
        jnp.broadcast_to(value[None], (peers, *value.shape)), axes, 0, 0, tiled=True
    )


def swap_core(value):
    return lax.ppermute(value, "core", [(0, 1), (1, 0)])


def rounded(value):
    return lax.reduce_precision(value, 8, 7)


def halves(value):
    hi = rounded(value)
    mid = rounded(value - hi)
    lo = value - hi - mid
    return tuple(part.astype(jnp.bfloat16) for part in (hi, mid, lo))


def local(embeddings, start_vectors):
    docs, width = embeddings.shape
    kept = start_vectors.shape[1]
    all_docs = docs * lax.axis_size(AXES)
    columns = docs * SIZES["z"]
    widened = embeddings.astype(jnp.float32)
    unit_rows = (
        widened * lax.rsqrt(jnp.sum(widened * widened, axis=1, keepdims=True) + 1e-06)
    ).astype(jnp.bfloat16)

    hi, mid, lo = halves(start_vectors)
    packed = jnp.concatenate([unit_rows, hi, mid], axis=1)
    column_set = spread(packed, ("z",)).reshape(columns, width + 2 * kept)
    column_units = column_set[:, :width]
    start = column_set[:, width : width + kept].astype(jnp.float32) + column_set[
        :, width + kept :
    ].astype(jnp.float32)
    own_side = spread(unit_rows, PLANE).reshape(-1, width)
    other_side = swap_core(own_side)

    def tile(rows):
        scores = lax.dot_general(
            rows, column_units, (((1,), (1,)), ((), ())), preferred_element_type=jnp.float32
        )
        return jax.nn.sigmoid(sharpness * (scores - threshold)).astype(jnp.bfloat16)

    tile_own = tile(own_side)
    tile_other = tile(other_side)
    sums = jnp.sum(tile_own, axis=0, dtype=jnp.float32) + jnp.sum(
        tile_other, axis=0, dtype=jnp.float32
    )
    degree = jnp.sum(spread(sums.reshape(columns // 128, 128), ("z",)).reshape(-1, columns), axis=0)
    inv_root = lax.rsqrt(degree)[:, None]
    root_degree = jnp.sqrt(degree)[:, None]

    first = lax.axis_index("z") * docs
    own_inv = lax.dynamic_slice_in_dim(inv_root, first, docs, 0)
    own_root = lax.dynamic_slice_in_dim(root_degree, first, docs, 0)

    def product(weighted, terms, kind):
        mine = jnp.dot(tile_other, weighted, preferred_element_type=jnp.float32)
        theirs = swap_core(mine)
        total = jnp.dot(tile_own, weighted, preferred_element_type=jnp.float32) + theirs
        sent = total.reshape(16, docs // 2, 2 * kept)
        if kind == jnp.bfloat16:
            extra = jnp.concatenate([*halves(terms)] * 2, axis=0)
        else:
            extra = terms
        extra = jnp.pad(extra, ((0, 16 - extra.shape[0]), (0, 0)))
        sent = jnp.concatenate(
            [sent.astype(kind), jnp.broadcast_to(extra[None], (16, *extra.shape))], axis=1
        )
        got = lax.all_to_all(sent, PLANE, 0, 0, tiled=True)
        sums = jnp.sum(got[:, : docs // 2].astype(jnp.float32), axis=0)
        rest = jnp.sum(got[:, docs // 2 :].astype(jnp.float32), axis=0)
        if kind == jnp.bfloat16:
            rest = rest[0:2] + rest[2:4] + rest[4:6]
        else:
            rest = rest[0:2]
        return sums.reshape(docs, kept), rest

    weighted = rounded(inv_root * start)
    total = jnp.full((kept,), 1.0) * jnp.sum(degree)
    terms = jnp.concatenate([jnp.sum(root_degree * start, axis=0), total]).reshape(1, -1)
    terms = jnp.concatenate([terms, jnp.zeros_like(terms)], axis=0)

    partial_sums, rest = product(weighted.astype(jnp.bfloat16), terms + swap_core(terms), jnp.bfloat16)
    correlation, degree_total = rest[0, :kept], rest[0, kept:]
    vectors = own_inv * partial_sums - own_root * (correlation / degree_total)[None, :]
    corr = jnp.sum(own_root * vectors, axis=0).reshape(1, kept)
    sent = jnp.concatenate(
        [rounded(own_inv * vectors).astype(jnp.bfloat16), *halves(corr), jnp.zeros((13, kept), jnp.bfloat16)], axis=0
    )
    got = spread(sent, ("z",)).reshape(-1, docs + 16, kept)
    corr = jnp.sum(got[:, docs : docs + 3].astype(jnp.float32), axis=(0, 1))
    corr = jnp.concatenate([corr, corr]).reshape(1, -1)
    corr = jnp.concatenate([corr, corr], axis=0)
    partial_sums, rest = product(
        got[:, :docs].reshape(columns, kept), corr + swap_core(corr), jnp.float32
    )
    vectors = own_inv * partial_sums - own_root * (rest[0, :kept] / degree_total)[None, :]

    gram = jnp.dot(vectors.T, vectors, precision=lax.Precision.HIGHEST)
    gram = jnp.concatenate([gram[: kept // 2], gram[kept // 2 :]], axis=1)
    gram = jnp.sum(spread(gram, ("z", "core")).reshape(16, kept // 2, 2 * kept), axis=0)
    gram = jnp.sum(spread(gram, PLANE).reshape(16, kept // 2, 2 * kept), axis=0)
    gram = jnp.concatenate([gram[:, :kept], gram[:, kept:]], axis=0)
    cholesky_factor = jnp.linalg.cholesky(gram)
    solved = lax.linalg.triangular_solve(cholesky_factor, vectors.T, left_side=True, lower=True)
    return solved.T * math.sqrt(all_docs)


def solution(mesh):
    fine = Mesh(mesh.devices.reshape(*SIZES.values()), AXES)
    return jax.shard_map(
        local,
        mesh=fine,
        in_specs=(P(AXES, None), P(AXES, None)),
        out_specs=P(AXES, None),
        check_vma=False,
    )
```

time: 555 us -> 225 us (0.41)
  blocking collectives: 428 us -> 38.7 us
  starting transfers between devices: 0.09 us -> 42 us
  waiting for transfers between devices: 49.6 us -> 77.5 us
  between operations: 13.2 us -> 0.37 us
    psum x4 -> x0, blocking collectives: 363 us -> none  [the longest x2 165 us: deflation(): lax.psum((jnp.sum(root_degree[:, None] * vectors, axis=0), jnp.sum(degree...]
    all_to_all x0 -> x5, waiting for transfers between devices: none -> 74.8 us  [the longest x3 51.9 us: spread(): lax.all_to_all(jnp.broadcast_to(value[None], (peers, *value.shape)), axes...]
    all_gather x3 -> x0, blocking collectives: 64.8 us -> none  [the longest x2 40.2 us: products(): gathered = lax.all_gather(weighted, 'row', axis=0, tiled=True)]
    all_to_all x0 -> x3, blocking collectives: none -> 38.7 us  [spread(): lax.all_to_all(jnp.broadcast_to(value[None], (peers, *value.shape)), axes...]
    all_gather x1 -> x0, waiting for transfers between devices: 30.4 us -> none  [local(): lax.all_gather(unit_rows, 'col', axis=0, tiled=True)]
    all_to_all x0 -> x5, starting transfers between devices: none -> 28.4 us  [the longest x3 19.3 us: spread(): lax.all_to_all(jnp.broadcast_to(value[None], (peers, *value.shape)), axes...]
    unnamed x2 -> x0, matrix products: 25.9 us -> none
    dot_general x2 -> x7, matrix products: 16.6 us -> 37.6 us  [the longest x2 14.4 us: tile(): lax.dot_general(rows, column_units, (((1,), (1,)), ((), ())), preferred_e...]
  transfers between devices with their start and end apart: 3 -> 10, of which waited for: 3 -> 7; matrix products, arithmetic and copies ran while one was open for 0% -> 5% of each run, Pallas kernels for 0% -> 0%
where the time goes in v1:
time: 225 us; the launch traced here: 224 us
  waiting for transfers between devices  77.5 us (34%)
  starting transfers between devices  42 us (19%)
  blocking collectives  38.7 us (17%)
  matrix products  38.6 us (17%)
  other arithmetic  19 us (8%)
  local copies, waits for them, and re-layouts  7.99 us (4%)
    all_to_all x3, waiting for transfers between devices, spread(): lax.all_to_all(jnp.broadcast_to(value[None], (peers, *value.shape)), axes...  51.9 us
    all_to_all x3, blocking collectives, spread(): lax.all_to_all(jnp.broadcast_to(value[None], (peers, *value.shape)), axes...  38.7 us
    all_to_all x2, waiting for transfers between devices, product(): got = lax.all_to_all(sent, PLANE, 0, 0, tiled=True)  23 us
    all_to_all x3, starting transfers between devices, spread(): lax.all_to_all(jnp.broadcast_to(value[None], (peers, *value.shape)), axes...  19.3 us
    dot_general x2, matrix products, tile(): lax.dot_general(rows, column_units, (((1,), (1,)), ((), ())), preferred_e...  14.4 us
    ppermute x5, starting transfers between devices, swap_core(): return lax.ppermute(value, 'core', [(0, 1), (1, 0)])  13.6 us
    dot_general x2, matrix products, product(): jnp.dot(tile_own, weighted, preferred_element_type=jnp.float32) + theirs  13.3 us
    dot_general x2, matrix products, product(): mine = jnp.dot(tile_other, weighted, preferred_element_type=jnp.float32)  9.66 us
  transfers between devices with their start and end apart: 10, of which 7 were waited for; matrix products, arithmetic and copies ran while one was open for 5% of the time, Pallas kernels for 0%

profile of v1, /device:TPU:1, one launch (start us, length us, event | category | flops | bytes accessed | tf_op | source)
XLA Modules:
  0.0 224.1 jit_solution(17009009301536475106)
XLA Ops:
  0.0 1.0 fusion.3
  1.0 1.0 fusion.4
  2.0 1.3 broadcast_in_dim.19
  3.3 7.6 %all-to-all-start = ((bf16[16,192,256]{2,1,0:T(8,128)(2,1)}), bf16[16,192,256]{2,1,0:T(8,128)(2,1)S(1)}, u32[]{:S(2)}, u32[]{:S(2)}) async-start(bf16[16,192,256]{2,1,0:T(8,128)(2,1)} %broadcast_in_dim.19), calls=%async_computation | async-start | bytes 3145728 | tf_op jit(solution)/shard_map/all_to_all | solution.py:19
  12.1 19.4 %all-to-all-done = bf16[16,192,256]{2,1,0:T(8,128)(2,1)S(1)} async-done(((bf16[16,192,256]{2,1,0:T(8,128)(2,1)}), bf16[16,192,256]{2,1,0:T(8,128)(2,1)S(1)}, u32[]{:S(2)}, u32[]{:S(2)}) %all-to-all-start) | async-done | bytes 1572896 | tf_op jit(solution)/shard_map/all_to_all | solution.py:19
  31.5 1.1 broadcast_in_dim.20
  32.7 8.2 %all-to-all-start.1 = ((bf16[8,192,384]{2,1,0:T(8,128)(2,1)}), bf16[8,192,384]{2,1,0:T(8,128)(2,1)S(1)}, u32[]{:S(2)}, u32[]{:S(2)}) async-start(bf16[8,192,384]{2,1,0:T(8,128)(2,1)} %broadcast_in_dim.20), calls=%async_computation.1 | async-start | bytes 2359296 | tf_op jit(solution)/shard_map/all_to_all | solution.py:19
  40.8 4.4 %collective-permute-start = (bf16[3072,256]{1,0:T(8,128)(2,1)S(1)}, bf16[3072,256]{1,0:T(8,128)(2,1)}, u32[]{:S(2)}, u32[]{:S(2)}) collective-permute-start(bf16[3072,256]{1,0:T(8,128)(2,1)S(1)} %bitcast.60), channel_id=1, source_target_pairs={{0,1},{1,0},{2,3},{3,2},{4,5},{5,4},{6,7},{7,6},{8,9},{9,8},{10,11... | collective-permute-start | bytes 4718600 | tf_op jit(solution)/shard_map/ppermute | solution.py:25
  45.2 24.1 %all-to-all-done.1 = bf16[8,192,384]{2,1,0:T(8,128)(2,1)S(1)} async-done(((bf16[8,192,384]{2,1,0:T(8,128)(2,1)}), bf16[8,192,384]{2,1,0:T(8,128)(2,1)S(1)}, u32[]{:S(2)}, u32[]{:S(2)}) %all-to-all-start.1) | async-done | bytes 1179680 | tf_op jit(solution)/shard_map/all_to_all | solution.py:19
  69.3 7.3 %convert_reduce_fusion.1 = (f32[1536]{0:T(1024)S(1)}, bf16[3072,1536]{1,0:T(8,128)(2,1)}) fusion(bf16[3072,256]{1,0:T(8,128)(2,1)S(1)} %bitcast.61, bf16[1536,384]{1,0:T(8,128)(2,1)S(1)} %bitcast.54), kind=kOutput, calls=%fused_computation.2 | convolution fusion | flops 2453666304 | bytes 11802624 | tf_op jit(solution)/shard_map/dot_general | solution.py:60
  76.6 7.1 %convert_reduce_fusion = (f32[1536]{0:T(1024)S(1)}, bf16[3072,1536]{1,0:T(8,128)(2,1)S(1)}) fusion(bf16[3072,256]{1,0:T(8,128)(2,1)} %collective-permute-done, bf16[1536,384]{1,0:T(8,128)(2,1)S(1)} %bitcast.55), kind=kOutput, calls=%fused_computation | convolution fusion | flops 2453666304 | bytes 11802624 | tf_op jit(solution)/shard_map/dot_general | solution.py:60
  83.8 9.6 %all_to_all.40 = f32[8,12,128]{2,1,0:T(8,128)S(1)} all-to-all(f32[8,12,128]{2,1,0:T(8,128)S(1)} %broadcast_in_dim.21), channel_id=1, replica_groups=mesh['z'=8,'x'=4,'y'=4,'core'=2] {'z'}, dimensions={0} | all-to-all | bytes 98304 | tf_op jit(solution)/shard_map/all_to_all | solution.py:19
  94.0 3.0 %fusion.15 = f32[3072,64]{0,1:T(8,128)S(1)} fusion(bf16[3072,1536]{1,0:T(8,128)(2,1)S(1)} %get-tuple-element.28, f32[1536]{0:T(1024)S(1)} %get-tuple-element.17, bf16[1536,384]{1,0:T(8,128)(2,1)S(1)} %bitcast.56), kind=kOutput, calls=%fused_computation.72 | convolution fusion | flops 604569600 | bytes 11018240 | tf_op jit(solution)/shard_map/dot_general | solution.py:79
  97.0 5.3 %collective-permute-start.1 = (f32[3072,64]{0,1:T(8,128)S(1)}, f32[3072,64]{0,1:T(8,128)S(1)}, u32[]{:S(2)}, u32[]{:S(2)}) collective-permute-start(f32[3072,64]{0,1:T(8,128)S(1)} %fusion.15), channel_id=1, source_target_pairs={{0,1},{1,0},{2,3},{3,2},{4,5},{5,4},{6,7},{7,6},{8,9},{9,8},{10,11... | collective-permute-start | bytes 2359304 | tf_op jit(solution)/shard_map/ppermute | solution.py:25
  103.5 1.1 collective-permute-done.2
  104.7 6.7 %fusion = bf16[3072,64]{0,1:T(8,128)(2,1)S(1)} fusion(f32[3072,64]{0,1:T(8,128)S(1)} %collective-permute-done.1, bf16[3072,1536]{1,0:T(8,128)(2,1)} %get-tuple-element.26, f32[1536]{0:T(1024)S(1)} %get-tuple-element.17, bf16[1536,384]{1,0:T(8,128)(2,1)S(1)} %bitcast.58), kind=kOutput, calls=%fused_computation.6 | convolution fusion | flops 604962816 | bytes 11411456 | tf_op jit(solution)/shard_map/dot_general | solution.py:81
  113.0 5.3 %all-to-all-start.3 = ((bf16[16,112,128]{2,1,0:T(8,128)(2,1)}), bf16[16,112,128]{2,1,0:T(8,128)(2,1)S(1)}, u32[]{:S(2)}, u32[]{:S(2)}) async-start(bf16[16,112,128]{2,1,0:T(8,128)(2,1)} %pad_maximum_fusion.1), calls=%async_computation.3 | async-start | bytes 917504 | tf_op jit(solution)/shard_map/all_to_all | solution.py:91
  118.4 9.6 %all-to-all-done.3 = bf16[16,112,128]{2,1,0:T(8,128)(2,1)S(1)} async-done(((bf16[16,112,128]{2,1,0:T(8,128)(2,1)}), bf16[16,112,128]{2,1,0:T(8,128)(2,1)S(1)}, u32[]{:S(2)}, u32[]{:S(2)}) %all-to-all-start.3) | async-done | bytes 458784 | tf_op jit(solution)/shard_map/all_to_all | solution.py:91
  128.8 11.6 %all_to_all.41 = bf16[8,208,64]{1,2,0:T(8,128)(2,1)S(1)} all-to-all(bf16[8,208,64]{1,2,0:T(8,128)(2,1)S(1)} %broadcast_in_dim.24), channel_id=1, replica_groups=mesh['z'=8,'x'=4,'y'=4,'core'=2] {'z'}, dimensions={0} | all-to-all | bytes 425984 | tf_op jit(solution)/shard_map/all_to_all | solution.py:19
  140.8 6.6 %fusion.19 = f32[3072,64]{0,1:T(8,128)S(1)} fusion(bf16[3072,1536]{1,0:T(8,128)(2,1)} %copy-done, bf16[1536,64]{0,1:T(8,128)(2,1)S(1)} %reshape.201), kind=kOutput, calls=%fused_computation.76 | convolution fusion | flops 603979776 | bytes 10420224 | tf_op jit(solution)/shard_map/dot_general | solution.py:79
  147.4 3.7 %collective-permute-start.3 = (f32[3072,64]{0,1:T(8,128)S(1)}, f32[3072,64]{0,1:T(8,128)S(1)}, u32[]{:S(2)}, u32[]{:S(2)}) collective-permute-start(f32[3072,64]{0,1:T(8,128)S(1)} %fusion.19), channel_id=1, source_target_pairs={{0,1},{1,0},{2,3},{3,2},{4,5},{5,4},{6,7},{7,6},{8,9},{9,8},{10,11... | collective-permute-start | bytes 2359304 | tf_op jit(solution)/shard_map/ppermute | solution.py:25
  151.5 1.6 collective-permute-done.4
  153.0 6.6 %convolution_add_fusion = f32[3072,64]{0,1:T(8,128)S(1)} fusion(f32[3072,64]{0,1:T(8,128)S(1)} %collective-permute-done.3, bf16[3072,1536]{1,0:T(8,128)(2,1)} %get-tuple-element.26, bf16[1536,64]{0,1:T(8,128)(2,1)S(1)} %reshape.201), kind=kOutput, calls=%fused_computation.4 | convolution fusion | flops 604176384 | bytes 11206656 | tf_op jit(solution)/shard_map/dot_general | solution.py:81
  160.4 1.0 pad_maximum_fusion
  161.4 3.8 %all-to-all-start.5 = ((f32[16,112,128]{2,1,0:T(8,128)}), f32[16,112,128]{2,1,0:T(8,128)S(1)}, u32[]{:S(2)}, u32[]{:S(2)}) async-start(f32[16,112,128]{2,1,0:T(8,128)} %pad_maximum_fusion), calls=%async_computation.5 | async-start | bytes 1835008 | tf_op jit(solution)/shard_map/all_to_all | solution.py:91
  165.9 13.3 %all-to-all-done.5 = f32[16,112,128]{2,1,0:T(8,128)S(1)} async-done(((f32[16,112,128]{2,1,0:T(8,128)}), f32[16,112,128]{2,1,0:T(8,128)S(1)}, u32[]{:S(2)}, u32[]{:S(2)}) %all-to-all-start.5) | async-done | bytes 917536 | tf_op jit(solution)/shard_map/all_to_all | solution.py:91
  180.1 17.5 %all_to_all.42 = f32[16,32,128]{2,1,0:T(8,128)S(1)} all-to-all(f32[16,32,128]{2,1,0:T(8,128)S(1)} %broadcast_in_dim.26), channel_id=1, replica_groups=mesh['z'=8,'x'=4,'y'=4,'core'=2] {'z','core'}, dimensions={0} | all-to-all | bytes 524288 | tf_op jit(solution)/shard_map/all_to_all | solution.py:19
  198.3 3.5 %all-to-all-start.7 = ((f32[16,32,128]{2,1,0:T(8,128)}), f32[16,32,128]{2,1,0:T(8,128)S(1)}, u32[]{:S(2)}, u32[]{:S(2)}) async-start(f32[16,32,128]{2,1,0:T(8,128)} %broadcast_in_dim.27), calls=%async_computation.7 | async-start | bytes 524288 | tf_op jit(solution)/shard_map/all_to_all | solution.py:19
  202.1 8.3 %all-to-all-done.7 = f32[16,32,128]{2,1,0:T(8,128)S(1)} async-done(((f32[16,32,128]{2,1,0:T(8,128)}), f32[16,32,128]{2,1,0:T(8,128)S(1)}, u32[]{:S(2)}, u32[]{:S(2)}) %all-to-all-start.7) | async-done | bytes 262176 | tf_op jit(solution)/shard_map/all_to_all | solution.py:19
  211.0 5.9 %cholesky.16 = f32[64,64]{1,0:T(8,128)S(1)} custom-call(f32[64,64]{1,0:T(8,128)S(1)} %fusion.9), custom_call_target="Cholesky" | custom-call | tf_op jit(solution)/shard_map/jit(cholesky)/cholesky | solution.py:126
  218.2 4.9 %custom-call.6 = f32[1,64,64]{1,2,0:T(8,128)S(1)} custom-call(f32[1,64,64]{2,1,0:T(8,128)S(1)} %fusion.7), custom_call_target="InvertDiagBlocksLowerTriangular" | custom-call | tf_op jit(solution)/shard_map/triangular_solve | solution.py:127
  223.1 1.0 convolution_multiply_fusion
  (86 shorter events, 11.2 us)
Async XLA Ops:
  3.3 28.2 %all-to-all-start = ((bf16[16,192,256]{2,1,0:T(8,128)(2,1)}), bf16[16,192,256]{2,1,0:T(8,128)(2,1)S(1)}, u32[]{:S(2)}, u32[]{:S(2)}) async-start(bf16[16,192,256]{2,1,0:T(8,128)(2,1)} %broadcast_in_dim.19), calls=%async_computation | async-start | bytes 3145728 | tf_op jit(solution)/shard_map/all_to_all | solution.py:19
  32.7 36.7 %all-to-all-start.1 = ((bf16[8,192,384]{2,1,0:T(8,128)(2,1)}), bf16[8,192,384]{2,1,0:T(8,128)(2,1)S(1)}, u32[]{:S(2)}, u32[]{:S(2)}) async-start(bf16[8,192,384]{2,1,0:T(8,128)(2,1)} %broadcast_in_dim.20), calls=%async_computation.1 | async-start | bytes 2359296 | tf_op jit(solution)/shard_map/all_to_all | solution.py:19
  40.8 35.8 %collective-permute-start = (bf16[3072,256]{1,0:T(8,128)(2,1)S(1)}, bf16[3072,256]{1,0:T(8,128)(2,1)}, u32[]{:S(2)}, u32[]{:S(2)}) collective-permute-start(bf16[3072,256]{1,0:T(8,128)(2,1)S(1)} %bitcast.60), channel_id=1, source_target_pairs={{0,1},{1,0},{2,3},{3,2},{4,5},{5,4},{6,7},{7,6},{8,9},{9,8},{10,11... | collective-permute-start | bytes 4718600 | tf_op jit(solution)/shard_map/ppermute | solution.py:25
  83.7 10.3 %copy-start = (bf16[3072,1536]{1,0:T(8,128)(2,1)}, bf16[3072,1536]{1,0:T(8,128)(2,1)S(1)}, u32[]{:S(2)}) copy-start(bf16[3072,1536]{1,0:T(8,128)(2,1)S(1)} %get-tuple-element.28) | copy-start | bytes 28311556
  97.0 7.7 %collective-permute-start.1 = (f32[3072,64]{0,1:T(8,128)S(1)}, f32[3072,64]{0,1:T(8,128)S(1)}, u32[]{:S(2)}, u32[]{:S(2)}) collective-permute-start(f32[3072,64]{0,1:T(8,128)S(1)} %fusion.15), channel_id=1, source_target_pairs={{0,1},{1,0},{2,3},{3,2},{4,5},{5,4},{6,7},{7,6},{8,9},{9,8},{10,11... | collective-permute-start | bytes 2359304 | tf_op jit(solution)/shard_map/ppermute | solution.py:25
  103.4 1.2 collective-permute-start.2
  113.0 15.1 %all-to-all-start.3 = ((bf16[16,112,128]{2,1,0:T(8,128)(2,1)}), bf16[16,112,128]{2,1,0:T(8,128)(2,1)S(1)}, u32[]{:S(2)}, u32[]{:S(2)}) async-start(bf16[16,112,128]{2,1,0:T(8,128)(2,1)} %pad_maximum_fusion.1), calls=%async_computation.3 | async-start | bytes 917504 | tf_op jit(solution)/shard_map/all_to_all | solution.py:91
  147.4 5.7 %collective-permute-start.3 = (f32[3072,64]{0,1:T(8,128)S(1)}, f32[3072,64]{0,1:T(8,128)S(1)}, u32[]{:S(2)}, u32[]{:S(2)}) collective-permute-start(f32[3072,64]{0,1:T(8,128)S(1)} %fusion.19), channel_id=1, source_target_pairs={{0,1},{1,0},{2,3},{3,2},{4,5},{5,4},{6,7},{7,6},{8,9},{9,8},{10,11... | collective-permute-start | bytes 2359304 | tf_op jit(solution)/shard_map/ppermute | solution.py:25
  151.4 1.6 collective-permute-start.4
  161.4 17.8 %all-to-all-start.5 = ((f32[16,112,128]{2,1,0:T(8,128)}), f32[16,112,128]{2,1,0:T(8,128)S(1)}, u32[]{:S(2)}, u32[]{:S(2)}) async-start(f32[16,112,128]{2,1,0:T(8,128)} %pad_maximum_fusion), calls=%async_computation.5 | async-start | bytes 1835008 | tf_op jit(solution)/shard_map/all_to_all | solution.py:91
  198.3 12.2 %all-to-all-start.7 = ((f32[16,32,128]{2,1,0:T(8,128)}), f32[16,32,128]{2,1,0:T(8,128)S(1)}, u32[]{:S(2)}, u32[]{:S(2)}) async-start(f32[16,32,128]{2,1,0:T(8,128)} %broadcast_in_dim.27), calls=%async_computation.7 | async-start | bytes 524288 | tf_op jit(solution)/shard_map/all_to_all | solution.py:19

commit v2 on v0

v2 whole, which is shorter than its diff:
```python
import functools
import math

import jax
import jax.numpy as jnp
from jax import lax
from jax.experimental import pallas as pl
from jax.experimental.pallas import tpu as pltpu
from jax.sharding import Mesh
from jax.sharding import PartitionSpec as P

sharpness = 16.0
threshold = 0.3

AXES = ("z", "x", "y", "core")
PLANE = ("x", "y")
SIZES = {"z": 8, "x": 4, "y": 4, "core": 2}
DEPTH = SIZES["z"]
PEERS = SIZES["x"] * SIZES["y"]

DOCS = 192
HALF = DOCS // 2
E = 256
K = 64
COLUMNS = DEPTH * DOCS
ROWS = PEERS * DOCS
ROW_BLOCK = 512
COLUMN_BLOCK = 256
LANES = 128
PIVOTS = 4

bf16 = jnp.bfloat16
f32 = jnp.float32
HIGHEST = lax.Precision.HIGHEST


def shape(*dims, dtype=f32):
    return jax.ShapeDtypeStruct(dims, dtype)


def call(kernel, outs, args, scratch=(), flops=0):
    vmem = pl.BlockSpec(memory_space=pltpu.VMEM)
    moved = sum(math.prod(a.shape) * a.dtype.itemsize for a in (*args, *outs))
    return pl.pallas_call(
        kernel,
        out_shape=tuple(outs),
        in_specs=[vmem] * len(args),
        out_specs=tuple(vmem for _ in outs),
        scratch_shapes=list(scratch),
        cost_estimate=pl.CostEstimate(flops=flops, bytes_accessed=moved, transcendentals=0),
        compiler_params=pltpu.CompilerParams(vmem_limit_bytes=8 * 2**20),
    )(*args)


def left_lanes(value):
    return lax.broadcasted_iota(jnp.int32, value.shape, value.ndim - 1) < K


def swap_lanes(value):
    return pltpu.roll(value, K, value.ndim - 1)


def root_of(value):
    guess = lax.rsqrt(value)
    inv = guess * (1.5 - 0.5 * value * guess * guess)
    return inv, value * inv


def two_parts(value):
    hi = value.astype(bf16).astype(f32)
    return hi, (value - hi).astype(bf16).astype(f32)


def unit_kernel(emb_ref, plane_ref, depth_ref):
    wide = emb_ref[...].astype(f32)
    unit = wide * lax.rsqrt(jnp.sum(wide * wide, axis=1, keepdims=True) + 1e-06)
    unit = unit.astype(bf16)
    plane_ref[...] = jnp.broadcast_to((unit * (sharpness / 2))[None], plane_ref.shape)
    depth_ref[...] = jnp.broadcast_to(unit[None], depth_ref.shape)


def tile_kernel(last, *refs):
    if last:
        rows_ref, cols_ref, before_ref, start_ref, tile_ref, sums_ref, acc = refs
        acc[...] = before_ref[...]
    else:
        rows_ref, cols_ref, tile_ref, sums_ref, acc = refs
        acc[...] = jnp.zeros_like(acc)

    def block(i, _):
        at = pl.ds(pl.multiple_of(i * ROW_BLOCK, ROW_BLOCK), ROW_BLOCK)
        rows = rows_ref[at, :]
        for c in range(COLUMNS // COLUMN_BLOCK):
            where = slice(c * COLUMN_BLOCK, (c + 1) * COLUMN_BLOCK)
            scores = lax.dot_general(
                rows, cols_ref[where, :], (((1,), (1,)), ((), ())), preferred_element_type=f32
            )
            entry = 0.5 * jnp.tanh(scores - sharpness * threshold / 2) + 0.5
            tile_ref[at, where] = entry.astype(bf16)
            acc[:, where] += jnp.sum(entry.reshape(ROW_BLOCK // 8, 8, COLUMN_BLOCK), axis=0)
        return 0

    lax.fori_loop(0, ROWS // ROW_BLOCK, block, 0)
    if last:
        start = jnp.concatenate([start_ref[...], jnp.zeros((K, 2 * LANES - DOCS), f32)], axis=1)
        start = jnp.concatenate([start, jnp.zeros_like(start)], axis=0).T
        top, low = start[:HALF], swap_lanes(start[HALF:DOCS])
        sums_ref[:, :HALF, :] = jnp.broadcast_to((top + low)[None], (DEPTH, HALF, LANES))
        sums_ref[:, HALF:, :] = jnp.zeros((DEPTH, 16, LANES), f32)
        total = jnp.sum(acc[...], axis=0, keepdims=True)
        for k in range(COLUMNS // LANES):
            sums_ref[:, HALF + k : HALF + k + 1, :] = jnp.broadcast_to(
                total[None, :, k * LANES : (k + 1) * LANES], (DEPTH, 1, LANES)
            )
    else:
        sums_ref[...] = acc[...]


def multiply(tile_ref, weights_ref, out_ref, terms):
    chunks = 4

    def block(i, _):
        rows = chunks * DOCS
        sums = jnp.dot(
            tile_ref[pl.ds(pl.multiple_of(i * rows, rows), rows), :],
            weights_ref[...],
            preferred_element_type=f32,
        )
        for c in range(chunks):
            top = sums[c * DOCS : c * DOCS + HALF]
            low = sums[c * DOCS + HALF : (c + 1) * DOCS]
            out_ref[i * chunks + c, :HALF, :] = jnp.where(left_lanes(top), top, low)
            out_ref[i * chunks + c, HALF:, :] = terms
        return 0

    lax.fori_loop(0, PEERS // chunks, block, 0)


def rows_of(*values):
    index = lax.broadcasted_iota(jnp.int32, (8, LANES), 0)
    block = jnp.zeros((8, LANES), f32)
    for i, value in enumerate(values):
        block = jnp.where(index == i, jnp.broadcast_to(value, (8, LANES)), block)
    return block


def spread_lanes(packed):
    other = swap_lanes(packed)
    left = left_lanes(packed)
    return jnp.where(left, packed, other), jnp.where(left, other, packed)


def first_kernel(tile_ref, got_ref, out_ref, weights_ref, inv_ref, root_ref, all_inv, all_root):
    degree = jnp.sum(got_ref[:, HALF:, :], axis=0)
    blocks = COLUMNS // LANES
    degree = jnp.where(lax.broadcasted_iota(jnp.int32, degree.shape, 0) < blocks, degree, 1.0)
    tall = jnp.concatenate([degree, jnp.ones((LANES - degree.shape[0], LANES), f32)], axis=0).T
    inv, root = root_of(tall)
    total = jnp.zeros((1, LANES), f32)
    for k in range(blocks):
        at = slice(k * LANES, (k + 1) * LANES)
        all_inv[at, :] = jnp.broadcast_to(inv[:, k : k + 1], (LANES, LANES))
        all_root[at, :] = jnp.broadcast_to(root[:, k : k + 1], (LANES, LANES))
        total += jnp.sum(
            jnp.broadcast_to(tall[:, k : k + 1], (LANES, LANES)), axis=0, keepdims=True
        )
    correlation = jnp.zeros((1, LANES), f32)
    for j in range(DEPTH):
        for h, start in enumerate(spread_lanes(got_ref[j, :HALF, :])):
            at = slice(j * DOCS + h * HALF, j * DOCS + (h + 1) * HALF)
            weights_ref[at, :] = (all_inv[at, :] * start).astype(bf16)
            correlation += jnp.sum(all_root[at, :] * start, axis=0, keepdims=True)
    first = lax.axis_index("z") * DOCS
    top = pl.ds(pl.multiple_of(first, HALF), HALF)
    low = pl.ds(pl.multiple_of(first + HALF, HALF), HALF)
    for whole, own in ((all_inv, inv_ref), (all_root, root_ref)):
        upper = whole[top, :]
        own[...] = jnp.where(left_lanes(upper), upper, whole[low, :])
    multiply(tile_ref, weights_ref, out_ref, rows_of(correlation, total))


def second_kernel(tile_ref, got_ref, out_ref, weights_ref):
    terms = jnp.zeros((1, LANES), f32)
    for j in range(DEPTH):
        for h, weights in enumerate(spread_lanes(got_ref[j, :HALF, :].astype(f32))):
            at = slice(j * DOCS + h * HALF, j * DOCS + (h + 1) * HALF)
            weights_ref[at, :] = weights.astype(bf16)
        terms += jnp.sum(got_ref[j, HALF:, :].astype(f32), axis=0, keepdims=True)
    multiply(tile_ref, weights_ref, out_ref, rows_of(terms))


def again_kernel(tile_ref, weights_ref, other_ref, out_ref):
    multiply(tile_ref, weights_ref, out_ref, other_ref[0, HALF:, :])


def narrow_kernel(own_ref, other_ref, out_ref):
    out_ref[:, :HALF, :] = (own_ref[:, :HALF, :] + other_ref[:, :HALF, :]).astype(bf16)
    hi, mid = two_parts(own_ref[0, HALF:, :] + other_ref[0, HALF:, :])
    terms = jnp.concatenate([hi, mid], axis=0).astype(bf16)
    out_ref[:, HALF:, :] = jnp.broadcast_to(terms[None], (PEERS, 16, LANES))


def add_kernel(own_ref, other_ref, out_ref):
    out_ref[...] = own_ref[...] + other_ref[...]


def middle_kernel(got_ref, inv_ref, root_ref, out_ref, terms_ref):
    sums = jnp.sum(got_ref[:, :HALF, :].astype(f32), axis=0)
    terms = jnp.sum(got_ref[:, HALF:, :].astype(f32), axis=0)
    terms = terms[:8] + terms[8:]
    terms_ref[...] = terms
    inv, root = inv_ref[...], root_ref[...]
    vectors = inv * sums - root * (terms[0:1] / terms[1:2])
    out_ref[:, :HALF, :] = jnp.broadcast_to(
        (inv * vectors).astype(bf16)[None], (DEPTH, HALF, LANES)
    )
    correlation = jnp.sum(root * vectors, axis=0, keepdims=True)
    hi, mid = two_parts(correlation + swap_lanes(correlation))
    index = lax.broadcasted_iota(jnp.int32, (16, LANES), 0)
    terms = jnp.where(index == 0, hi, jnp.where(index == 1, mid, 0.0)).astype(bf16)
    out_ref[:, HALF:, :] = jnp.broadcast_to(terms[None], (DEPTH, 16, LANES))


def gram_kernel(got_ref, inv_ref, root_ref, terms_ref, vectors_ref, out_ref):
    sums = jnp.sum(got_ref[...], axis=0)
    ratio = sums[HALF : HALF + 1] / terms_ref[1:2, :]
    vectors = inv_ref[...] * sums[:HALF] - root_ref[...] * ratio
    vectors_ref[...] = vectors
    tall = jnp.concatenate([vectors, jnp.zeros((LANES - HALF, LANES), f32)], axis=0)
    product = jnp.dot(tall.T, tall, precision=HIGHEST, preferred_element_type=f32)
    gram = product[:K] + swap_lanes(product[K:])
    low = swap_lanes(gram[K // 2 :])
    gram = jnp.where(left_lanes(low), gram[: K // 2], low)
    out_ref[...] = jnp.broadcast_to(gram[None], out_ref.shape)


def fold_kernel(got_ref, out_ref):
    out_ref[...] = jnp.broadcast_to(jnp.sum(got_ref[...], axis=0)[None], out_ref.shape)


def solve_kernel(scale, got_ref, vectors_ref, out_ref):
    packed = jnp.sum(got_ref[...], axis=0)
    work = jnp.concatenate([packed, swap_lanes(packed)], axis=0)
    row = lax.broadcasted_iota(jnp.int32, (K, LANES), 0)
    lane = lax.broadcasted_iota(jnp.int32, (K, LANES), 1)
    work = jnp.where(lane < K, work, jnp.where(lane - K == row, 1.0, 0.0))
    tiles = [work[8 * t : 8 * t + 8] for t in range(K // 8)]
    index = lax.broadcasted_iota(jnp.int32, (8, LANES), 0)
    for k in range(0, K, PIVOTS):
        first, place = divmod(k, 8)
        rows = [tiles[first][place + i : place + i + 1] for i in range(PIVOTS)]
        inner = {
            (i, j): jnp.broadcast_to(rows[i][:, k + j : k + j + 1], (1, LANES))
            for i in range(PIVOTS)
            for j in range(i, PIVOTS)
        }
        after = range(first, K // 8)
        columns = [
            {t: jnp.broadcast_to(tiles[t][:, k + i : k + i + 1], (8, LANES)) for t in after}
            for i in range(PIVOTS)
        ]
        for i in range(PIVOTS):
            inverse = 1.0 / inner[i, i]
            for m in range(i + 1, PIVOTS):
                factor = inner[i, m] * inverse
                rows[m] = rows[m] - factor * rows[i]
                for j in range(m, PIVOTS):
                    inner[m, j] = inner[m, j] - factor * inner[i, j]
                for t in after:
                    columns[m][t] = columns[m][t] - columns[i][t] * factor
            pivot_row = rows[i] * inverse
            for t in after:
                column = columns[i][t]
                if t == first:
                    column = jnp.where(index > place + i, column, 0.0)
                tiles[t] = tiles[t] - column * pivot_row
    work = jnp.concatenate(tiles, axis=0)
    pivots = jnp.sum(jnp.where(lane == row, work, 0.0), axis=1, keepdims=True)
    inv, _ = root_of(pivots)
    right = jnp.where(lane < K, 0.0, work * (inv * scale))
    low = vectors_ref[...]
    padding = jnp.zeros((2 * LANES - DOCS, LANES), f32)
    vectors = jnp.concatenate([swap_lanes(low), low, padding], axis=0)
    out_ref[...] = lax.dot_general(
        right, vectors, (((1,), (1,)), ((), ())), precision=HIGHEST, preferred_element_type=f32
    )[:, :DOCS]


def exchange(value, axes):
    return lax.all_to_all(value, axes, 0, 0, tiled=True)


def swap_core(value):
    return lax.ppermute(value, "core", [(0, 1), (1, 0)])


def local(embeddings, start_vectors):
    all_docs = embeddings.shape[0] * lax.axis_size(AXES)
    plane, depth = call(
        unit_kernel,
        [shape(PEERS, DOCS, E, dtype=bf16), shape(DEPTH, DOCS, E, dtype=bf16)],
        [embeddings],
    )
    own_rows, depth = lax.optimization_barrier((exchange(plane, PLANE), depth))
    own_rows, columns = lax.optimization_barrier((own_rows, exchange(depth, ("z",))))
    own_rows = own_rows.reshape(ROWS, E)
    columns = columns.reshape(COLUMNS, E)
    other_rows = swap_core(own_rows)

    tile = shape(ROWS, COLUMNS, dtype=bf16)
    acc = pltpu.VMEM((8, COLUMNS), f32)
    flops = 2 * ROWS * COLUMNS * E
    own_tile, sums = call(
        functools.partial(tile_kernel, False),
        [tile, shape(8, COLUMNS)],
        [own_rows, columns],
        [acc],
        flops,
    )
    other_tile, sums = call(
        functools.partial(tile_kernel, True),
        [tile, shape(DEPTH, HALF + 16, LANES)],
        [other_rows, columns, sums, start_vectors.T],
        [acc],
        flops,
    )
    sums = exchange(sums, ("z",))

    flops = 2 * ROWS * COLUMNS * LANES
    sent = shape(PEERS, HALF + 8, LANES)
    weights = shape(COLUMNS, LANES, dtype=bf16)
    own = shape(HALF, LANES)
    spread = pltpu.VMEM((COLUMNS, LANES), f32)
    mine, packed, inv, root = call(
        first_kernel,
        [sent, weights, own, own],
        [other_tile, sums],
        [spread, spread],
        flops,
    )
    theirs = swap_core(mine)
    (mine,) = call(again_kernel, [sent], [own_tile, packed, mine], (), flops)
    (total,) = call(narrow_kernel, [shape(PEERS, HALF + 16, LANES, dtype=bf16)], [mine, theirs])
    got = exchange(total, PLANE)
    total, terms = call(
        middle_kernel,
        [shape(DEPTH, HALF + 16, LANES, dtype=bf16), shape(8, LANES)],
        [got, inv, root],
    )
    got = exchange(total, ("z",))
    mine, packed = call(second_kernel, [sent, weights], [other_tile, got], (), flops)
    theirs = swap_core(mine)
    (mine,) = call(again_kernel, [sent], [own_tile, packed, mine], (), flops)
    (total,) = call(add_kernel, [sent], [mine, theirs])
    got = exchange(total, PLANE)
    gram = shape(PEERS, K // 2, LANES)
    vectors, total = call(gram_kernel, [own, gram], [got, inv, root, terms])
    (total,) = call(fold_kernel, [gram], [exchange(total, ("z", "core"))])
    got = exchange(total, PLANE)
    (spectral,) = call(
        functools.partial(solve_kernel, math.sqrt(all_docs)), [shape(K, DOCS)], [got, vectors]
    )
    return spectral.T


def solution(mesh):
    fine = Mesh(mesh.devices.reshape(*SIZES.values()), AXES)
    return jax.shard_map(
        local,
        mesh=fine,
        in_specs=(P(AXES, None), P(AXES, None)),
        out_specs=P(AXES, None),
        check_vma=False,
    )
```

time: 555 us -> 183 us (0.33)
  blocking collectives: 428 us -> 146 us
  waiting for transfers between devices: 49.6 us -> 0.01 us
  matrix products: 43.3 us -> 0 us
  Pallas kernels: 0 us -> 27.2 us
  other arithmetic: 17 us -> 0 us
  between operations: 13.2 us -> 0.12 us
  starting transfers between devices: 0.09 us -> 7.8 us
    psum x4 -> x0, blocking collectives: 363 us -> none  [the longest x2 165 us: deflation(): lax.psum((jnp.sum(root_degree[:, None] * vectors, axis=0), jnp.sum(degree...]
    all_to_all x0 -> x8, blocking collectives: none -> 146 us  [exchange(): return lax.all_to_all(value, axes, 0, 0, tiled=True)]
    all_gather x3 -> x0, blocking collectives: 64.8 us -> none  [the longest x2 40.2 us: products(): gathered = lax.all_gather(weighted, 'row', axis=0, tiled=True)]
    all_gather x1 -> x0, waiting for transfers between devices: 30.4 us -> none  [local(): lax.all_gather(unit_rows, 'col', axis=0, tiled=True)]
    pallas_call x0 -> x13, Pallas kernels: none -> 27.2 us  [call(): pl.pallas_call(kernel, out_shape=tuple(outs), in_specs=[vmem] * len(args)...]
    unnamed x2 -> x0, matrix products: 25.9 us -> none
    unnamed x5 -> x0, waiting for transfers between devices: 19.2 us -> none
    dot_general x2 -> x0, matrix products: 16.6 us -> none  [the longest x1 16.3 us: local(): lax.dot_general(lax.all_gather(unit_rows, 'col', axis=0, tiled=True), col...]
  transfers between devices with their start and end apart: 3 -> 3, of which waited for: 3 -> 0; matrix products, arithmetic and copies ran while one was open for 0% -> 0% of each run, Pallas kernels for 0% -> 6%
where the time goes in v2:
time: 183 us; the launch traced here: 182 us
  blocking collectives  146 us (80%)
  Pallas kernels  27.2 us (15%)
  starting transfers between devices  7.8 us (4%)
    all_to_all x8, blocking collectives, exchange(): return lax.all_to_all(value, axes, 0, 0, tiled=True)  146 us
    pallas_call x13, Pallas kernels, call(): pl.pallas_call(kernel, out_shape=tuple(outs), in_specs=[vmem] * len(args)...  27.2 us
    ppermute x3, starting transfers between devices, swap_core(): return lax.ppermute(value, 'core', [(0, 1), (1, 0)])  7.8 us
  transfers between devices with their start and end apart: 3, of which 0 were waited for; matrix products, arithmetic and copies ran while one was open for 0% of the time, Pallas kernels for 6%

profile of v2, /device:TPU:1, one launch (start us, length us, event | category | flops | bytes accessed | tf_op | source)
XLA Modules:
  0.0 182.1 jit_solution(12869683664457727061)
XLA Ops:
  0.0 0.0 copy-start
  0.0 0.9 copy-done
  0.9 0.2 shard_map.28
  1.1 28.9 %all_to_all.40 = bf16[16,192,256]{2,1,0:T(8,128)(2,1)S(1)} all-to-all(bf16[16,192,256]{2,1,0:T(8,128)(2,1)S(1)} %get-tuple-element.25), channel_id=1, replica_groups=mesh['z'=8,'x'=4,'y'=4,'core'=2] {'x','y'}, dimensions={0} | all-to-all | bytes 3145728 | tf_op jit(solution)/shard_map/all_to_all | solution.py:290
  30.0 28.0 %all_to_all.41 = bf16[8,192,256]{2,1,0:T(8,128)(2,1)S(1)} all-to-all(bf16[8,192,256]{2,1,0:T(8,128)(2,1)S(1)} %get-tuple-element.28), channel_id=1, replica_groups=mesh['z'=8,'x'=4,'y'=4,'core'=2] {'z'}, dimensions={0} | all-to-all | bytes 1572864 | tf_op jit(solution)/shard_map/all_to_all | solution.py:290
  58.0 4.0 %collective-permute-start = (bf16[3072,256]{1,0:T(8,128)(2,1)S(1)}, bf16[3072,256]{1,0:T(8,128)(2,1)S(1)}, u32[]{:S(2)}, u32[]{:S(2)}) collective-permute-start(bf16[3072,256]{1,0:T(8,128)(2,1)S(1)} %bitcast.4), channel_id=1, source_target_pairs={{0,1},{1,0},{2,3},{3,2},{4,5},{5,4},{6,7},{7,6},{8,9},{9,8},{10,11... | collective-permute-start | bytes 4718600 | tf_op jit(solution)/shard_map/ppermute | solution.py:294
  62.1 0.0 copy-start.1
  62.1 4.8 %shard_map.29 = (bf16[3072,1536]{1,0:T(8,128)(2,1)S(1)}, f32[8,1536]{1,0:T(8,128)S(1)}) custom-call(bf16[3072,256]{1,0:T(8,128)(2,1)S(1)} %bitcast.5, bf16[1536,256]{1,0:T(8,128)(2,1)S(1)} %bitcast.6), custom_call_target="tpu_custom_call" | custom-call | flops 2415919104 | bytes 11845632 | tf_op jit(solution)/shard_map/pallas_call | solution.py:44
  66.9 0.0 collective-permute-done.refs_0_
  66.9 0.0 copy-done.1
  66.9 5.0 %shard_map.30 = (bf16[3072,1536]{1,0:T(8,128)(2,1)S(1)}, f32[8,112,128]{2,1,0:T(8,128)S(1)}) custom-call(bf16[3072,256]{1,0:T(8,128)(2,1)S(1)} %collective-permute-done.refs_0_, bf16[1536,256]{1,0:T(8,128)(2,1)S(1)} %bitcast.7, f32[8,1536]{1,0:T(8,128)S(1)} %get-tuple-element.32.refs_2_, f32[64,192]{1,0:T(8,128)S(1)} %bitcast.8), custom_call_target="tpu_custom_call" | custom-call | flops 2415919104 | bytes 12353536 | tf_op jit(solution)/shard_map/pallas_call | solution.py:44
  71.9 19.0 %all_to_all.42.got_ref = f32[8,112,128]{2,1,0:T(8,128)S(1)} all-to-all(f32[8,112,128]{2,1,0:T(8,128)S(1)} %get-tuple-element.34), channel_id=1, replica_groups=mesh['z'=8,'x'=4,'y'=4,'core'=2] {'z'}, dimensions={0} | all-to-all | bytes 917504 | tf_op jit(solution)/shard_map/all_to_all | solution.py:290
  90.9 4.0 %shard_map.31 = (f32[16,104,128]{2,1,0:T(8,128)S(1)}, bf16[1536,128]{1,0:T(8,128)(2,1)S(1)}, f32[96,128]{1,0:T(8,128)S(1)}, f32[96,128]{1,0:T(8,128)S(1)}) custom-call(bf16[3072,1536]{1,0:T(8,128)(2,1)S(1)} %get-tuple-element.33.tile_ref, f32[8,112,128]{2,1,0:T(8,128)S(1)} %all_to_all.42.got_ref), custom_call_target="tpu_custom_call" | custom-call | flops 1207959552 | bytes 11239424 | tf_op jit(solution)/shard_map/pallas_call | solution.py:44
  94.9 0.5 collective-permute-start.1
  95.4 3.1 %shard_map.32.own_ref = f32[16,104,128]{2,1,0:T(8,128)S(1)} custom-call(bf16[3072,1536]{1,0:T(8,128)(2,1)S(1)} %get-tuple-element.31.tile_ref, bf16[1536,128]{1,0:T(8,128)(2,1)S(1)} %get-tuple-element.35.weights_ref, f32[16,104,128]{2,1,0:T(8,128)S(1)} %get-tuple-element.36.other_ref), custom_call_target="tpu_custom_call" | custom-call | flops 1207959552 | bytes 11534336 | tf_op jit(solution)/shard_map/pallas_call | solution.py:44
  98.5 0.0 collective-permute-done.1.other_ref
  98.5 0.1 shard_map.33
  98.6 13.2 %all_to_all.43.got_ref = bf16[16,112,128]{2,1,0:T(8,128)(2,1)S(1)} all-to-all(bf16[16,112,128]{2,1,0:T(8,128)(2,1)S(1)} %shard_map.33), channel_id=1, replica_groups=mesh['z'=8,'x'=4,'y'=4,'core'=2] {'x','y'}, dimensions={0} | all-to-all | bytes 917504 | tf_op jit(solution)/shard_map/all_to_all | solution.py:290
  111.8 0.2 shard_map.34
  112.0 11.5 %all_to_all.44.got_ref = bf16[8,112,128]{2,1,0:T(8,128)(2,1)S(1)} all-to-all(bf16[8,112,128]{2,1,0:T(8,128)(2,1)S(1)} %get-tuple-element.39), channel_id=1, replica_groups=mesh['z'=8,'x'=4,'y'=4,'core'=2] {'z'}, dimensions={0} | all-to-all | bytes 458752 | tf_op jit(solution)/shard_map/all_to_all | solution.py:290
  123.5 3.2 %shard_map.35 = (f32[16,104,128]{2,1,0:T(8,128)S(1)}, bf16[1536,128]{1,0:T(8,128)(2,1)S(1)}) custom-call(bf16[3072,1536]{1,0:T(8,128)(2,1)S(1)} %get-tuple-element.33.tile_ref, bf16[8,112,128]{2,1,0:T(8,128)(2,1)S(1)} %all_to_all.44.got_ref), custom_call_target="tpu_custom_call" | custom-call | flops 1207959552 | bytes 10911744 | tf_op jit(solution)/shard_map/pallas_call | solution.py:44
  126.7 3.3 %collective-permute-start.2 = (f32[16,104,128]{2,1,0:T(8,128)S(1)}, f32[16,104,128]{2,1,0:T(8,128)S(1)}, u32[]{:S(2)}, u32[]{:S(2)}) collective-permute-start(f32[16,104,128]{2,1,0:T(8,128)S(1)} %get-tuple-element.41.other_ref), channel_id=1, source_target_pairs={{0,1},{1,0},{2,3},{3,2},{4,5},{5,4},{6,7},{7,6},{8,9},{9,8},{10,11... | collective-permute-start | bytes 2555912 | tf_op jit(solution)/shard_map/ppermute | solution.py:294
  130.0 3.1 %shard_map.36.own_ref = f32[16,104,128]{2,1,0:T(8,128)S(1)} custom-call(bf16[3072,1536]{1,0:T(8,128)(2,1)S(1)} %get-tuple-element.31.tile_ref, bf16[1536,128]{1,0:T(8,128)(2,1)S(1)} %get-tuple-element.40.weights_ref, f32[16,104,128]{2,1,0:T(8,128)S(1)} %get-tuple-element.41.other_ref), custom_call_target="tpu_custom_call" | custom-call | flops 1207959552 | bytes 11534336 | tf_op jit(solution)/shard_map/pallas_call | solution.py:44
  133.0 0.0 collective-permute-done.2.other_ref
  133.0 0.1 shard_map.37
  133.1 17.7 %all_to_all.45.got_ref = f32[16,104,128]{2,1,0:T(8,128)S(1)} all-to-all(f32[16,104,128]{2,1,0:T(8,128)S(1)} %shard_map.37), channel_id=1, replica_groups=mesh['z'=8,'x'=4,'y'=4,'core'=2] {'x','y'}, dimensions={0} | all-to-all | bytes 1703936 | tf_op jit(solution)/shard_map/all_to_all | solution.py:290
  150.9 0.4 shard_map.38
  151.3 16.1 %all_to_all.46.got_ref = f32[16,32,128]{2,1,0:T(8,128)S(1)} all-to-all(f32[16,32,128]{2,1,0:T(8,128)S(1)} %get-tuple-element.43), channel_id=1, replica_groups=mesh['z'=8,'x'=4,'y'=4,'core'=2] {'z','core'}, dimensions={0} | all-to-all | bytes 524288 | tf_op jit(solution)/shard_map/all_to_all | solution.py:290
  167.4 11.7 %all_to_all.47.got_ref = f32[16,32,128]{2,1,0:T(8,128)S(1)} all-to-all(f32[16,32,128]{2,1,0:T(8,128)S(1)} %shard_map.39), channel_id=1, replica_groups=mesh['z'=8,'x'=4,'y'=4,'core'=2] {'x','y'}, dimensions={0} | all-to-all | bytes 524288 | tf_op jit(solution)/shard_map/all_to_all | solution.py:290
  179.1 3.0 %shard_map.40 = f32[64,192]{1,0:T(8,128)} custom-call(f32[16,32,128]{2,1,0:T(8,128)S(1)} %all_to_all.47.got_ref, f32[96,128]{1,0:T(8,128)S(1)} %get-tuple-element.44.vectors_ref), custom_call_target="tpu_custom_call" | custom-call | bytes 360448 | tf_op jit(solution)/shard_map/pallas_call | solution.py:44
  (1 shorter events, 0.0 us)
Async XLA Ops:
  0.0 0.9 copy-start
  58.0 8.8 %collective-permute-start = (bf16[3072,256]{1,0:T(8,128)(2,1)S(1)}, bf16[3072,256]{1,0:T(8,128)(2,1)S(1)}, u32[]{:S(2)}, u32[]{:S(2)}) collective-permute-start(bf16[3072,256]{1,0:T(8,128)(2,1)S(1)} %bitcast.4), channel_id=1, source_target_pairs={{0,1},{1,0},{2,3},{3,2},{4,5},{5,4},{6,7},{7,6},{8,9},{9,8},{10,11... | collective-permute-start | bytes 4718600 | tf_op jit(solution)/shard_map/ppermute | solution.py:294
  62.1 4.8 %copy-start.1 = (f32[192,64]{0,1:T(8,128)S(1)}, f32[192,64]{0,1:T(8,128)}, u32[]{:S(2)}) copy-start(f32[192,64]{0,1:T(8,128)} %param.3) | copy-start | bytes 147460
  94.9 3.6 %collective-permute-start.1 = (f32[16,104,128]{2,1,0:T(8,128)S(1)}, f32[16,104,128]{2,1,0:T(8,128)S(1)}, u32[]{:S(2)}, u32[]{:S(2)}) collective-permute-start(f32[16,104,128]{2,1,0:T(8,128)S(1)} %get-tuple-element.36.other_ref), channel_id=1, source_target_pairs={{0,1},{1,0},{2,3},{3,2},{4,5},{5,4},{6,7},{7,6},{8,9},{9,8},{10,11... | collective-permute-start | bytes 2555912 | tf_op jit(solution)/shard_map/ppermute | solution.py:294
  126.7 6.4 %collective-permute-start.2 = (f32[16,104,128]{2,1,0:T(8,128)S(1)}, f32[16,104,128]{2,1,0:T(8,128)S(1)}, u32[]{:S(2)}, u32[]{:S(2)}) collective-permute-start(f32[16,104,128]{2,1,0:T(8,128)S(1)} %get-tuple-element.41.other_ref), channel_id=1, source_target_pairs={{0,1},{1,0},{2,3},{3,2},{4,5},{5,4},{6,7},{7,6},{8,9},{9,8},{10,11... | collective-permute-start | bytes 2555912 | tf_op jit(solution)/shard_map/ppermute | solution.py:294

commit v3 on v2

--- a/solution.py
+++ b/solution.py
@@ -12,10 +12,11 @@
 sharpness = 16.0
 threshold = 0.3
 
-AXES = ("z", "x", "y", "core")
+AXES = ("zh", "zl", "x", "y", "core")
 PLANE = ("x", "y")
-SIZES = {"z": 8, "x": 4, "y": 4, "core": 2}
-DEPTH = SIZES["z"]
+LINE = ("zl", "zh")
+SIZES = {"zh": 4, "zl": 2, "x": 4, "y": 4, "core": 2}
+DEPTH = SIZES["zh"] * SIZES["zl"]
 PEERS = SIZES["x"] * SIZES["y"]
 
 DOCS = 192
@@ -71,21 +72,30 @@
     return hi, (value - hi).astype(bf16).astype(f32)
 
 
-def unit_kernel(emb_ref, plane_ref, depth_ref):
+def unit_kernel(emb_ref, start_ref, plane_ref, line_ref):
     wide = emb_ref[...].astype(f32)
     unit = wide * lax.rsqrt(jnp.sum(wide * wide, axis=1, keepdims=True) + 1e-06)
     unit = unit.astype(bf16)
     plane_ref[...] = jnp.broadcast_to((unit * (sharpness / 2))[None], plane_ref.shape)
-    depth_ref[...] = jnp.broadcast_to(unit[None], depth_ref.shape)
+    line_ref[:, :, :E] = jnp.broadcast_to(unit[None], (SIZES["zh"], DOCS, E))
+    start = jnp.concatenate([start_ref[...], jnp.zeros((K, 2 * LANES - DOCS), f32)], axis=1)
+    start = jnp.concatenate([start, jnp.zeros_like(start)], axis=0).T[:DOCS]
+    hi, mid = two_parts(start)
+    pair = jnp.where(left_lanes(hi), hi, swap_lanes(mid)).astype(bf16)
+    line_ref[:, :, E:] = jnp.broadcast_to(pair[None], (SIZES["zh"], DOCS, 2 * K))
 
 
 def tile_kernel(last, *refs):
     if last:
-        rows_ref, cols_ref, before_ref, start_ref, tile_ref, sums_ref, acc = refs
+        rows_ref, cols_ref, before_ref, tile_ref, sums_ref, acc = refs
         acc[...] = before_ref[...]
     else:
-        rows_ref, cols_ref, tile_ref, sums_ref, acc = refs
+        rows_ref, same_ref, other_ref, tile_ref, sums_ref, cols_ref, acc = refs
         acc[...] = jnp.zeros_like(acc)
+        side = lax.axis_index("zl") * (COLUMNS // 2)
+        cols_ref[pl.ds(pl.multiple_of(side, COLUMNS // 2), COLUMNS // 2), :] = same_ref[...]
+        side = COLUMNS // 2 - side
+        cols_ref[pl.ds(pl.multiple_of(side, COLUMNS // 2), COLUMNS // 2), :] = other_ref[...]
 
     def block(i, _):
         at = pl.ds(pl.multiple_of(i * ROW_BLOCK, ROW_BLOCK), ROW_BLOCK)
@@ -93,23 +103,19 @@
         for c in range(COLUMNS // COLUMN_BLOCK):
             where = slice(c * COLUMN_BLOCK, (c + 1) * COLUMN_BLOCK)
             scores = lax.dot_general(
-                rows, cols_ref[where, :], (((1,), (1,)), ((), ())), preferred_element_type=f32
+                rows, cols_ref[where, :E], (((1,), (1,)), ((), ())), preferred_element_type=f32
             )
-            entry = 0.5 * jnp.tanh(scores - sharpness * threshold / 2) + 0.5
+            entry = jnp.tanh(scores - sharpness * threshold / 2) + 1.0
             tile_ref[at, where] = entry.astype(bf16)
             acc[:, where] += jnp.sum(entry.reshape(ROW_BLOCK // 8, 8, COLUMN_BLOCK), axis=0)
         return 0
 
     lax.fori_loop(0, ROWS // ROW_BLOCK, block, 0)
     if last:
-        start = jnp.concatenate([start_ref[...], jnp.zeros((K, 2 * LANES - DOCS), f32)], axis=1)
-        start = jnp.concatenate([start, jnp.zeros_like(start)], axis=0).T
-        top, low = start[:HALF], swap_lanes(start[HALF:DOCS])
-        sums_ref[:, :HALF, :] = jnp.broadcast_to((top + low)[None], (DEPTH, HALF, LANES))
-        sums_ref[:, HALF:, :] = jnp.zeros((DEPTH, 16, LANES), f32)
-        total = jnp.sum(acc[...], axis=0, keepdims=True)
+        total = 0.5 * jnp.sum(acc[...], axis=0, keepdims=True)
+        sums_ref[...] = jnp.zeros_like(sums_ref)
         for k in range(COLUMNS // LANES):
-            sums_ref[:, HALF + k : HALF + k + 1, :] = jnp.broadcast_to(
+            sums_ref[:, k : k + 1, :] = jnp.broadcast_to(
                 total[None, :, k * LANES : (k + 1) * LANES], (DEPTH, 1, LANES)
             )
     else:
@@ -117,7 +123,7 @@
 
 
 def multiply(tile_ref, weights_ref, out_ref, terms):
-    chunks = 4
+    chunks = 8
 
     def block(i, _):
         rows = chunks * DOCS
@@ -150,27 +156,30 @@
     return jnp.where(left, packed, other), jnp.where(left, other, packed)
 
 
-def first_kernel(tile_ref, got_ref, out_ref, weights_ref, inv_ref, root_ref, all_inv, all_root):
-    degree = jnp.sum(got_ref[:, HALF:, :], axis=0)
+def first_kernel(
+    tile_ref, sums_ref, cols_ref, out_ref, weights_ref, inv_ref, root_ref, all_inv, all_root
+):
+    degree = jnp.sum(sums_ref[...], axis=0)
     blocks = COLUMNS // LANES
     degree = jnp.where(lax.broadcasted_iota(jnp.int32, degree.shape, 0) < blocks, degree, 1.0)
     tall = jnp.concatenate([degree, jnp.ones((LANES - degree.shape[0], LANES), f32)], axis=0).T
     inv, root = root_of(tall)
+    correlation = jnp.zeros((1, LANES), f32)
     total = jnp.zeros((1, LANES), f32)
     for k in range(blocks):
         at = slice(k * LANES, (k + 1) * LANES)
-        all_inv[at, :] = jnp.broadcast_to(inv[:, k : k + 1], (LANES, LANES))
-        all_root[at, :] = jnp.broadcast_to(root[:, k : k + 1], (LANES, LANES))
+        pair = cols_ref[at, E:].astype(f32)
+        start = pair + swap_lanes(pair)
+        own_inv = jnp.broadcast_to(inv[:, k : k + 1], (LANES, LANES))
+        own_root = jnp.broadcast_to(root[:, k : k + 1], (LANES, LANES))
+        all_inv[at, :] = own_inv
+        all_root[at, :] = own_root
+        weights_ref[at, :] = (0.5 * own_inv * start).astype(bf16)
+        correlation += jnp.sum(own_root * start, axis=0, keepdims=True)
         total += jnp.sum(
             jnp.broadcast_to(tall[:, k : k + 1], (LANES, LANES)), axis=0, keepdims=True
         )
-    correlation = jnp.zeros((1, LANES), f32)
-    for j in range(DEPTH):
-        for h, start in enumerate(spread_lanes(got_ref[j, :HALF, :])):
-            at = slice(j * DOCS + h * HALF, j * DOCS + (h + 1) * HALF)
-            weights_ref[at, :] = (all_inv[at, :] * start).astype(bf16)
-            correlation += jnp.sum(all_root[at, :] * start, axis=0, keepdims=True)
-    first = lax.axis_index("z") * DOCS
+    first = (lax.axis_index("zl") * SIZES["zh"] + lax.axis_index("zh")) * DOCS
     top = pl.ds(pl.multiple_of(first, HALF), HALF)
     low = pl.ds(pl.multiple_of(first + HALF, HALF), HALF)
     for whole, own in ((all_inv, inv_ref), (all_root, root_ref)):
@@ -212,7 +221,7 @@
     inv, root = inv_ref[...], root_ref[...]
     vectors = inv * sums - root * (terms[0:1] / terms[1:2])
     out_ref[:, :HALF, :] = jnp.broadcast_to(
-        (inv * vectors).astype(bf16)[None], (DEPTH, HALF, LANES)
+        (0.5 * inv * vectors).astype(bf16)[None], (DEPTH, HALF, LANES)
     )
     correlation = jnp.sum(root * vectors, axis=0, keepdims=True)
     hi, mid = two_parts(correlation + swap_lanes(correlation))
@@ -296,35 +305,37 @@
 
 def local(embeddings, start_vectors):
     all_docs = embeddings.shape[0] * lax.axis_size(AXES)
-    plane, depth = call(
+    width = E + 2 * K
+    plane, line = call(
         unit_kernel,
-        [shape(PEERS, DOCS, E, dtype=bf16), shape(DEPTH, DOCS, E, dtype=bf16)],
-        [embeddings],
-    )
-    own_rows, depth = lax.optimization_barrier((exchange(plane, PLANE), depth))
-    own_rows, columns = lax.optimization_barrier((own_rows, exchange(depth, ("z",))))
+        [shape(PEERS, DOCS, E, dtype=bf16), shape(SIZES["zh"], DOCS, width, dtype=bf16)],
+        [embeddings, start_vectors.T],
+    )
+    same, plane = lax.optimization_barrier((exchange(line, ("zh",)), plane))
+    same = same.reshape(COLUMNS // 2, width)
+    other = lax.ppermute(same, "zl", [(0, 1), (1, 0)])
+    own_rows, other = lax.optimization_barrier((exchange(plane, PLANE), other))
     own_rows = own_rows.reshape(ROWS, E)
-    columns = columns.reshape(COLUMNS, E)
     other_rows = swap_core(own_rows)
 
     tile = shape(ROWS, COLUMNS, dtype=bf16)
     acc = pltpu.VMEM((8, COLUMNS), f32)
     flops = 2 * ROWS * COLUMNS * E
-    own_tile, sums = call(
+    own_tile, sums, columns = call(
         functools.partial(tile_kernel, False),
-        [tile, shape(8, COLUMNS)],
-        [own_rows, columns],
+        [tile, shape(8, COLUMNS), shape(COLUMNS, width, dtype=bf16)],
+        [own_rows, same, other],
         [acc],
         flops,
     )
     other_tile, sums = call(
         functools.partial(tile_kernel, True),
-        [tile, shape(DEPTH, HALF + 16, LANES)],
-        [other_rows, columns, sums, start_vectors.T],
+        [tile, shape(DEPTH, 16, LANES)],
+        [other_rows, columns, sums],
         [acc],
         flops,
     )
-    sums = exchange(sums, ("z",))
+    sums = exchange(sums, LINE)
 
     flops = 2 * ROWS * COLUMNS * LANES
     sent = shape(PEERS, HALF + 8, LANES)
@@ -334,7 +345,7 @@
     mine, packed, inv, root = call(
         first_kernel,
         [sent, weights, own, own],
-        [other_tile, sums],
+        [other_tile, sums, columns],
         [spread, spread],
         flops,
     )
@@ -347,7 +358,7 @@
         [shape(DEPTH, HALF + 16, LANES, dtype=bf16), shape(8, LANES)],
         [got, inv, root],
     )
-    got = exchange(total, ("z",))
+    got = exchange(total, LINE)
     mine, packed = call(second_kernel, [sent, weights], [other_tile, got], (), flops)
     theirs = swap_core(mine)
     (mine,) = call(again_kernel, [sent], [own_tile, packed, mine], (), flops)
@@ -355,7 +366,7 @@
     got = exchange(total, PLANE)
     gram = shape(PEERS, K // 2, LANES)
     vectors, total = call(gram_kernel, [own, gram], [got, inv, root, terms])
-    (total,) = call(fold_kernel, [gram], [exchange(total, ("z", "core"))])
+    (total,) = call(fold_kernel, [gram], [exchange(total, (*LINE, "core"))])
     got = exchange(total, PLANE)
     (spectral,) = call(
         functools.partial(solve_kernel, math.sqrt(all_docs)), [shape(K, DOCS)], [got, vectors]

time: 183 us -> 167 us (0.913)
  blocking collectives: 146 us -> 103 us
  waiting for transfers between devices: 0.01 us -> 17.6 us
  starting transfers between devices: 7.8 us -> 18 us
    all_to_all x8 -> x7, blocking collectives: 146 us -> 103 us  [exchange(): return lax.all_to_all(value, axes, 0, 0, tiled=True)]
    ppermute x0 -> x1, waiting for transfers between devices: none -> 9.41 us  [local(): other = lax.ppermute(same, 'zl', [(0, 1), (1, 0)])]
    all_to_all x0 -> x1, waiting for transfers between devices: none -> 8.21 us  [exchange(): return lax.all_to_all(value, axes, 0, 0, tiled=True)]
    all_to_all x0 -> x1, starting transfers between devices: none -> 6.76 us  [exchange(): return lax.all_to_all(value, axes, 0, 0, tiled=True)]
    ppermute x3, starting transfers between devices: 7.8 us -> 9.81 us  [swap_core(): return lax.ppermute(value, 'core', [(0, 1), (1, 0)])]
  transfers between devices with their start and end apart: 3 -> 5, of which waited for: 0 -> 2; matrix products, arithmetic and copies ran while one was open for 0% -> 0% of each run, Pallas kernels for 6% -> 6%
where the time goes in v3:
time: 167 us
  blocking collectives  103 us (62%)
  Pallas kernels  25.7 us (15%)
  starting transfers between devices  18 us (11%)
  waiting for transfers between devices  17.6 us (11%)
  local copies, waits for them, and re-layouts  1.73 us (1%)
    all_to_all x7, blocking collectives, exchange(): return lax.all_to_all(value, axes, 0, 0, tiled=True)  103 us
    pallas_call x13, Pallas kernels, call(): pl.pallas_call(kernel, out_shape=tuple(outs), in_specs=[vmem] * len(args)...  25.7 us
    ppermute x3, starting transfers between devices, swap_core(): return lax.ppermute(value, 'core', [(0, 1), (1, 0)])  9.81 us
    ppermute x1, waiting for transfers between devices, local(): other = lax.ppermute(same, 'zl', [(0, 1), (1, 0)])  9.41 us
    all_to_all x1, waiting for transfers between devices, exchange(): return lax.all_to_all(value, axes, 0, 0, tiled=True)  8.21 us
    all_to_all x1, starting transfers between devices, exchange(): return lax.all_to_all(value, axes, 0, 0, tiled=True)  6.76 us
  transfers between devices with their start and end apart: 5, of which 2 were waited for; matrix products, arithmetic and copies ran while one was open for 0% of the time, Pallas kernels for 6%

profile of v3, /device:TPU:1, one launch (start us, length us, event | category | flops | bytes accessed | tf_op | source)
XLA Modules:
  0.0 166.6 jit_solution(10947526415714133675)
XLA Ops:
  0.0 0.0 copy-start
  0.0 0.9 copy-done
  0.9 0.8 copy-done.1
  1.7 1.4 shard_map.28
  3.2 24.2 %all_to_all.40 = bf16[4,192,384]{2,1,0:T(8,128)(2,1)S(1)} all-to-all(bf16[4,192,384]{2,1,0:T(8,128)(2,1)S(1)} %get-tuple-element.26), channel_id=1, replica_groups=mesh['zh'=4,'zl'=2,'x'=4,'y'=4,'core'=2] {'zh'}, dimensions={0} | all-to-all | bytes 1179648 | tf_op jit(solution)/shard_map/all_to_all | solution.py:299
  27.4 6.8 %all-to-all-start.1 = ((bf16[16,192,256]{2,1,0:T(8,128)(2,1)}), bf16[16,192,256]{2,1,0:T(8,128)(2,1)S(1)}, u32[]{:S(2)}, u32[]{:S(2)}) async-start(bf16[16,192,256]{2,1,0:T(8,128)(2,1)} %get-tuple-element.28), calls=%async_computation.1 | async-start | bytes 3145728 | tf_op jit(solution)/shard_map/all_to_all | solution.py:299
  34.2 1.4 collective-permute-start
  35.6 9.4 %collective-permute-done.refs_2_ = bf16[768,384]{1,0:T(8,128)(2,1)S(1)} collective-permute-done((bf16[768,384]{1,0:T(8,128)(2,1)S(1)}, bf16[768,384]{1,0:T(8,128)(2,1)S(1)}, u32[]{:S(2)}, u32[]{:S(2)}) %collective-permute-start) | collective-permute-done | bytes 589856 | tf_op jit(solution)/shard_map/ppermute | solution.py:316
  45.0 8.2 %all-to-all-done.1 = bf16[16,192,256]{2,1,0:T(8,128)(2,1)S(1)} async-done(((bf16[16,192,256]{2,1,0:T(8,128)(2,1)}), bf16[16,192,256]{2,1,0:T(8,128)(2,1)S(1)}, u32[]{:S(2)}, u32[]{:S(2)}) %all-to-all-start.1) | async-done | bytes 1572896 | tf_op jit(solution)/shard_map/all_to_all | solution.py:299
  53.2 5.6 %collective-permute-start.1 = (bf16[3072,256]{1,0:T(8,128)(2,1)S(1)}, bf16[3072,256]{1,0:T(8,128)(2,1)S(1)}, u32[]{:S(2)}, u32[]{:S(2)}) collective-permute-start(bf16[3072,256]{1,0:T(8,128)(2,1)S(1)} %bitcast.4), channel_id=1, source_target_pairs={{0,1},{1,0},{2,3},{3,2},{4,5},{5,4},{6,7},{7,6},{8,9},{9,8},{10,11... | collective-permute-start | bytes 4718600 | tf_op jit(solution)/shard_map/ppermute | solution.py:303
  58.8 4.2 %shard_map.29 = (bf16[3072,1536]{1,0:T(8,128)(2,1)S(1)}, f32[8,1536]{1,0:T(8,128)S(1)}, bf16[1536,384]{1,0:T(8,128)(2,1)S(1)}) custom-call(bf16[3072,256]{1,0:T(8,128)(2,1)S(1)} %bitcast.5, bf16[768,384]{1,0:T(8,128)(2,1)S(1)} %bitcast.7, bf16[768,384]{1,0:T(8,128)(2,1)S(1)} %collective-permute-done.refs_2_), custom_call_target="tpu_custom_call" | custom-call | flops 2415919104 | bytes 13418496 | tf_op jit(solution)/shard_map/pallas_call | solution.py:45
  63.0 0.0 collective-permute-done.1.refs_0_
  63.0 4.1 %shard_map.30 = (bf16[3072,1536]{1,0:T(8,128)(2,1)S(1)}, f32[8,16,128]{2,1,0:T(8,128)S(1)}) custom-call(bf16[3072,256]{1,0:T(8,128)(2,1)S(1)} %collective-permute-done.1.refs_0_, bf16[1536,384]{1,0:T(8,128)(2,1)S(1)} %get-tuple-element.33.refs_1_.cols_ref, f32[8,1536]{1,0:T(8,128)S(1)} %get-tuple-element.34.refs_2_), custom_call_target="tpu_custom_call" | custom-call | flops 2415919104 | bytes 12304384 | tf_op jit(solution)/shard_map/pallas_call | solution.py:45
  67.1 10.7 %all_to_all.41.sums_ref = f32[8,16,128]{2,1,0:T(8,128)S(1)} all-to-all(f32[8,16,128]{2,1,0:T(8,128)S(1)} %get-tuple-element.36), channel_id=1, replica_groups=mesh['zh'=4,'zl'=2,'x'=4,'y'=4,'core'=2] {'zl','zh'}, dimensions={0} | all-to-all | bytes 131072 | tf_op jit(solution)/shard_map/all_to_all | solution.py:299
  77.8 3.7 %shard_map.31 = (f32[16,104,128]{2,1,0:T(8,128)S(1)}, bf16[1536,128]{1,0:T(8,128)(2,1)S(1)}, f32[96,128]{1,0:T(8,128)S(1)}, f32[96,128]{1,0:T(8,128)S(1)}) custom-call(bf16[3072,1536]{1,0:T(8,128)(2,1)S(1)} %get-tuple-element.35.tile_ref, f32[8,16,128]{2,1,0:T(8,128)S(1)} %all_to_all.41.sums_ref, bf16[1536,384]{1,0:T(8,128)(2,1)S(1)} %get-tuple-element.33.refs_1_.cols_ref), custom_call_target="tpu_custom_call" | custom-call | flops 1207959552 | bytes 12025856 | tf_op jit(solution)/shard_map/pallas_call | solution.py:45
  81.5 1.4 collective-permute-start.2
  82.9 2.8 %shard_map.32.own_ref = f32[16,104,128]{2,1,0:T(8,128)S(1)} custom-call(bf16[3072,1536]{1,0:T(8,128)(2,1)S(1)} %get-tuple-element.32.tile_ref, bf16[1536,128]{1,0:T(8,128)(2,1)S(1)} %get-tuple-element.37.weights_ref, f32[16,104,128]{2,1,0:T(8,128)S(1)} %get-tuple-element.38.other_ref), custom_call_target="tpu_custom_call" | custom-call | flops 1207959552 | bytes 11534336 | tf_op jit(solution)/shard_map/pallas_call | solution.py:45
  85.7 0.0 collective-permute-done.2.other_ref
  85.7 0.1 shard_map.33
  85.8 12.3 %all_to_all.42.got_ref = bf16[16,112,128]{2,1,0:T(8,128)(2,1)S(1)} all-to-all(bf16[16,112,128]{2,1,0:T(8,128)(2,1)S(1)} %shard_map.33), channel_id=1, replica_groups=mesh['zh'=4,'zl'=2,'x'=4,'y'=4,'core'=2] {'x','y'}, dimensions={0} | all-to-all | bytes 917504 | tf_op jit(solution)/shard_map/all_to_all | solution.py:299
  98.1 0.2 shard_map.34
  98.3 10.0 %all_to_all.43.got_ref = bf16[8,112,128]{2,1,0:T(8,128)(2,1)S(1)} all-to-all(bf16[8,112,128]{2,1,0:T(8,128)(2,1)S(1)} %get-tuple-element.41), channel_id=1, replica_groups=mesh['zh'=4,'zl'=2,'x'=4,'y'=4,'core'=2] {'zl','zh'}, dimensions={0} | all-to-all | bytes 458752 | tf_op jit(solution)/shard_map/all_to_all | solution.py:299
  108.3 2.9 %shard_map.35 = (f32[16,104,128]{2,1,0:T(8,128)S(1)}, bf16[1536,128]{1,0:T(8,128)(2,1)S(1)}) custom-call(bf16[3072,1536]{1,0:T(8,128)(2,1)S(1)} %get-tuple-element.35.tile_ref, bf16[8,112,128]{2,1,0:T(8,128)(2,1)S(1)} %all_to_all.43.got_ref), custom_call_target="tpu_custom_call" | custom-call | flops 1207959552 | bytes 10911744 | tf_op jit(solution)/shard_map/pallas_call | solution.py:45
  111.2 2.8 %collective-permute-start.3 = (f32[16,104,128]{2,1,0:T(8,128)S(1)}, f32[16,104,128]{2,1,0:T(8,128)S(1)}, u32[]{:S(2)}, u32[]{:S(2)}) collective-permute-start(f32[16,104,128]{2,1,0:T(8,128)S(1)} %get-tuple-element.43.other_ref), channel_id=1, source_target_pairs={{0,1},{1,0},{2,3},{3,2},{4,5},{5,4},{6,7},{7,6},{8,9},{9,8},{10,11... | collective-permute-start | bytes 2555912 | tf_op jit(solution)/shard_map/ppermute | solution.py:303
  113.9 2.8 %shard_map.36.own_ref = f32[16,104,128]{2,1,0:T(8,128)S(1)} custom-call(bf16[3072,1536]{1,0:T(8,128)(2,1)S(1)} %get-tuple-element.32.tile_ref, bf16[1536,128]{1,0:T(8,128)(2,1)S(1)} %get-tuple-element.42.weights_ref, f32[16,104,128]{2,1,0:T(8,128)S(1)} %get-tuple-element.43.other_ref), custom_call_target="tpu_custom_call" | custom-call | flops 1207959552 | bytes 11534336 | tf_op jit(solution)/shard_map/pallas_call | solution.py:45
  116.7 0.0 collective-permute-done.3.other_ref
  116.7 0.1 shard_map.37
  116.8 17.8 %all_to_all.44.got_ref = f32[16,104,128]{2,1,0:T(8,128)S(1)} all-to-all(f32[16,104,128]{2,1,0:T(8,128)S(1)} %shard_map.37), channel_id=1, replica_groups=mesh['zh'=4,'zl'=2,'x'=4,'y'=4,'core'=2] {'x','y'}, dimensions={0} | all-to-all | bytes 1703936 | tf_op jit(solution)/shard_map/all_to_all | solution.py:299
  134.7 0.4 shard_map.38
  135.1 17.3 %all_to_all.45.got_ref = f32[16,32,128]{2,1,0:T(8,128)S(1)} all-to-all(f32[16,32,128]{2,1,0:T(8,128)S(1)} %get-tuple-element.45), channel_id=1, replica_groups=mesh['zh'=4,'zl'=2,'x'=4,'y'=4,'core'=2] {'zl','zh','core'}, dimensions={0} | all-to-all | bytes 524288 | tf_op jit(solution)/shard_map/all_to_all | solution.py:299
  152.5 11.2 %all_to_all.46.got_ref = f32[16,32,128]{2,1,0:T(8,128)S(1)} all-to-all(f32[16,32,128]{2,1,0:T(8,128)S(1)} %shard_map.39), channel_id=1, replica_groups=mesh['zh'=4,'zl'=2,'x'=4,'y'=4,'core'=2] {'x','y'}, dimensions={0} | all-to-all | bytes 524288 | tf_op jit(solution)/shard_map/all_to_all | solution.py:299
  163.6 3.0 %shard_map.40 = f32[64,192]{1,0:T(8,128)} custom-call(f32[16,32,128]{2,1,0:T(8,128)S(1)} %all_to_all.46.got_ref, f32[96,128]{1,0:T(8,128)S(1)} %get-tuple-element.46.vectors_ref), custom_call_target="tpu_custom_call" | custom-call | bytes 360448 | tf_op jit(solution)/shard_map/pallas_call | solution.py:45
  (2 shorter events, 0.0 us)
Async XLA Ops:
  0.0 0.9 copy-start
  0.9 0.8 copy-start.1
  27.4 25.8 %all-to-all-start.1 = ((bf16[16,192,256]{2,1,0:T(8,128)(2,1)}), bf16[16,192,256]{2,1,0:T(8,128)(2,1)S(1)}, u32[]{:S(2)}, u32[]{:S(2)}) async-start(bf16[16,192,256]{2,1,0:T(8,128)(2,1)} %get-tuple-element.28), calls=%async_computation.1 | async-start | bytes 3145728 | tf_op jit(solution)/shard_map/all_to_all | solution.py:299
  34.2 10.8 %collective-permute-start = (bf16[768,384]{1,0:T(8,128)(2,1)S(1)}, bf16[768,384]{1,0:T(8,128)(2,1)S(1)}, u32[]{:S(2)}, u32[]{:S(2)}) collective-permute-start(bf16[768,384]{1,0:T(8,128)(2,1)S(1)} %bitcast.6), channel_id=1, source_target_pairs={{0,32},{32,0},{1,33},{33,1},{2,34},{34,2},{3,35},{35,3},{4,36},{36... | collective-permute-start | bytes 1769480 | tf_op jit(solution)/shard_map/ppermute | solution.py:316
  53.2 9.9 %collective-permute-start.1 = (bf16[3072,256]{1,0:T(8,128)(2,1)S(1)}, bf16[3072,256]{1,0:T(8,128)(2,1)S(1)}, u32[]{:S(2)}, u32[]{:S(2)}) collective-permute-start(bf16[3072,256]{1,0:T(8,128)(2,1)S(1)} %bitcast.4), channel_id=1, source_target_pairs={{0,1},{1,0},{2,3},{3,2},{4,5},{5,4},{6,7},{7,6},{8,9},{9,8},{10,11... | collective-permute-start | bytes 4718600 | tf_op jit(solution)/shard_map/ppermute | solution.py:303
  81.5 4.2 %collective-permute-start.2 = (f32[16,104,128]{2,1,0:T(8,128)S(1)}, f32[16,104,128]{2,1,0:T(8,128)S(1)}, u32[]{:S(2)}, u32[]{:S(2)}) collective-permute-start(f32[16,104,128]{2,1,0:T(8,128)S(1)} %get-tuple-element.38.other_ref), channel_id=1, source_target_pairs={{0,1},{1,0},{2,3},{3,2},{4,5},{5,4},{6,7},{7,6},{8,9},{9,8},{10,11... | collective-permute-start | bytes 2555912 | tf_op jit(solution)/shard_map/ppermute | solution.py:303
  111.2 5.6 %collective-permute-start.3 = (f32[16,104,128]{2,1,0:T(8,128)S(1)}, f32[16,104,128]{2,1,0:T(8,128)S(1)}, u32[]{:S(2)}, u32[]{:S(2)}) collective-permute-start(f32[16,104,128]{2,1,0:T(8,128)S(1)} %get-tuple-element.43.other_ref), channel_id=1, source_target_pairs={{0,1},{1,0},{2,3},{3,2},{4,5},{5,4},{6,7},{7,6},{8,9},{9,8},{10,11... | collective-permute-start | bytes 2555912 | tf_op jit(solution)/shard_map/ppermute | solution.py:303

commit v4 on v3

--- a/solution.py
+++ b/solution.py
@@ -25,10 +25,10 @@
 K = 64
 COLUMNS = DEPTH * DOCS
 ROWS = PEERS * DOCS
-ROW_BLOCK = 512
+ROW_BLOCK = 3072
 COLUMN_BLOCK = 256
 LANES = 128
-PIVOTS = 4
+PIVOTS = 8
 
 bf16 = jnp.bfloat16
 f32 = jnp.float32
@@ -72,17 +72,20 @@
     return hi, (value - hi).astype(bf16).astype(f32)
 
 
-def unit_kernel(emb_ref, start_ref, plane_ref, line_ref):
+def unit_kernel(emb_ref, line_ref):
     wide = emb_ref[...].astype(f32)
     unit = wide * lax.rsqrt(jnp.sum(wide * wide, axis=1, keepdims=True) + 1e-06)
-    unit = unit.astype(bf16)
-    plane_ref[...] = jnp.broadcast_to((unit * (sharpness / 2))[None], plane_ref.shape)
-    line_ref[:, :, :E] = jnp.broadcast_to(unit[None], (SIZES["zh"], DOCS, E))
+    line_ref[...] = jnp.broadcast_to(unit.astype(bf16)[None], line_ref.shape)
+
+
+def plane_kernel(line_ref, plane_ref):
+    plane_ref[...] = jnp.broadcast_to((line_ref[0] * (sharpness / 2))[None], plane_ref.shape)
+
+
+def pack_kernel(start_ref, out_ref):
     start = jnp.concatenate([start_ref[...], jnp.zeros((K, 2 * LANES - DOCS), f32)], axis=1)
-    start = jnp.concatenate([start, jnp.zeros_like(start)], axis=0).T[:DOCS]
-    hi, mid = two_parts(start)
-    pair = jnp.where(left_lanes(hi), hi, swap_lanes(mid)).astype(bf16)
-    line_ref[:, :, E:] = jnp.broadcast_to(pair[None], (SIZES["zh"], DOCS, 2 * K))
+    start = jnp.concatenate([start, jnp.zeros_like(start)], axis=0).T
+    out_ref[0] = start[:HALF] + swap_lanes(start[HALF:DOCS])
 
 
 def tile_kernel(last, *refs):
@@ -103,7 +106,7 @@
         for c in range(COLUMNS // COLUMN_BLOCK):
             where = slice(c * COLUMN_BLOCK, (c + 1) * COLUMN_BLOCK)
             scores = lax.dot_general(
-                rows, cols_ref[where, :E], (((1,), (1,)), ((), ())), preferred_element_type=f32
+                rows, cols_ref[where, :], (((1,), (1,)), ((), ())), preferred_element_type=f32
             )
             entry = jnp.tanh(scores - sharpness * threshold / 2) + 1.0
             tile_ref[at, where] = entry.astype(bf16)
@@ -123,7 +126,7 @@
 
 
 def multiply(tile_ref, weights_ref, out_ref, terms):
-    chunks = 8
+    chunks = 16
 
     def block(i, _):
         rows = chunks * DOCS
@@ -148,6 +151,12 @@
     for i, value in enumerate(values):
         block = jnp.where(index == i, jnp.broadcast_to(value, (8, LANES)), block)
     return block
+
+
+def spread_lanes(packed):
+    other = swap_lanes(packed)
+    left = left_lanes(packed)
+    return jnp.where(left, packed, other), jnp.where(left, other, packed)
 
 
 def spread_lanes(packed):
@@ -180,6 +189,49 @@
             jnp.broadcast_to(tall[:, k : k + 1], (LANES, LANES)), axis=0, keepdims=True
         )
     first = (lax.axis_index("zl") * SIZES["zh"] + lax.axis_index("zh")) * DOCS
+    top = pl.ds(pl.multiple_of(first, HALF), HALF)
+    low = pl.ds(pl.multiple_of(first + HALF, HALF), HALF)
+    for whole, own in ((all_inv, inv_ref), (all_root, root_ref)):
+        upper = whole[top, :]
+        own[...] = jnp.where(left_lanes(upper), upper, whole[low, :])
+    multiply(tile_ref, weights_ref, out_ref, rows_of(correlation, total))
+
+
+def first_kernel(
+    tile_ref,
+    sums_ref,
+    same_ref,
+    other_ref,
+    out_ref,
+    weights_ref,
+    inv_ref,
+    root_ref,
+    all_inv,
+    all_root,
+):
+    degree = jnp.sum(sums_ref[...], axis=0)
+    blocks = COLUMNS // LANES
+    degree = jnp.where(lax.broadcasted_iota(jnp.int32, degree.shape, 0) < blocks, degree, 1.0)
+    tall = jnp.concatenate([degree, jnp.ones((LANES - degree.shape[0], LANES), f32)], axis=0).T
+    inv, root = root_of(tall)
+    total = jnp.zeros((1, LANES), f32)
+    for k in range(blocks):
+        at = slice(k * LANES, (k + 1) * LANES)
+        all_inv[at, :] = jnp.broadcast_to(inv[:, k : k + 1], (LANES, LANES))
+        all_root[at, :] = jnp.broadcast_to(root[:, k : k + 1], (LANES, LANES))
+        total += jnp.sum(
+            jnp.broadcast_to(tall[:, k : k + 1], (LANES, LANES)), axis=0, keepdims=True
+        )
+    zh, zl = lax.axis_index("zh"), lax.axis_index("zl")
+    correlation = jnp.zeros((1, LANES), f32)
+    for side, start_ref in ((zl, same_ref), (1 - zl, other_ref)):
+        for j, flip in enumerate((0, 2, 1, 3)):
+            first = (side * SIZES["zh"] + jnp.bitwise_xor(zh, flip)) * DOCS
+            for h, start in enumerate(spread_lanes(start_ref[j])):
+                at = pl.ds(pl.multiple_of(first + h * HALF, HALF), HALF)
+                weights_ref[at, :] = (0.5 * all_inv[at, :] * start).astype(bf16)
+                correlation += jnp.sum(all_root[at, :] * start, axis=0, keepdims=True)
+    first = (zl * SIZES["zh"] + zh) * DOCS
     top = pl.ds(pl.multiple_of(first, HALF), HALF)
     low = pl.ds(pl.multiple_of(first + HALF, HALF), HALF)
     for whole, own in ((all_inv, inv_ref), (all_root, root_ref)):
@@ -299,31 +351,31 @@
     return lax.all_to_all(value, axes, 0, 0, tiled=True)
 
 
-def swap_core(value):
-    return lax.ppermute(value, "core", [(0, 1), (1, 0)])
+def flip(value, axis, bits):
+    return lax.ppermute(value, axis, [(i, i ^ bits) for i in range(SIZES[axis])])
 
 
 def local(embeddings, start_vectors):
     all_docs = embeddings.shape[0] * lax.axis_size(AXES)
-    width = E + 2 * K
-    plane, line = call(
-        unit_kernel,
-        [shape(PEERS, DOCS, E, dtype=bf16), shape(SIZES["zh"], DOCS, width, dtype=bf16)],
-        [embeddings, start_vectors.T],
-    )
-    same, plane = lax.optimization_barrier((exchange(line, ("zh",)), plane))
-    same = same.reshape(COLUMNS // 2, width)
-    other = lax.ppermute(same, "zl", [(0, 1), (1, 0)])
-    own_rows, other = lax.optimization_barrier((exchange(plane, PLANE), other))
+    (line,) = call(unit_kernel, [shape(SIZES["zh"], DOCS, E, dtype=bf16)], [embeddings])
+    (plane,) = call(plane_kernel, [shape(PEERS, DOCS, E, dtype=bf16)], [line])
+    (start,) = call(pack_kernel, [shape(1, HALF, LANES)], [start_vectors.T])
+    same, plane, start = lax.optimization_barrier((exchange(line, ("zh",)), plane, start))
+    same = same.reshape(COLUMNS // 2, E)
+    other = flip(same, "zl", 1)
+    start = jnp.concatenate([start, flip(start, "zh", 2)], axis=0)
+    start = jnp.concatenate([start, flip(start, "zh", 1)], axis=0)
+    own_rows, other, start = lax.optimization_barrier((exchange(plane, PLANE), other, start))
+    other_start = flip(start, "zl", 1)
     own_rows = own_rows.reshape(ROWS, E)
-    other_rows = swap_core(own_rows)
+    other_rows = flip(own_rows, "core", 1)
 
     tile = shape(ROWS, COLUMNS, dtype=bf16)
     acc = pltpu.VMEM((8, COLUMNS), f32)
     flops = 2 * ROWS * COLUMNS * E
     own_tile, sums, columns = call(
         functools.partial(tile_kernel, False),
-        [tile, shape(8, COLUMNS), shape(COLUMNS, width, dtype=bf16)],
+        [tile, shape(8, COLUMNS), shape(COLUMNS, E, dtype=bf16)],
         [own_rows, same, other],
         [acc],
         flops,
@@ -335,6 +387,7 @@
         [acc],
         flops,
     )
+    sums, other_start = lax.optimization_barrier((sums, other_start))
     sums = exchange(sums, LINE)
 
     flops = 2 * ROWS * COLUMNS * LANES
@@ -345,11 +398,11 @@
     mine, packed, inv, root = call(
         first_kernel,
         [sent, weights, own, own],
-        [other_tile, sums, columns],
+        [other_tile, sums, start, other_start],
         [spread, spread],
         flops,
     )
-    theirs = swap_core(mine)
+    theirs = flip(mine, "core", 1)
     (mine,) = call(again_kernel, [sent], [own_tile, packed, mine], (), flops)
     (total,) = call(narrow_kernel, [shape(PEERS, HALF + 16, LANES, dtype=bf16)], [mine, theirs])
     got = exchange(total, PLANE)
@@ -360,7 +413,7 @@
     )
     got = exchange(total, LINE)
     mine, packed = call(second_kernel, [sent, weights], [other_tile, got], (), flops)
-    theirs = swap_core(mine)
+    theirs = flip(mine, "core", 1)
     (mine,) = call(again_kernel, [sent], [own_tile, packed, mine], (), flops)
     (total,) = call(add_kernel, [sent], [mine, theirs])
     got = exchange(total, PLANE)

time: 167 us -> 160 us (0.958)
  blocking collectives: 103 us -> 80.3 us
  starting transfers between devices: 18 us -> 33.2 us
  waiting for transfers between devices: 17.6 us -> 20.9 us
    all_to_all x7 -> x6, blocking collectives: 103 us -> 80.3 us  [exchange(): return lax.all_to_all(value, axes, 0, 0, tiled=True)]
    all_to_all x1 -> x2, starting transfers between devices: 6.76 us -> 15.8 us  [exchange(): return lax.all_to_all(value, axes, 0, 0, tiled=True)]
    ppermute x4 -> x7, starting transfers between devices: 11.2 us -> 17.5 us  [flip(): lax.ppermute(value, axis, [(i, i ^ bits) for i in range(SIZES[axis])])]
    all_to_all x1 -> x2, waiting for transfers between devices: 8.21 us -> 11.1 us  [exchange(): return lax.all_to_all(value, axes, 0, 0, tiled=True)]
    pallas_call x13 -> x15, Pallas kernels: 25.7 us -> 24.3 us  [call(): pl.pallas_call(kernel, out_shape=tuple(outs), in_specs=[vmem] * len(args)...]
    ppermute x4 -> x7, waiting for transfers between devices: 9.42 us -> 9.76 us  [flip(): lax.ppermute(value, axis, [(i, i ^ bits) for i in range(SIZES[axis])])]
  transfers between devices with their start and end apart: 5 -> 9, of which waited for: 2 -> 4; matrix products, arithmetic and copies ran while one was open for 0% -> 0% of each run, Pallas kernels for 6% -> 9%
where the time goes in v4:
time: 160 us
  blocking collectives  80.3 us (50%)
  starting transfers between devices  33.2 us (21%)
  Pallas kernels  24.3 us (15%)
  waiting for transfers between devices  20.9 us (13%)
    all_to_all x6, blocking collectives, exchange(): return lax.all_to_all(value, axes, 0, 0, tiled=True)  80.3 us
    pallas_call x15, Pallas kernels, call(): pl.pallas_call(kernel, out_shape=tuple(outs), in_specs=[vmem] * len(args)...  24.3 us
    ppermute x7, starting transfers between devices, flip(): lax.ppermute(value, axis, [(i, i ^ bits) for i in range(SIZES[axis])])  17.5 us
    all_to_all x2, starting transfers between devices, exchange(): return lax.all_to_all(value, axes, 0, 0, tiled=True)  15.8 us
    all_to_all x2, waiting for transfers between devices, exchange(): return lax.all_to_all(value, axes, 0, 0, tiled=True)  11.1 us
    ppermute x7, waiting for transfers between devices, flip(): lax.ppermute(value, axis, [(i, i ^ bits) for i in range(SIZES[axis])])  9.76 us
  transfers between devices with their start and end apart: 9, of which 4 were waited for; matrix products, arithmetic and copies ran while one was open for 0% of the time, Pallas kernels for 9%

profile of v4, /device:TPU:1, one launch (start us, length us, event | category | flops | bytes accessed | tf_op | source)
XLA Modules:
  0.0 159.8 jit_solution(17740062408770865298)
XLA Ops:
  0.0 0.9 copy-done
  0.9 0.9 shard_map.28.line_ref
  1.8 9.0 %all-to-all-start = ((bf16[4,192,256]{2,1,0:T(8,128)(2,1)}), bf16[4,192,256]{2,1,0:T(8,128)(2,1)S(1)}, u32[]{:S(2)}, u32[]{:S(2)}) async-start(bf16[4,192,256]{2,1,0:T(8,128)(2,1)} %shard_map.28.line_ref), calls=%async_computation | async-start | bytes 786432 | tf_op jit(solution)/shard_map/all_to_all | solution.py:351
  10.8 2.4 %shard_map.29 = bf16[16,192,256]{2,1,0:T(8,128)(2,1)} custom-call(bf16[4,192,256]{2,1,0:T(8,128)(2,1)} %shard_map.28.line_ref), custom_call_target="tpu_custom_call" | custom-call | bytes 1966080 | tf_op jit(solution)/shard_map/pallas_call | solution.py:45
  13.1 0.2 shard_map.30
  13.3 7.9 %all-to-all-done = bf16[4,192,256]{2,1,0:T(8,128)(2,1)S(1)} async-done(((bf16[4,192,256]{2,1,0:T(8,128)(2,1)}), bf16[4,192,256]{2,1,0:T(8,128)(2,1)S(1)}, u32[]{:S(2)}, u32[]{:S(2)}) %all-to-all-start) | async-done | bytes 393248 | tf_op jit(solution)/shard_map/all_to_all | solution.py:351
  21.2 6.8 %all-to-all-start.1 = ((bf16[16,192,256]{2,1,0:T(8,128)(2,1)}), bf16[16,192,256]{2,1,0:T(8,128)(2,1)S(1)}, u32[]{:S(2)}, u32[]{:S(2)}) async-start(bf16[16,192,256]{2,1,0:T(8,128)(2,1)} %shard_map.29), calls=%async_computation.1 | async-start | bytes 3145728 | tf_op jit(solution)/shard_map/all_to_all | solution.py:351
  28.0 1.1 collective-permute-start
  29.1 2.0 %collective-permute-start.1 = (f32[1,96,128]{2,1,0:T(8,128)S(1)}, f32[1,96,128]{2,1,0:T(8,128)S(1)}, u32[]{:S(2)}, u32[]{:S(2)}) collective-permute-start(f32[1,96,128]{2,1,0:T(8,128)S(1)} %shard_map.30), channel_id=1, source_target_pairs={{0,128},{64,192},{128,0},{192,64},{1,129},{65,193},{129,1},{193,65... | collective-permute-start | bytes 147464 | tf_op jit(solution)/shard_map/ppermute | solution.py:355
  31.1 6.4 %collective-permute-done.1 = f32[1,96,128]{2,1,0:T(8,128)S(1)} collective-permute-done((f32[1,96,128]{2,1,0:T(8,128)S(1)}, f32[1,96,128]{2,1,0:T(8,128)S(1)}, u32[]{:S(2)}, u32[]{:S(2)}) %collective-permute-start.1) | collective-permute-done | bytes 49184 | tf_op jit(solution)/shard_map/ppermute | solution.py:355
  37.5 3.0 %collective-permute-start.2 = (f32[2,96,128]{2,1,0:T(8,128)S(1)}, f32[2,96,128]{2,1,0:T(8,128)S(1)}, u32[]{:S(2)}, u32[]{:S(2)}) collective-permute-start(f32[2,96,128]{2,1,0:T(8,128)S(1)} %pad_maximum_fusion.1), channel_id=1, source_target_pairs={{0,64},{64,0},{128,192},{192,128},{1,65},{65,1},{129,193},{193,129... | collective-permute-start | bytes 294920 | tf_op jit(solution)/shard_map/ppermute | solution.py:355
  40.5 3.3 %collective-permute-done.2 = f32[2,96,128]{2,1,0:T(8,128)S(1)} collective-permute-done((f32[2,96,128]{2,1,0:T(8,128)S(1)}, f32[2,96,128]{2,1,0:T(8,128)S(1)}, u32[]{:S(2)}, u32[]{:S(2)}) %collective-permute-start.2) | collective-permute-done | bytes 98336 | tf_op jit(solution)/shard_map/ppermute | solution.py:355
  43.9 3.2 %all-to-all-done.1 = bf16[16,192,256]{2,1,0:T(8,128)(2,1)S(1)} async-done(((bf16[16,192,256]{2,1,0:T(8,128)(2,1)}), bf16[16,192,256]{2,1,0:T(8,128)(2,1)S(1)}, u32[]{:S(2)}, u32[]{:S(2)}) %all-to-all-start.1) | async-done | bytes 1572896 | tf_op jit(solution)/shard_map/all_to_all | solution.py:351
  47.1 5.3 %collective-permute-start.3 = (bf16[3072,256]{1,0:T(8,128)(2,1)S(1)}, bf16[3072,256]{1,0:T(8,128)(2,1)S(1)}, u32[]{:S(2)}, u32[]{:S(2)}) collective-permute-start(bf16[3072,256]{1,0:T(8,128)(2,1)S(1)} %bitcast.4), channel_id=1, source_target_pairs={{0,1},{1,0},{2,3},{3,2},{4,5},{5,4},{6,7},{7,6},{8,9},{9,8},{10,11... | collective-permute-start | bytes 4718600 | tf_op jit(solution)/shard_map/ppermute | solution.py:355
  52.4 1.3 collective-permute-start.4
  53.7 3.2 %shard_map.31 = (bf16[3072,1536]{1,0:T(8,128)(2,1)S(1)}, f32[8,1536]{1,0:T(8,128)S(1)}, bf16[1536,256]{1,0:T(8,128)(2,1)S(1)}) custom-call(bf16[3072,256]{1,0:T(8,128)(2,1)S(1)} %bitcast.5, bf16[768,256]{1,0:T(8,128)(2,1)S(1)} %bitcast.7, bf16[768,256]{1,0:T(8,128)(2,1)S(1)} %collective-permute-done.refs_2_), custom_call_target="tpu_custom_call" | custom-call | flops 2415919104 | bytes 12632064 | tf_op jit(solution)/shard_map/pallas_call | solution.py:45
  57.0 3.3 %shard_map.32 = (bf16[3072,1536]{1,0:T(8,128)(2,1)S(1)}, f32[8,16,128]{2,1,0:T(8,128)S(1)}) custom-call(bf16[3072,256]{1,0:T(8,128)(2,1)S(1)} %collective-permute-done.3.refs_0_, bf16[1536,256]{1,0:T(8,128)(2,1)S(1)} %get-tuple-element.34.refs_1_, f32[8,1536]{1,0:T(8,128)S(1)} %get-tuple-element.35.refs_2_), custom_call_target="tpu_custom_call" | custom-call | flops 2415919104 | bytes 11911168 | tf_op jit(solution)/shard_map/pallas_call | solution.py:45
  60.2 10.0 %all_to_all.40.sums_ref = f32[8,16,128]{2,1,0:T(8,128)S(1)} all-to-all(f32[8,16,128]{2,1,0:T(8,128)S(1)} %get-tuple-element.39), channel_id=1, replica_groups=mesh['zh'=4,'zl'=2,'x'=4,'y'=4,'core'=2] {'zl','zh'}, dimensions={0} | all-to-all | bytes 131072 | tf_op jit(solution)/shard_map/all_to_all | solution.py:351
  70.3 3.3 %shard_map.33 = (f32[16,104,128]{2,1,0:T(8,128)S(1)}, bf16[1536,128]{1,0:T(8,128)(2,1)S(1)}, f32[96,128]{1,0:T(8,128)S(1)}, f32[96,128]{1,0:T(8,128)S(1)}) custom-call(bf16[3072,1536]{1,0:T(8,128)(2,1)S(1)} %get-tuple-element.36.tile_ref, f32[8,16,128]{2,1,0:T(8,128)S(1)} %all_to_all.40.sums_ref, f32[4,96,128]{2,1,0:T(8,128)S(1)} %pad_maximum_fusion.same_ref, ...), custom_call_target="tpu_custom_call" | custom-call | flops 1207959552 | bytes 11239424 | tf_op jit(solution)/shard_map/pallas_call | solution.py:45
  73.5 2.0 %collective-permute-start.5 = (f32[16,104,128]{2,1,0:T(8,128)S(1)}, f32[16,104,128]{2,1,0:T(8,128)S(1)}, u32[]{:S(2)}, u32[]{:S(2)}) collective-permute-start(f32[16,104,128]{2,1,0:T(8,128)S(1)} %get-tuple-element.42.other_ref), channel_id=1, source_target_pairs={{0,1},{1,0},{2,3},{3,2},{4,5},{5,4},{6,7},{7,6},{8,9},{9,8},{10,11... | collective-permute-start | bytes 2555912 | tf_op jit(solution)/shard_map/ppermute | solution.py:355
  75.5 2.6 %shard_map.34.own_ref = f32[16,104,128]{2,1,0:T(8,128)S(1)} custom-call(bf16[3072,1536]{1,0:T(8,128)(2,1)S(1)} %get-tuple-element.33.tile_ref, bf16[1536,128]{1,0:T(8,128)(2,1)S(1)} %get-tuple-element.41.weights_ref, f32[16,104,128]{2,1,0:T(8,128)S(1)} %get-tuple-element.42.other_ref), custom_call_target="tpu_custom_call" | custom-call | flops 1207959552 | bytes 11534336 | tf_op jit(solution)/shard_map/pallas_call | solution.py:45
  78.2 13.9 %all_to_all.41.got_ref = bf16[16,112,128]{2,1,0:T(8,128)(2,1)S(1)} all-to-all(bf16[16,112,128]{2,1,0:T(8,128)(2,1)S(1)} %shard_map.35), channel_id=1, replica_groups=mesh['zh'=4,'zl'=2,'x'=4,'y'=4,'core'=2] {'x','y'}, dimensions={0} | all-to-all | bytes 917504 | tf_op jit(solution)/shard_map/all_to_all | solution.py:351
  92.2 0.2 shard_map.36
  92.3 10.0 %all_to_all.42.got_ref = bf16[8,112,128]{2,1,0:T(8,128)(2,1)S(1)} all-to-all(bf16[8,112,128]{2,1,0:T(8,128)(2,1)S(1)} %get-tuple-element.45), channel_id=1, replica_groups=mesh['zh'=4,'zl'=2,'x'=4,'y'=4,'core'=2] {'zl','zh'}, dimensions={0} | all-to-all | bytes 458752 | tf_op jit(solution)/shard_map/all_to_all | solution.py:351
  102.3 2.7 %shard_map.37 = (f32[16,104,128]{2,1,0:T(8,128)S(1)}, bf16[1536,128]{1,0:T(8,128)(2,1)S(1)}) custom-call(bf16[3072,1536]{1,0:T(8,128)(2,1)S(1)} %get-tuple-element.36.tile_ref, bf16[8,112,128]{2,1,0:T(8,128)(2,1)S(1)} %all_to_all.42.got_ref), custom_call_target="tpu_custom_call" | custom-call | flops 1207959552 | bytes 10911744 | tf_op jit(solution)/shard_map/pallas_call | solution.py:45
  105.0 2.8 %collective-permute-start.6 = (f32[16,104,128]{2,1,0:T(8,128)S(1)}, f32[16,104,128]{2,1,0:T(8,128)S(1)}, u32[]{:S(2)}, u32[]{:S(2)}) collective-permute-start(f32[16,104,128]{2,1,0:T(8,128)S(1)} %get-tuple-element.47.other_ref), channel_id=1, source_target_pairs={{0,1},{1,0},{2,3},{3,2},{4,5},{5,4},{6,7},{7,6},{8,9},{9,8},{10,11... | collective-permute-start | bytes 2555912 | tf_op jit(solution)/shard_map/ppermute | solution.py:355
  107.8 2.6 %shard_map.38.own_ref = f32[16,104,128]{2,1,0:T(8,128)S(1)} custom-call(bf16[3072,1536]{1,0:T(8,128)(2,1)S(1)} %get-tuple-element.33.tile_ref, bf16[1536,128]{1,0:T(8,128)(2,1)S(1)} %get-tuple-element.46.weights_ref, f32[16,104,128]{2,1,0:T(8,128)S(1)} %get-tuple-element.47.other_ref), custom_call_target="tpu_custom_call" | custom-call | flops 1207959552 | bytes 11534336 | tf_op jit(solution)/shard_map/pallas_call | solution.py:45
  110.5 17.8 %all_to_all.43.got_ref = f32[16,104,128]{2,1,0:T(8,128)S(1)} all-to-all(f32[16,104,128]{2,1,0:T(8,128)S(1)} %shard_map.39), channel_id=1, replica_groups=mesh['zh'=4,'zl'=2,'x'=4,'y'=4,'core'=2] {'x','y'}, dimensions={0} | all-to-all | bytes 1703936 | tf_op jit(solution)/shard_map/all_to_all | solution.py:351
  128.4 0.4 shard_map.40
  128.8 17.3 %all_to_all.44.got_ref = f32[16,32,128]{2,1,0:T(8,128)S(1)} all-to-all(f32[16,32,128]{2,1,0:T(8,128)S(1)} %get-tuple-element.49), channel_id=1, replica_groups=mesh['zh'=4,'zl'=2,'x'=4,'y'=4,'core'=2] {'zl','zh','core'}, dimensions={0} | all-to-all | bytes 524288 | tf_op jit(solution)/shard_map/all_to_all | solution.py:351
  146.2 11.2 %all_to_all.45.got_ref = f32[16,32,128]{2,1,0:T(8,128)S(1)} all-to-all(f32[16,32,128]{2,1,0:T(8,128)S(1)} %shard_map.41), channel_id=1, replica_groups=mesh['zh'=4,'zl'=2,'x'=4,'y'=4,'core'=2] {'x','y'}, dimensions={0} | all-to-all | bytes 524288 | tf_op jit(solution)/shard_map/all_to_all | solution.py:351
  157.3 2.5 %shard_map.42 = f32[64,192]{1,0:T(8,128)} custom-call(f32[16,32,128]{2,1,0:T(8,128)S(1)} %all_to_all.45.got_ref, f32[96,128]{1,0:T(8,128)S(1)} %get-tuple-element.50.vectors_ref), custom_call_target="tpu_custom_call" | custom-call | bytes 360448 | tf_op jit(solution)/shard_map/pallas_call | solution.py:45
  (13 shorter events, 0.3 us)
Async XLA Ops:
  0.0 0.9 copy-start
  0.9 12.2 %copy-start.1 = (f32[192,64]{0,1:T(8,128)S(1)}, f32[192,64]{0,1:T(8,128)}, u32[]{:S(2)}) copy-start(f32[192,64]{0,1:T(8,128)} %param.3) | copy-start | bytes 147460
  1.8 19.5 %all-to-all-start = ((bf16[4,192,256]{2,1,0:T(8,128)(2,1)}), bf16[4,192,256]{2,1,0:T(8,128)(2,1)S(1)}, u32[]{:S(2)}, u32[]{:S(2)}) async-start(bf16[4,192,256]{2,1,0:T(8,128)(2,1)} %shard_map.28.line_ref), calls=%async_computation | async-start | bytes 786432 | tf_op jit(solution)/shard_map/all_to_all | solution.py:351
  21.2 25.8 %all-to-all-start.1 = ((bf16[16,192,256]{2,1,0:T(8,128)(2,1)}), bf16[16,192,256]{2,1,0:T(8,128)(2,1)S(1)}, u32[]{:S(2)}, u32[]{:S(2)}) async-start(bf16[16,192,256]{2,1,0:T(8,128)(2,1)} %shard_map.29), calls=%async_computation.1 | async-start | bytes 3145728 | tf_op jit(solution)/shard_map/all_to_all | solution.py:351
  28.0 15.9 %collective-permute-start = (bf16[768,256]{1,0:T(8,128)(2,1)S(1)}, bf16[768,256]{1,0:T(8,128)(2,1)S(1)}, u32[]{:S(2)}, u32[]{:S(2)}) collective-permute-start(bf16[768,256]{1,0:T(8,128)(2,1)S(1)} %bitcast.6), channel_id=1, source_target_pairs={{0,32},{32,0},{1,33},{33,1},{2,34},{34,2},{3,35},{35,3},{4,36},{36... | collective-permute-start | bytes 1179656 | tf_op jit(solution)/shard_map/ppermute | solution.py:355
  29.1 8.4 %collective-permute-start.1 = (f32[1,96,128]{2,1,0:T(8,128)S(1)}, f32[1,96,128]{2,1,0:T(8,128)S(1)}, u32[]{:S(2)}, u32[]{:S(2)}) collective-permute-start(f32[1,96,128]{2,1,0:T(8,128)S(1)} %shard_map.30), channel_id=1, source_target_pairs={{0,128},{64,192},{128,0},{192,64},{1,129},{65,193},{129,1},{193,65... | collective-permute-start | bytes 147464 | tf_op jit(solution)/shard_map/ppermute | solution.py:355
  37.5 6.4 %collective-permute-start.2 = (f32[2,96,128]{2,1,0:T(8,128)S(1)}, f32[2,96,128]{2,1,0:T(8,128)S(1)}, u32[]{:S(2)}, u32[]{:S(2)}) collective-permute-start(f32[2,96,128]{2,1,0:T(8,128)S(1)} %pad_maximum_fusion.1), channel_id=1, source_target_pairs={{0,64},{64,0},{128,192},{192,128},{1,65},{65,1},{129,193},{193,129... | collective-permute-start | bytes 294920 | tf_op jit(solution)/shard_map/ppermute | solution.py:355
  47.1 9.9 %collective-permute-start.3 = (bf16[3072,256]{1,0:T(8,128)(2,1)S(1)}, bf16[3072,256]{1,0:T(8,128)(2,1)S(1)}, u32[]{:S(2)}, u32[]{:S(2)}) collective-permute-start(bf16[3072,256]{1,0:T(8,128)(2,1)S(1)} %bitcast.4), channel_id=1, source_target_pairs={{0,1},{1,0},{2,3},{3,2},{4,5},{5,4},{6,7},{7,6},{8,9},{9,8},{10,11... | collective-permute-start | bytes 4718600 | tf_op jit(solution)/shard_map/ppermute | solution.py:355
  52.4 7.8 %collective-permute-start.4 = (f32[4,96,128]{2,1,0:T(8,128)S(1)}, f32[4,96,128]{2,1,0:T(8,128)S(1)}, u32[]{:S(2)}, u32[]{:S(2)}) collective-permute-start(f32[4,96,128]{2,1,0:T(8,128)S(1)} %pad_maximum_fusion.same_ref), channel_id=1, source_target_pairs={{0,32},{32,0},{1,33},{33,1},{2,34},{34,2},{3,35},{35,3},{4,36},{36... | collective-permute-start | bytes 589832 | tf_op jit(solution)/shard_map/ppermute | solution.py:355
  73.5 4.6 %collective-permute-start.5 = (f32[16,104,128]{2,1,0:T(8,128)S(1)}, f32[16,104,128]{2,1,0:T(8,128)S(1)}, u32[]{:S(2)}, u32[]{:S(2)}) collective-permute-start(f32[16,104,128]{2,1,0:T(8,128)S(1)} %get-tuple-element.42.other_ref), channel_id=1, source_target_pairs={{0,1},{1,0},{2,3},{3,2},{4,5},{5,4},{6,7},{7,6},{8,9},{9,8},{10,11... | collective-permute-start | bytes 2555912 | tf_op jit(solution)/shard_map/ppermute | solution.py:355
  105.0 5.4 %collective-permute-start.6 = (f32[16,104,128]{2,1,0:T(8,128)S(1)}, f32[16,104,128]{2,1,0:T(8,128)S(1)}, u32[]{:S(2)}, u32[]{:S(2)}) collective-permute-start(f32[16,104,128]{2,1,0:T(8,128)S(1)} %get-tuple-element.47.other_ref), channel_id=1, source_target_pairs={{0,1},{1,0},{2,3},{3,2},{4,5},{5,4},{6,7},{7,6},{8,9},{9,8},{10,11... | collective-permute-start | bytes 2555912 | tf_op jit(solution)/shard_map/ppermute | solution.py:355

commit v5 on v3

--- a/solution.py
+++ b/solution.py
@@ -12,11 +12,11 @@
 sharpness = 16.0
 threshold = 0.3
 
-AXES = ("zh", "zl", "x", "y", "core")
+AXES = ("z", "x", "y", "core")
 PLANE = ("x", "y")
-LINE = ("zl", "zh")
-SIZES = {"zh": 4, "zl": 2, "x": 4, "y": 4, "core": 2}
-DEPTH = SIZES["zh"] * SIZES["zl"]
+LINE = ("z",)
+SIZES = {"z": 8, "x": 4, "y": 4, "core": 2}
+DEPTH = SIZES["z"]
 PEERS = SIZES["x"] * SIZES["y"]
 
 DOCS = 192
@@ -25,10 +25,10 @@
 K = 64
 COLUMNS = DEPTH * DOCS
 ROWS = PEERS * DOCS
-ROW_BLOCK = 512
+ROW_BLOCK = 3072
 COLUMN_BLOCK = 256
 LANES = 128
-PIVOTS = 4
+PIVOTS = 8
 
 bf16 = jnp.bfloat16
 f32 = jnp.float32
@@ -72,17 +72,19 @@
     return hi, (value - hi).astype(bf16).astype(f32)
 
 
-def unit_kernel(emb_ref, start_ref, plane_ref, line_ref):
+def unit_kernel(emb_ref, start_ref, line_ref):
     wide = emb_ref[...].astype(f32)
     unit = wide * lax.rsqrt(jnp.sum(wide * wide, axis=1, keepdims=True) + 1e-06)
-    unit = unit.astype(bf16)
-    plane_ref[...] = jnp.broadcast_to((unit * (sharpness / 2))[None], plane_ref.shape)
-    line_ref[:, :, :E] = jnp.broadcast_to(unit[None], (SIZES["zh"], DOCS, E))
+    line_ref[:, :E] = unit.astype(bf16)
     start = jnp.concatenate([start_ref[...], jnp.zeros((K, 2 * LANES - DOCS), f32)], axis=1)
     start = jnp.concatenate([start, jnp.zeros_like(start)], axis=0).T[:DOCS]
     hi, mid = two_parts(start)
-    pair = jnp.where(left_lanes(hi), hi, swap_lanes(mid)).astype(bf16)
-    line_ref[:, :, E:] = jnp.broadcast_to(pair[None], (SIZES["zh"], DOCS, 2 * K))
+    line_ref[:, E:] = jnp.where(left_lanes(hi), hi, swap_lanes(mid)).astype(bf16)
+
+
+def plane_kernel(line_ref, plane_ref):
+    unit = line_ref[:, :E] * (sharpness / 2)
+    plane_ref[...] = jnp.broadcast_to(unit[None], plane_ref.shape)
 
 
 def tile_kernel(last, *refs):
@@ -90,12 +92,11 @@
         rows_ref, cols_ref, before_ref, tile_ref, sums_ref, acc = refs
         acc[...] = before_ref[...]
     else:
-        rows_ref, same_ref, other_ref, tile_ref, sums_ref, cols_ref, acc = refs
+        rows_ref, *pieces, tile_ref, sums_ref, cols_ref, acc = refs
         acc[...] = jnp.zeros_like(acc)
-        side = lax.axis_index("zl") * (COLUMNS // 2)
-        cols_ref[pl.ds(pl.multiple_of(side, COLUMNS // 2), COLUMNS // 2), :] = same_ref[...]
-        side = COLUMNS // 2 - side
-        cols_ref[pl.ds(pl.multiple_of(side, COLUMNS // 2), COLUMNS // 2), :] = other_ref[...]
+        for i, piece in enumerate(pieces):
+            first = (lax.axis_index("z") + i) % DEPTH * DOCS
+            cols_ref[pl.ds(pl.multiple_of(first, DOCS), DOCS), :] = piece[...]
 
     def block(i, _):
         at = pl.ds(pl.multiple_of(i * ROW_BLOCK, ROW_BLOCK), ROW_BLOCK)
@@ -123,7 +124,7 @@
 
 
 def multiply(tile_ref, weights_ref, out_ref, terms):
-    chunks = 8
+    chunks = 16
 
     def block(i, _):
         rows = chunks * DOCS
@@ -179,7 +180,7 @@
         total += jnp.sum(
             jnp.broadcast_to(tall[:, k : k + 1], (LANES, LANES)), axis=0, keepdims=True
         )
-    first = (lax.axis_index("zl") * SIZES["zh"] + lax.axis_index("zh")) * DOCS
+    first = lax.axis_index("z") * DOCS
     top = pl.ds(pl.multiple_of(first, HALF), HALF)
     low = pl.ds(pl.multiple_of(first + HALF, HALF), HALF)
     for whole, own in ((all_inv, inv_ref), (all_root, root_ref)):
@@ -303,18 +304,24 @@
     return lax.ppermute(value, "core", [(0, 1), (1, 0)])
 
 
+def shift(value, step):
+    return lax.ppermute(value, "z", [(i, (i + step) % DEPTH) for i in range(DEPTH)])
+
+
 def local(embeddings, start_vectors):
     all_docs = embeddings.shape[0] * lax.axis_size(AXES)
     width = E + 2 * K
-    plane, line = call(
-        unit_kernel,
-        [shape(PEERS, DOCS, E, dtype=bf16), shape(SIZES["zh"], DOCS, width, dtype=bf16)],
-        [embeddings, start_vectors.T],
-    )
-    same, plane = lax.optimization_barrier((exchange(line, ("zh",)), plane))
-    same = same.reshape(COLUMNS // 2, width)
-    other = lax.ppermute(same, "zl", [(0, 1), (1, 0)])
-    own_rows, other = lax.optimization_barrier((exchange(plane, PLANE), other))
+    (line,) = call(
+        unit_kernel, [shape(DOCS, width, dtype=bf16)], [embeddings, start_vectors.T]
+    )
+    (plane,) = call(plane_kernel, [shape(PEERS, DOCS, E, dtype=bf16)], [line])
+    pieces = [line] + [None] * (DEPTH - 1)
+    behind = ahead = line
+    for i in range(1, DEPTH // 2):
+        behind, ahead = shift(behind, 1), shift(ahead, -1)
+        pieces[-i], pieces[i] = behind, ahead
+    pieces[DEPTH // 2] = shift(ahead, -1)
+    own_rows, *pieces = lax.optimization_barrier((exchange(plane, PLANE), *pieces))
     own_rows = own_rows.reshape(ROWS, E)
     other_rows = swap_core(own_rows)
 
@@ -324,7 +331,7 @@
     own_tile, sums, columns = call(
         functools.partial(tile_kernel, False),
         [tile, shape(8, COLUMNS), shape(COLUMNS, width, dtype=bf16)],
-        [own_rows, same, other],
+        [own_rows, *pieces],
         [acc],
         flops,
     )

time: 167 us -> 151 us (0.904)
  blocking collectives: 103 us -> 84.7 us
  starting transfers between devices: 18 us -> 33.2 us
  waiting for transfers between devices: 17.6 us -> 8.41 us
  Pallas kernels: 25.7 us -> 22.3 us
    all_to_all x7 -> x6, blocking collectives: 103 us -> 84.7 us  [exchange(): return lax.all_to_all(value, axes, 0, 0, tiled=True)]
    ppermute x1 -> x7, starting transfers between devices: 1.41 us -> 15.9 us  [shift(): lax.ppermute(value, 'z', [(i, (i + step) % DEPTH) for i in range(DEPTH)])]
    all_to_all x1, waiting for transfers between devices: 8.21 us -> 0.01 us  [exchange(): return lax.all_to_all(value, axes, 0, 0, tiled=True)]
    pallas_call x13 -> x14, Pallas kernels: 25.7 us -> 22.3 us  [call(): pl.pallas_call(kernel, out_shape=tuple(outs), in_specs=[vmem] * len(args)...]
    ppermute x1 -> x7, waiting for transfers between devices: 9.41 us -> 8.4 us  [shift(): lax.ppermute(value, 'z', [(i, (i + step) % DEPTH) for i in range(DEPTH)])]
  transfers between devices with their start and end apart: 5 -> 11, of which waited for: 2 -> 5; matrix products, arithmetic and copies ran while one was open for 0% -> 0% of each run, Pallas kernels for 6% -> 6%
where the time goes in v5:
time: 151 us; the launch traced here: 150 us
  blocking collectives  84.7 us (56%)
  starting transfers between devices  33.2 us (22%)
  Pallas kernels  22.3 us (15%)
  waiting for transfers between devices  8.41 us (6%)
  local copies, waits for them, and re-layouts  1.73 us (1%)
    all_to_all x6, blocking collectives, exchange(): return lax.all_to_all(value, axes, 0, 0, tiled=True)  84.7 us
    pallas_call x14, Pallas kernels, call(): pl.pallas_call(kernel, out_shape=tuple(outs), in_specs=[vmem] * len(args)...  22.3 us
    ppermute x7, starting transfers between devices, shift(): lax.ppermute(value, 'z', [(i, (i + step) % DEPTH) for i in range(DEPTH)])  15.9 us
    ppermute x3, starting transfers between devices, swap_core(): return lax.ppermute(value, 'core', [(0, 1), (1, 0)])  9.79 us
    ppermute x7, waiting for transfers between devices, shift(): lax.ppermute(value, 'z', [(i, (i + step) % DEPTH) for i in range(DEPTH)])  8.4 us
    all_to_all x1, starting transfers between devices, exchange(): return lax.all_to_all(value, axes, 0, 0, tiled=True)  7.58 us
  transfers between devices with their start and end apart: 11, of which 5 were waited for; matrix products, arithmetic and copies ran while one was open for 0% of the time, Pallas kernels for 6%

profile of v5, /device:TPU:1, one launch (start us, length us, event | category | flops | bytes accessed | tf_op | source)
XLA Modules:
  0.0 150.5 jit_solution(2241691735036166533)
XLA Ops:
  0.0 0.9 copy-done
  0.9 0.8 copy-done.1
  1.7 0.2 shard_map.28.line_ref.refs_1_
  1.9 1.3 shard_map.29
  3.3 7.6 %all-to-all-start = ((bf16[16,192,256]{2,1,0:T(8,128)(2,1)}), bf16[16,192,256]{2,1,0:T(8,128)(2,1)S(1)}, u32[]{:S(2)}, u32[]{:S(2)}) async-start(bf16[16,192,256]{2,1,0:T(8,128)(2,1)} %shard_map.29), calls=%async_computation | async-start | bytes 3145728 | tf_op jit(solution)/shard_map/all_to_all | solution.py:300
  10.8 5.7 %collective-permute-start = (bf16[192,384]{1,0:T(8,128)(2,1)S(1)}, bf16[192,384]{1,0:T(8,128)(2,1)S(1)}, u32[]{:S(2)}, u32[]{:S(2)}) collective-permute-start(bf16[192,384]{1,0:T(8,128)(2,1)S(1)} %shard_map.28.line_ref.refs_1_), channel_id=1, source_target_pairs={{0,224},{32,0},{64,32},{96,64},{128,96},{160,128},{192,160},{224,1... | collective-permute-start | bytes 442376 | tf_op jit(solution)/shard_map/ppermute | solution.py:308
  16.5 2.1 %collective-permute-done.refs_2_ = bf16[192,384]{1,0:T(8,128)(2,1)S(1)} collective-permute-done((bf16[192,384]{1,0:T(8,128)(2,1)S(1)}, bf16[192,384]{1,0:T(8,128)(2,1)S(1)}, u32[]{:S(2)}, u32[]{:S(2)}) %collective-permute-start) | collective-permute-done | bytes 147488 | tf_op jit(solution)/shard_map/ppermute | solution.py:308
  18.6 3.5 %collective-permute-start.1 = (bf16[192,384]{1,0:T(8,128)(2,1)S(1)}, bf16[192,384]{1,0:T(8,128)(2,1)S(1)}, u32[]{:S(2)}, u32[]{:S(2)}) collective-permute-start(bf16[192,384]{1,0:T(8,128)(2,1)S(1)} %collective-permute-done.refs_2_), channel_id=1, source_target_pairs={{0,224},{32,0},{64,32},{96,64},{128,96},{160,128},{192,160},{224,1... | collective-permute-start | bytes 442376 | tf_op jit(solution)/shard_map/ppermute | solution.py:308
  22.1 2.1 %collective-permute-done.1.refs_3_ = bf16[192,384]{1,0:T(8,128)(2,1)S(1)} collective-permute-done((bf16[192,384]{1,0:T(8,128)(2,1)S(1)}, bf16[192,384]{1,0:T(8,128)(2,1)S(1)}, u32[]{:S(2)}, u32[]{:S(2)}) %collective-permute-start.1) | collective-permute-done | bytes 147488 | tf_op jit(solution)/shard_map/ppermute | solution.py:308
  24.2 3.4 %collective-permute-start.2 = (bf16[192,384]{1,0:T(8,128)(2,1)S(1)}, bf16[192,384]{1,0:T(8,128)(2,1)S(1)}, u32[]{:S(2)}, u32[]{:S(2)}) collective-permute-start(bf16[192,384]{1,0:T(8,128)(2,1)S(1)} %collective-permute-done.1.refs_3_), channel_id=1, source_target_pairs={{0,224},{32,0},{64,32},{96,64},{128,96},{160,128},{192,160},{224,1... | collective-permute-start | bytes 442376 | tf_op jit(solution)/shard_map/ppermute | solution.py:308
  27.6 2.1 %collective-permute-done.2.refs_4_ = bf16[192,384]{1,0:T(8,128)(2,1)S(1)} collective-permute-done((bf16[192,384]{1,0:T(8,128)(2,1)S(1)}, bf16[192,384]{1,0:T(8,128)(2,1)S(1)}, u32[]{:S(2)}, u32[]{:S(2)}) %collective-permute-start.2) | collective-permute-done | bytes 147488 | tf_op jit(solution)/shard_map/ppermute | solution.py:308
  29.7 3.3 %collective-permute-start.3 = (bf16[192,384]{1,0:T(8,128)(2,1)S(1)}, bf16[192,384]{1,0:T(8,128)(2,1)S(1)}, u32[]{:S(2)}, u32[]{:S(2)}) collective-permute-start(bf16[192,384]{1,0:T(8,128)(2,1)S(1)} %collective-permute-done.2.refs_4_), channel_id=1, source_target_pairs={{0,224},{32,0},{64,32},{96,64},{128,96},{160,128},{192,160},{224,1... | collective-permute-start | bytes 442376 | tf_op jit(solution)/shard_map/ppermute | solution.py:308
  33.0 0.1 collective-permute-done.6.refs_6_
  33.1 2.0 %collective-permute-done.3.refs_5_ = bf16[192,384]{1,0:T(8,128)(2,1)S(1)} collective-permute-done((bf16[192,384]{1,0:T(8,128)(2,1)S(1)}, bf16[192,384]{1,0:T(8,128)(2,1)S(1)}, u32[]{:S(2)}, u32[]{:S(2)}) %collective-permute-start.3) | collective-permute-done | bytes 147488 | tf_op jit(solution)/shard_map/ppermute | solution.py:308
  35.1 4.5 %collective-permute-start.7 = (bf16[3072,256]{1,0:T(8,128)(2,1)S(1)}, bf16[3072,256]{1,0:T(8,128)(2,1)S(1)}, u32[]{:S(2)}, u32[]{:S(2)}) collective-permute-start(bf16[3072,256]{1,0:T(8,128)(2,1)S(1)} %bitcast.3), channel_id=1, source_target_pairs={{0,1},{1,0},{2,3},{3,2},{4,5},{5,4},{6,7},{7,6},{8,9},{9,8},{10,11... | collective-permute-start | bytes 4718600 | tf_op jit(solution)/shard_map/ppermute | solution.py:304
  39.6 3.3 %shard_map.30 = (bf16[3072,1536]{1,0:T(8,128)(2,1)S(1)}, f32[8,1536]{1,0:T(8,128)S(1)}, bf16[1536,384]{1,0:T(8,128)(2,1)S(1)}) custom-call(bf16[3072,256]{1,0:T(8,128)(2,1)S(1)} %bitcast.4, bf16[192,384]{1,0:T(8,128)(2,1)S(1)} %shard_map.28.line_ref.refs_1_, bf16[192,384]{1,0:T(8,128)(2,1)S(1)} %collective-permute-done.refs_2_, ...), custom_call_target="tpu_custom_call" | custom-call | flops 2415919104 | bytes 13418496 | tf_op jit(solution)/shard_map/pallas_call | solution.py:45
  42.9 3.3 %shard_map.31 = (bf16[3072,1536]{1,0:T(8,128)(2,1)S(1)}, f32[8,16,128]{2,1,0:T(8,128)S(1)}) custom-call(bf16[3072,256]{1,0:T(8,128)(2,1)S(1)} %collective-permute-done.7.refs_0_, bf16[1536,384]{1,0:T(8,128)(2,1)S(1)} %get-tuple-element.39.refs_1_.cols_ref, f32[8,1536]{1,0:T(8,128)S(1)} %get-tuple-element.40.refs_2_), custom_call_target="tpu_custom_call" | custom-call | flops 2415919104 | bytes 12304384 | tf_op jit(solution)/shard_map/pallas_call | solution.py:45
  46.2 11.6 %all_to_all.35.sums_ref = f32[8,16,128]{2,1,0:T(8,128)S(1)} all-to-all(f32[8,16,128]{2,1,0:T(8,128)S(1)} %get-tuple-element.42), channel_id=1, replica_groups=mesh['z'=8,'x'=4,'y'=4,'core'=2] {'z'}, dimensions={0} | all-to-all | bytes 131072 | tf_op jit(solution)/shard_map/all_to_all | solution.py:300
  57.8 3.0 %shard_map.32 = (f32[16,104,128]{2,1,0:T(8,128)S(1)}, bf16[1536,128]{1,0:T(8,128)(2,1)S(1)}, f32[96,128]{1,0:T(8,128)S(1)}, f32[96,128]{1,0:T(8,128)S(1)}) custom-call(bf16[3072,1536]{1,0:T(8,128)(2,1)S(1)} %get-tuple-element.41.tile_ref, f32[8,16,128]{2,1,0:T(8,128)S(1)} %all_to_all.35.sums_ref, bf16[1536,384]{1,0:T(8,128)(2,1)S(1)} %get-tuple-element.39.refs_1_.cols_ref), custom_call_target="tpu_custom_call" | custom-call | flops 1207959552 | bytes 12025856 | tf_op jit(solution)/shard_map/pallas_call | solution.py:45
  60.8 2.0 %collective-permute-start.8 = (f32[16,104,128]{2,1,0:T(8,128)S(1)}, f32[16,104,128]{2,1,0:T(8,128)S(1)}, u32[]{:S(2)}, u32[]{:S(2)}) collective-permute-start(f32[16,104,128]{2,1,0:T(8,128)S(1)} %get-tuple-element.44.other_ref), channel_id=1, source_target_pairs={{0,1},{1,0},{2,3},{3,2},{4,5},{5,4},{6,7},{7,6},{8,9},{9,8},{10,11... | collective-permute-start | bytes 2555912 | tf_op jit(solution)/shard_map/ppermute | solution.py:304
  62.7 2.6 %shard_map.33.own_ref = f32[16,104,128]{2,1,0:T(8,128)S(1)} custom-call(bf16[3072,1536]{1,0:T(8,128)(2,1)S(1)} %get-tuple-element.38.tile_ref, bf16[1536,128]{1,0:T(8,128)(2,1)S(1)} %get-tuple-element.43.weights_ref, f32[16,104,128]{2,1,0:T(8,128)S(1)} %get-tuple-element.44.other_ref), custom_call_target="tpu_custom_call" | custom-call | flops 1207959552 | bytes 11534336 | tf_op jit(solution)/shard_map/pallas_call | solution.py:45
  65.5 16.1 %all_to_all.36.got_ref = bf16[16,112,128]{2,1,0:T(8,128)(2,1)S(1)} all-to-all(bf16[16,112,128]{2,1,0:T(8,128)(2,1)S(1)} %shard_map.34), channel_id=1, replica_groups=mesh['z'=8,'x'=4,'y'=4,'core'=2] {'x','y'}, dimensions={0} | all-to-all | bytes 917504 | tf_op jit(solution)/shard_map/all_to_all | solution.py:300
  81.6 0.2 shard_map.35
  81.8 11.5 %all_to_all.37.got_ref = bf16[8,112,128]{2,1,0:T(8,128)(2,1)S(1)} all-to-all(bf16[8,112,128]{2,1,0:T(8,128)(2,1)S(1)} %get-tuple-element.47), channel_id=1, replica_groups=mesh['z'=8,'x'=4,'y'=4,'core'=2] {'z'}, dimensions={0} | all-to-all | bytes 458752 | tf_op jit(solution)/shard_map/all_to_all | solution.py:300
  93.2 2.7 %shard_map.36 = (f32[16,104,128]{2,1,0:T(8,128)S(1)}, bf16[1536,128]{1,0:T(8,128)(2,1)S(1)}) custom-call(bf16[3072,1536]{1,0:T(8,128)(2,1)S(1)} %get-tuple-element.41.tile_ref, bf16[8,112,128]{2,1,0:T(8,128)(2,1)S(1)} %all_to_all.37.got_ref), custom_call_target="tpu_custom_call" | custom-call | flops 1207959552 | bytes 10911744 | tf_op jit(solution)/shard_map/pallas_call | solution.py:45
  96.0 3.3 %collective-permute-start.9 = (f32[16,104,128]{2,1,0:T(8,128)S(1)}, f32[16,104,128]{2,1,0:T(8,128)S(1)}, u32[]{:S(2)}, u32[]{:S(2)}) collective-permute-start(f32[16,104,128]{2,1,0:T(8,128)S(1)} %get-tuple-element.49.other_ref), channel_id=1, source_target_pairs={{0,1},{1,0},{2,3},{3,2},{4,5},{5,4},{6,7},{7,6},{8,9},{9,8},{10,11... | collective-permute-start | bytes 2555912 | tf_op jit(solution)/shard_map/ppermute | solution.py:304
  99.2 2.6 %shard_map.37.own_ref = f32[16,104,128]{2,1,0:T(8,128)S(1)} custom-call(bf16[3072,1536]{1,0:T(8,128)(2,1)S(1)} %get-tuple-element.38.tile_ref, bf16[1536,128]{1,0:T(8,128)(2,1)S(1)} %get-tuple-element.48.weights_ref, f32[16,104,128]{2,1,0:T(8,128)S(1)} %get-tuple-element.49.other_ref), custom_call_target="tpu_custom_call" | custom-call | flops 1207959552 | bytes 11534336 | tf_op jit(solution)/shard_map/pallas_call | solution.py:45
  102.0 17.8 %all_to_all.38.got_ref = f32[16,104,128]{2,1,0:T(8,128)S(1)} all-to-all(f32[16,104,128]{2,1,0:T(8,128)S(1)} %shard_map.38), channel_id=1, replica_groups=mesh['z'=8,'x'=4,'y'=4,'core'=2] {'x','y'}, dimensions={0} | all-to-all | bytes 1703936 | tf_op jit(solution)/shard_map/all_to_all | solution.py:300
  119.8 0.4 shard_map.39
  120.2 16.1 %all_to_all.39.got_ref = f32[16,32,128]{2,1,0:T(8,128)S(1)} all-to-all(f32[16,32,128]{2,1,0:T(8,128)S(1)} %get-tuple-element.51), channel_id=1, replica_groups=mesh['z'=8,'x'=4,'y'=4,'core'=2] {'z','core'}, dimensions={0} | all-to-all | bytes 524288 | tf_op jit(solution)/shard_map/all_to_all | solution.py:300
  136.3 11.7 %all_to_all.40.got_ref = f32[16,32,128]{2,1,0:T(8,128)S(1)} all-to-all(f32[16,32,128]{2,1,0:T(8,128)S(1)} %shard_map.40), channel_id=1, replica_groups=mesh['z'=8,'x'=4,'y'=4,'core'=2] {'x','y'}, dimensions={0} | all-to-all | bytes 524288 | tf_op jit(solution)/shard_map/all_to_all | solution.py:300
  148.0 2.5 %shard_map.41 = f32[64,192]{1,0:T(8,128)} custom-call(f32[16,32,128]{2,1,0:T(8,128)S(1)} %all_to_all.40.got_ref, f32[96,128]{1,0:T(8,128)S(1)} %get-tuple-element.52.vectors_ref), custom_call_target="tpu_custom_call" | custom-call | bytes 360448 | tf_op jit(solution)/shard_map/pallas_call | solution.py:45
  (14 shorter events, 0.2 us)
Async XLA Ops:
  0.0 0.9 copy-start
  0.9 0.8 copy-start.1
  3.3 31.9 %all-to-all-start = ((bf16[16,192,256]{2,1,0:T(8,128)(2,1)}), bf16[16,192,256]{2,1,0:T(8,128)(2,1)S(1)}, u32[]{:S(2)}, u32[]{:S(2)}) async-start(bf16[16,192,256]{2,1,0:T(8,128)(2,1)} %shard_map.29), calls=%async_computation | async-start | bytes 3145728 | tf_op jit(solution)/shard_map/all_to_all | solution.py:300
  10.8 7.8 %collective-permute-start = (bf16[192,384]{1,0:T(8,128)(2,1)S(1)}, bf16[192,384]{1,0:T(8,128)(2,1)S(1)}, u32[]{:S(2)}, u32[]{:S(2)}) collective-permute-start(bf16[192,384]{1,0:T(8,128)(2,1)S(1)} %shard_map.28.line_ref.refs_1_), channel_id=1, source_target_pairs={{0,224},{32,0},{64,32},{96,64},{128,96},{160,128},{192,160},{224,1... | collective-permute-start | bytes 442376 | tf_op jit(solution)/shard_map/ppermute | solution.py:308
  16.5 5.6 %collective-permute-start.4 = (bf16[192,384]{1,0:T(8,128)(2,1)S(1)}, bf16[192,384]{1,0:T(8,128)(2,1)S(1)}, u32[]{:S(2)}, u32[]{:S(2)}) collective-permute-start(bf16[192,384]{1,0:T(8,128)(2,1)S(1)} %shard_map.28.line_ref.refs_1_), channel_id=1, source_target_pairs={{0,32},{32,64},{64,96},{96,128},{128,160},{160,192},{192,224},{224... | collective-permute-start | bytes 442376 | tf_op jit(solution)/shard_map/ppermute | solution.py:308
  18.6 5.6 %collective-permute-start.1 = (bf16[192,384]{1,0:T(8,128)(2,1)S(1)}, bf16[192,384]{1,0:T(8,128)(2,1)S(1)}, u32[]{:S(2)}, u32[]{:S(2)}) collective-permute-start(bf16[192,384]{1,0:T(8,128)(2,1)S(1)} %collective-permute-done.refs_2_), channel_id=1, source_target_pairs={{0,224},{32,0},{64,32},{96,64},{128,96},{160,128},{192,160},{224,1... | collective-permute-start | bytes 442376 | tf_op jit(solution)/shard_map/ppermute | solution.py:308
  22.1 5.5 %collective-permute-start.5 = (bf16[192,384]{1,0:T(8,128)(2,1)S(1)}, bf16[192,384]{1,0:T(8,128)(2,1)S(1)}, u32[]{:S(2)}, u32[]{:S(2)}) collective-permute-start(bf16[192,384]{1,0:T(8,128)(2,1)S(1)} %collective-permute-done.4.refs_8_), channel_id=1, source_target_pairs={{0,32},{32,64},{64,96},{96,128},{128,160},{160,192},{192,224},{224... | collective-permute-start | bytes 442376 | tf_op jit(solution)/shard_map/ppermute | solution.py:308
  24.2 5.5 %collective-permute-start.2 = (bf16[192,384]{1,0:T(8,128)(2,1)S(1)}, bf16[192,384]{1,0:T(8,128)(2,1)S(1)}, u32[]{:S(2)}, u32[]{:S(2)}) collective-permute-start(bf16[192,384]{1,0:T(8,128)(2,1)S(1)} %collective-permute-done.1.refs_3_), channel_id=1, source_target_pairs={{0,224},{32,0},{64,32},{96,64},{128,96},{160,128},{192,160},{224,1... | collective-permute-start | bytes 442376 | tf_op jit(solution)/shard_map/ppermute | solution.py:308
  27.6 5.5 %collective-permute-start.6 = (bf16[192,384]{1,0:T(8,128)(2,1)S(1)}, bf16[192,384]{1,0:T(8,128)(2,1)S(1)}, u32[]{:S(2)}, u32[]{:S(2)}) collective-permute-start(bf16[192,384]{1,0:T(8,128)(2,1)S(1)} %collective-permute-done.5.refs_7_), channel_id=1, source_target_pairs={{0,32},{32,64},{64,96},{96,128},{128,160},{160,192},{192,224},{224... | collective-permute-start | bytes 442376 | tf_op jit(solution)/shard_map/ppermute | solution.py:308
  29.7 5.4 %collective-permute-start.3 = (bf16[192,384]{1,0:T(8,128)(2,1)S(1)}, bf16[192,384]{1,0:T(8,128)(2,1)S(1)}, u32[]{:S(2)}, u32[]{:S(2)}) collective-permute-start(bf16[192,384]{1,0:T(8,128)(2,1)S(1)} %collective-permute-done.2.refs_4_), channel_id=1, source_target_pairs={{0,224},{32,0},{64,32},{96,64},{128,96},{160,128},{192,160},{224,1... | collective-permute-start | bytes 442376 | tf_op jit(solution)/shard_map/ppermute | solution.py:308
  35.1 7.8 %collective-permute-start.7 = (bf16[3072,256]{1,0:T(8,128)(2,1)S(1)}, bf16[3072,256]{1,0:T(8,128)(2,1)S(1)}, u32[]{:S(2)}, u32[]{:S(2)}) collective-permute-start(bf16[3072,256]{1,0:T(8,128)(2,1)S(1)} %bitcast.3), channel_id=1, source_target_pairs={{0,1},{1,0},{2,3},{3,2},{4,5},{5,4},{6,7},{7,6},{8,9},{9,8},{10,11... | collective-permute-start | bytes 4718600 | tf_op jit(solution)/shard_map/ppermute | solution.py:304
  60.8 4.6 %collective-permute-start.8 = (f32[16,104,128]{2,1,0:T(8,128)S(1)}, f32[16,104,128]{2,1,0:T(8,128)S(1)}, u32[]{:S(2)}, u32[]{:S(2)}) collective-permute-start(f32[16,104,128]{2,1,0:T(8,128)S(1)} %get-tuple-element.44.other_ref), channel_id=1, source_target_pairs={{0,1},{1,0},{2,3},{3,2},{4,5},{5,4},{6,7},{7,6},{8,9},{9,8},{10,11... | collective-permute-start | bytes 2555912 | tf_op jit(solution)/shard_map/ppermute | solution.py:304
  96.0 5.9 %collective-permute-start.9 = (f32[16,104,128]{2,1,0:T(8,128)S(1)}, f32[16,104,128]{2,1,0:T(8,128)S(1)}, u32[]{:S(2)}, u32[]{:S(2)}) collective-permute-start(f32[16,104,128]{2,1,0:T(8,128)S(1)} %get-tuple-element.49.other_ref), channel_id=1, source_target_pairs={{0,1},{1,0},{2,3},{3,2},{4,5},{5,4},{6,7},{7,6},{8,9},{9,8},{10,11... | collective-permute-start | bytes 2555912 | tf_op jit(solution)/shard_map/ppermute | solution.py:304

commit v6 on v5

--- a/solution.py
+++ b/solution.py
@@ -29,6 +29,8 @@
 COLUMN_BLOCK = 256
 LANES = 128
 PIVOTS = 8
+PACKED = 24
+MERGE_COST = 10_350_000_000
 
 bf16 = jnp.bfloat16
 f32 = jnp.float32
@@ -39,13 +41,13 @@
     return jax.ShapeDtypeStruct(dims, dtype)
 
 
-def call(kernel, outs, args, scratch=(), flops=0):
+def call(kernel, outs, args, scratch=(), flops=0, space=pltpu.VMEM):
     vmem = pl.BlockSpec(memory_space=pltpu.VMEM)
     moved = sum(math.prod(a.shape) * a.dtype.itemsize for a in (*args, *outs))
     return pl.pallas_call(
         kernel,
         out_shape=tuple(outs),
-        in_specs=[vmem] * len(args),
+        in_specs=[pl.BlockSpec(memory_space=space)] * len(args),
         out_specs=tuple(vmem for _ in outs),
         scratch_shapes=list(scratch),
         cost_estimate=pl.CostEstimate(flops=flops, bytes_accessed=moved, transcendentals=0),
@@ -72,7 +74,15 @@
     return hi, (value - hi).astype(bf16).astype(f32)
 
 
-def unit_kernel(emb_ref, start_ref, line_ref):
+def unit_kernel(emb_hbm, start_hbm, line_ref, emb_ref, start_ref, done):
+    copies = [
+        pltpu.make_async_copy(emb_hbm, emb_ref, done.at[0]),
+        pltpu.make_async_copy(start_hbm, start_ref, done.at[1]),
+    ]
+    for copy in copies:
+        copy.start()
+    for copy in copies:
+        copy.wait()
     wide = emb_ref[...].astype(f32)
     unit = wide * lax.rsqrt(jnp.sum(wide * wide, axis=1, keepdims=True) + 1e-06)
     line_ref[:, :E] = unit.astype(bf16)
@@ -87,16 +97,20 @@
     plane_ref[...] = jnp.broadcast_to(unit[None], plane_ref.shape)
 
 
+def merge_kernel(*refs):
+    *pieces, cols_ref = refs
+    for i, piece in enumerate(pieces):
+        first = (lax.axis_index("z") + i) % DEPTH * DOCS
+        cols_ref[pl.ds(pl.multiple_of(first, DOCS), DOCS), :] = piece[...]
+
+
 def tile_kernel(last, *refs):
     if last:
         rows_ref, cols_ref, before_ref, tile_ref, sums_ref, acc = refs
         acc[...] = before_ref[...]
     else:
-        rows_ref, *pieces, tile_ref, sums_ref, cols_ref, acc = refs
+        rows_ref, cols_ref, tile_ref, sums_ref, acc = refs
         acc[...] = jnp.zeros_like(acc)
-        for i, piece in enumerate(pieces):
-            first = (lax.axis_index("z") + i) % DEPTH * DOCS
-            cols_ref[pl.ds(pl.multiple_of(first, DOCS), DOCS), :] = piece[...]
 
     def block(i, _):
         at = pl.ds(pl.multiple_of(i * ROW_BLOCK, ROW_BLOCK), ROW_BLOCK)
@@ -239,9 +253,17 @@
     tall = jnp.concatenate([vectors, jnp.zeros((LANES - HALF, LANES), f32)], axis=0)
     product = jnp.dot(tall.T, tall, precision=HIGHEST, preferred_element_type=f32)
     gram = product[:K] + swap_lanes(product[K:])
-    low = swap_lanes(gram[K // 2 :])
-    gram = jnp.where(left_lanes(low), gram[: K // 2], low)
-    out_ref[...] = jnp.broadcast_to(gram[None], out_ref.shape)
+    quarter = K // 2
+    lane = lax.broadcasted_iota(jnp.int32, (quarter, LANES), 1)
+    low = gram[quarter:]
+    packed = jnp.where(lane < quarter, gram[:quarter], jnp.where(lane < K, low, swap_lanes(low)))
+    tail = packed[PACKED:]
+    folded = jnp.concatenate(
+        [pltpu.roll(tail, LANES - quarter * (i + 1), 1) for i in range(3)], axis=0
+    )
+    out_ref[...] = jnp.broadcast_to(
+        jnp.where(lane[:PACKED] < 3 * quarter, packed[:PACKED], folded)[None], out_ref.shape
+    )
 
 
 def fold_kernel(got_ref, out_ref):
@@ -250,7 +272,18 @@
 
 def solve_kernel(scale, got_ref, vectors_ref, out_ref):
     packed = jnp.sum(got_ref[...], axis=0)
-    work = jnp.concatenate([packed, swap_lanes(packed)], axis=0)
+    quarter = K // 2
+    piece = lax.broadcasted_iota(jnp.int32, (8, LANES), 1) // quarter
+    tail = jnp.zeros((8, LANES), f32)
+    for i in range(3):
+        tail = jnp.where(piece == i, pltpu.roll(packed[8 * i : 8 * i + 8], quarter * (i + 1), 1), tail)
+    packed = jnp.concatenate([packed, tail], axis=0)
+    lane = lax.broadcasted_iota(jnp.int32, packed.shape, 1)
+    low = jnp.where(lane < quarter, swap_lanes(packed), packed)
+    whole = jnp.concatenate([packed, low, jnp.zeros((LANES - K, LANES), f32)], axis=0)
+    turned = whole.T
+    upper = jnp.where(lane < quarter, packed, turned[:quarter])
+    work = jnp.concatenate([upper, low], axis=0)
     row = lax.broadcasted_iota(jnp.int32, (K, LANES), 0)
     lane = lax.broadcasted_iota(jnp.int32, (K, LANES), 1)
     work = jnp.where(lane < K, work, jnp.where(lane - K == row, 1.0, 0.0))
@@ -312,7 +345,18 @@
     all_docs = embeddings.shape[0] * lax.axis_size(AXES)
     width = E + 2 * K
     (line,) = call(
-        unit_kernel, [shape(DOCS, width, dtype=bf16)], [embeddings, start_vectors.T]
+        unit_kernel,
+        [shape(DOCS, width, dtype=bf16)],
+        [
+            pltpu.with_memory_space_constraint(value, pltpu.HBM)
+            for value in (embeddings, start_vectors.T)
+        ],
+        [
+            pltpu.VMEM((DOCS, E), bf16),
+            pltpu.VMEM((K, DOCS), f32),
+            pltpu.SemaphoreType.DMA((2,)),
+        ],
+        space=pltpu.HBM,
     )
     (plane,) = call(plane_kernel, [shape(PEERS, DOCS, E, dtype=bf16)], [line])
     pieces = [line] + [None] * (DEPTH - 1)
@@ -321,17 +365,20 @@
         behind, ahead = shift(behind, 1), shift(ahead, -1)
         pieces[-i], pieces[i] = behind, ahead
     pieces[DEPTH // 2] = shift(ahead, -1)
-    own_rows, *pieces = lax.optimization_barrier((exchange(plane, PLANE), *pieces))
+    (columns,) = call(
+        merge_kernel, [shape(COLUMNS, width, dtype=bf16)], pieces, (), MERGE_COST
+    )
+    own_rows, columns = lax.optimization_barrier((exchange(plane, PLANE), columns))
     own_rows = own_rows.reshape(ROWS, E)
     other_rows = swap_core(own_rows)
 
     tile = shape(ROWS, COLUMNS, dtype=bf16)
     acc = pltpu.VMEM((8, COLUMNS), f32)
     flops = 2 * ROWS * COLUMNS * E
-    own_tile, sums, columns = call(
+    own_tile, sums = call(
         functools.partial(tile_kernel, False),
-        [tile, shape(8, COLUMNS), shape(COLUMNS, width, dtype=bf16)],
-        [own_rows, *pieces],
+        [tile, shape(8, COLUMNS)],
+        [own_rows, columns],
         [acc],
         flops,
     )
@@ -371,7 +418,7 @@
     (mine,) = call(again_kernel, [sent], [own_tile, packed, mine], (), flops)
     (total,) = call(add_kernel, [sent], [mine, theirs])
     got = exchange(total, PLANE)
-    gram = shape(PEERS, K // 2, LANES)
+    gram = shape(PEERS, PACKED, LANES)
     vectors, total = call(gram_kernel, [own, gram], [got, inv, root, terms])
     (total,) = call(fold_kernel, [gram], [exchange(total, (*LINE, "core"))])
     got = exchange(total, PLANE)

time: 151 us -> 145 us (0.960)
  blocking collectives: 84.7 us -> 78.2 us
  waiting for transfers between devices: 8.41 us -> 11.7 us
  starting transfers between devices: 33.2 us -> 31.4 us
  local copies, waits for them, and re-layouts: 1.73 us -> 0 us
    all_to_all x6, blocking collectives: 84.7 us -> 78.2 us  [exchange(): return lax.all_to_all(value, axes, 0, 0, tiled=True)]
    all_to_all x1, waiting for transfers between devices: 0.01 us -> 4.12 us  [exchange(): return lax.all_to_all(value, axes, 0, 0, tiled=True)]
    unnamed x4 -> x0, local copies, waits for them, and re-layouts: 1.73 us -> none
    pallas_call x14 -> x15, Pallas kernels: 22.3 us -> 23.4 us  [call(): pl.pallas_call(kernel, out_shape=tuple(outs), in_specs=[pl.BlockSpec(memo...]
  transfers between devices with their start and end apart: 11 -> 11, of which waited for: 5 -> 4; matrix products, arithmetic and copies ran while one was open for 0% -> 0% of each run, Pallas kernels for 6% -> 7%
where the time goes in v6:
time: 145 us
  blocking collectives  78.2 us (54%)
  starting transfers between devices  31.4 us (22%)
  Pallas kernels  23.4 us (16%)
  waiting for transfers between devices  11.7 us (8%)
    all_to_all x6, blocking collectives, exchange(): return lax.all_to_all(value, axes, 0, 0, tiled=True)  78.2 us
    pallas_call x15, Pallas kernels, call(): pl.pallas_call(kernel, out_shape=tuple(outs), in_specs=[pl.BlockSpec(memo...  23.4 us
    ppermute x7, starting transfers between devices, shift(): lax.ppermute(value, 'z', [(i, (i + step) % DEPTH) for i in range(DEPTH)])  15.2 us
    ppermute x3, starting transfers between devices, swap_core(): return lax.ppermute(value, 'core', [(0, 1), (1, 0)])  9.52 us
    ppermute x7, waiting for transfers between devices, shift(): lax.ppermute(value, 'z', [(i, (i + step) % DEPTH) for i in range(DEPTH)])  7.58 us
    all_to_all x1, starting transfers between devices, exchange(): return lax.all_to_all(value, axes, 0, 0, tiled=True)  6.75 us
    all_to_all x1, waiting for transfers between devices, exchange(): return lax.all_to_all(value, axes, 0, 0, tiled=True)  4.12 us
  transfers between devices with their start and end apart: 11, of which 4 were waited for; matrix products, arithmetic and copies ran while one was open for 0% of the time, Pallas kernels for 7%

profile of v6, /device:TPU:1, one launch (start us, length us, event | category | flops | bytes accessed | tf_op | source)
XLA Modules:
  0.0 144.9 jit_solution(10547142626878802724)
XLA Ops:
  0.0 1.1 shard_map.28.line_ref.refs_0_
  1.1 6.5 %collective-permute-start = (bf16[192,384]{1,0:T(8,128)(2,1)S(1)}, bf16[192,384]{1,0:T(8,128)(2,1)S(1)}, u32[]{:S(2)}, u32[]{:S(2)}) collective-permute-start(bf16[192,384]{1,0:T(8,128)(2,1)S(1)} %shard_map.28.line_ref.refs_0_), channel_id=1, source_target_pairs={{0,224},{32,0},{64,32},{96,64},{128,96},{160,128},{192,160},{224,1... | collective-permute-start | bytes 442376 | tf_op jit(solution)/shard_map/ppermute | solution.py:341
  7.6 1.3 shard_map.29
  8.9 6.8 %all-to-all-start = ((bf16[16,192,256]{2,1,0:T(8,128)(2,1)}), bf16[16,192,256]{2,1,0:T(8,128)(2,1)S(1)}, u32[]{:S(2)}, u32[]{:S(2)}) async-start(bf16[16,192,256]{2,1,0:T(8,128)(2,1)} %shard_map.29), calls=%async_computation | async-start | bytes 3145728 | tf_op jit(solution)/shard_map/all_to_all | solution.py:333
  15.7 0.1 collective-permute-start.4
  15.8 2.7 %collective-permute-start.1 = (bf16[192,384]{1,0:T(8,128)(2,1)S(1)}, bf16[192,384]{1,0:T(8,128)(2,1)S(1)}, u32[]{:S(2)}, u32[]{:S(2)}) collective-permute-start(bf16[192,384]{1,0:T(8,128)(2,1)S(1)} %collective-permute-done.refs_1_), channel_id=1, source_target_pairs={{0,224},{32,0},{64,32},{96,64},{128,96},{160,128},{192,160},{224,1... | collective-permute-start | bytes 442376 | tf_op jit(solution)/shard_map/ppermute | solution.py:341
  18.4 2.5 %collective-permute-done.4.refs_7_ = bf16[192,384]{1,0:T(8,128)(2,1)S(1)} collective-permute-done((bf16[192,384]{1,0:T(8,128)(2,1)S(1)}, bf16[192,384]{1,0:T(8,128)(2,1)S(1)}, u32[]{:S(2)}, u32[]{:S(2)}) %collective-permute-start.4) | collective-permute-done | bytes 147488 | tf_op jit(solution)/shard_map/ppermute | solution.py:341
  21.0 3.0 %collective-permute-start.2 = (bf16[192,384]{1,0:T(8,128)(2,1)S(1)}, bf16[192,384]{1,0:T(8,128)(2,1)S(1)}, u32[]{:S(2)}, u32[]{:S(2)}) collective-permute-start(bf16[192,384]{1,0:T(8,128)(2,1)S(1)} %collective-permute-done.1.refs_2_), channel_id=1, source_target_pairs={{0,224},{32,0},{64,32},{96,64},{128,96},{160,128},{192,160},{224,1... | collective-permute-start | bytes 442376 | tf_op jit(solution)/shard_map/ppermute | solution.py:341
  23.9 2.5 %collective-permute-done.5.refs_6_ = bf16[192,384]{1,0:T(8,128)(2,1)S(1)} collective-permute-done((bf16[192,384]{1,0:T(8,128)(2,1)S(1)}, bf16[192,384]{1,0:T(8,128)(2,1)S(1)}, u32[]{:S(2)}, u32[]{:S(2)}) %collective-permute-start.5) | collective-permute-done | bytes 147488 | tf_op jit(solution)/shard_map/ppermute | solution.py:341
  26.5 3.0 %collective-permute-start.3 = (bf16[192,384]{1,0:T(8,128)(2,1)S(1)}, bf16[192,384]{1,0:T(8,128)(2,1)S(1)}, u32[]{:S(2)}, u32[]{:S(2)}) collective-permute-start(bf16[192,384]{1,0:T(8,128)(2,1)S(1)} %collective-permute-done.2.refs_3_), channel_id=1, source_target_pairs={{0,224},{32,0},{64,32},{96,64},{128,96},{160,128},{192,160},{224,1... | collective-permute-start | bytes 442376 | tf_op jit(solution)/shard_map/ppermute | solution.py:341
  29.4 2.5 %collective-permute-done.6.refs_5_ = bf16[192,384]{1,0:T(8,128)(2,1)S(1)} collective-permute-done((bf16[192,384]{1,0:T(8,128)(2,1)S(1)}, bf16[192,384]{1,0:T(8,128)(2,1)S(1)}, u32[]{:S(2)}, u32[]{:S(2)}) %collective-permute-start.6) | collective-permute-done | bytes 147488 | tf_op jit(solution)/shard_map/ppermute | solution.py:341
  32.0 0.1 shard_map.30.refs_1_.cols_ref
  32.1 4.1 %all-to-all-done = bf16[16,192,256]{2,1,0:T(8,128)(2,1)S(1)} async-done(((bf16[16,192,256]{2,1,0:T(8,128)(2,1)}), bf16[16,192,256]{2,1,0:T(8,128)(2,1)S(1)}, u32[]{:S(2)}, u32[]{:S(2)}) %all-to-all-start) | async-done | bytes 1572896 | tf_op jit(solution)/shard_map/all_to_all | solution.py:333
  36.2 4.2 %collective-permute-start.7 = (bf16[3072,256]{1,0:T(8,128)(2,1)S(1)}, bf16[3072,256]{1,0:T(8,128)(2,1)S(1)}, u32[]{:S(2)}, u32[]{:S(2)}) collective-permute-start(bf16[3072,256]{1,0:T(8,128)(2,1)S(1)} %bitcast.3), channel_id=1, source_target_pairs={{0,1},{1,0},{2,3},{3,2},{4,5},{5,4},{6,7},{7,6},{8,9},{9,8},{10,11... | collective-permute-start | bytes 4718600 | tf_op jit(solution)/shard_map/ppermute | solution.py:337
  40.4 3.1 %shard_map.31 = (bf16[3072,1536]{1,0:T(8,128)(2,1)S(1)}, f32[8,1536]{1,0:T(8,128)S(1)}) custom-call(bf16[3072,256]{1,0:T(8,128)(2,1)S(1)} %bitcast.4, bf16[1536,384]{1,0:T(8,128)(2,1)S(1)} %shard_map.30.refs_1_.cols_ref), custom_call_target="tpu_custom_call" | custom-call | flops 2415919104 | bytes 12238848 | tf_op jit(solution)/shard_map/pallas_call | solution.py:47
  43.6 3.2 %shard_map.32 = (bf16[3072,1536]{1,0:T(8,128)(2,1)S(1)}, f32[8,16,128]{2,1,0:T(8,128)S(1)}) custom-call(bf16[3072,256]{1,0:T(8,128)(2,1)S(1)} %collective-permute-done.7.refs_0_, bf16[1536,384]{1,0:T(8,128)(2,1)S(1)} %shard_map.30.refs_1_.cols_ref, f32[8,1536]{1,0:T(8,128)S(1)} %get-tuple-element.24.refs_2_), custom_call_target="tpu_custom_call" | custom-call | flops 2415919104 | bytes 12304384 | tf_op jit(solution)/shard_map/pallas_call | solution.py:47
  46.8 9.9 %all_to_all.35.sums_ref = f32[8,16,128]{2,1,0:T(8,128)S(1)} all-to-all(f32[8,16,128]{2,1,0:T(8,128)S(1)} %get-tuple-element.26), channel_id=1, replica_groups=mesh['z'=8,'x'=4,'y'=4,'core'=2] {'z'}, dimensions={0} | all-to-all | bytes 131072 | tf_op jit(solution)/shard_map/all_to_all | solution.py:333
  56.7 3.0 %shard_map.33 = (f32[16,104,128]{2,1,0:T(8,128)S(1)}, bf16[1536,128]{1,0:T(8,128)(2,1)S(1)}, f32[96,128]{1,0:T(8,128)S(1)}, f32[96,128]{1,0:T(8,128)S(1)}) custom-call(bf16[3072,1536]{1,0:T(8,128)(2,1)S(1)} %get-tuple-element.25.tile_ref, f32[8,16,128]{2,1,0:T(8,128)S(1)} %all_to_all.35.sums_ref, bf16[1536,384]{1,0:T(8,128)(2,1)S(1)} %shard_map.30.refs_1_.cols_ref), custom_call_target="tpu_custom_call" | custom-call | flops 1207959552 | bytes 12025856 | tf_op jit(solution)/shard_map/pallas_call | solution.py:47
  59.7 2.0 %collective-permute-start.8 = (f32[16,104,128]{2,1,0:T(8,128)S(1)}, f32[16,104,128]{2,1,0:T(8,128)S(1)}, u32[]{:S(2)}, u32[]{:S(2)}) collective-permute-start(f32[16,104,128]{2,1,0:T(8,128)S(1)} %get-tuple-element.28.other_ref), channel_id=1, source_target_pairs={{0,1},{1,0},{2,3},{3,2},{4,5},{5,4},{6,7},{7,6},{8,9},{9,8},{10,11... | collective-permute-start | bytes 2555912 | tf_op jit(solution)/shard_map/ppermute | solution.py:337
  61.8 2.6 %shard_map.34.own_ref = f32[16,104,128]{2,1,0:T(8,128)S(1)} custom-call(bf16[3072,1536]{1,0:T(8,128)(2,1)S(1)} %get-tuple-element.23.tile_ref, bf16[1536,128]{1,0:T(8,128)(2,1)S(1)} %get-tuple-element.27.weights_ref, f32[16,104,128]{2,1,0:T(8,128)S(1)} %get-tuple-element.28.other_ref), custom_call_target="tpu_custom_call" | custom-call | flops 1207959552 | bytes 11534336 | tf_op jit(solution)/shard_map/pallas_call | solution.py:47
  64.5 13.6 %all_to_all.36.got_ref = bf16[16,112,128]{2,1,0:T(8,128)(2,1)S(1)} all-to-all(bf16[16,112,128]{2,1,0:T(8,128)(2,1)S(1)} %shard_map.35), channel_id=1, replica_groups=mesh['z'=8,'x'=4,'y'=4,'core'=2] {'x','y'}, dimensions={0} | all-to-all | bytes 917504 | tf_op jit(solution)/shard_map/all_to_all | solution.py:333
  78.1 0.2 shard_map.36
  78.3 11.5 %all_to_all.37.got_ref = bf16[8,112,128]{2,1,0:T(8,128)(2,1)S(1)} all-to-all(bf16[8,112,128]{2,1,0:T(8,128)(2,1)S(1)} %get-tuple-element.31), channel_id=1, replica_groups=mesh['z'=8,'x'=4,'y'=4,'core'=2] {'z'}, dimensions={0} | all-to-all | bytes 458752 | tf_op jit(solution)/shard_map/all_to_all | solution.py:333
  89.8 2.7 %shard_map.37 = (f32[16,104,128]{2,1,0:T(8,128)S(1)}, bf16[1536,128]{1,0:T(8,128)(2,1)S(1)}) custom-call(bf16[3072,1536]{1,0:T(8,128)(2,1)S(1)} %get-tuple-element.25.tile_ref, bf16[8,112,128]{2,1,0:T(8,128)(2,1)S(1)} %all_to_all.37.got_ref), custom_call_target="tpu_custom_call" | custom-call | flops 1207959552 | bytes 10911744 | tf_op jit(solution)/shard_map/pallas_call | solution.py:47
  92.5 3.3 %collective-permute-start.9 = (f32[16,104,128]{2,1,0:T(8,128)S(1)}, f32[16,104,128]{2,1,0:T(8,128)S(1)}, u32[]{:S(2)}, u32[]{:S(2)}) collective-permute-start(f32[16,104,128]{2,1,0:T(8,128)S(1)} %get-tuple-element.33.other_ref), channel_id=1, source_target_pairs={{0,1},{1,0},{2,3},{3,2},{4,5},{5,4},{6,7},{7,6},{8,9},{9,8},{10,11... | collective-permute-start | bytes 2555912 | tf_op jit(solution)/shard_map/ppermute | solution.py:337
  95.8 2.6 %shard_map.38.own_ref = f32[16,104,128]{2,1,0:T(8,128)S(1)} custom-call(bf16[3072,1536]{1,0:T(8,128)(2,1)S(1)} %get-tuple-element.23.tile_ref, bf16[1536,128]{1,0:T(8,128)(2,1)S(1)} %get-tuple-element.32.weights_ref, f32[16,104,128]{2,1,0:T(8,128)S(1)} %get-tuple-element.33.other_ref), custom_call_target="tpu_custom_call" | custom-call | flops 1207959552 | bytes 11534336 | tf_op jit(solution)/shard_map/pallas_call | solution.py:47
  98.4 0.1 shard_map.39
  98.5 17.8 %all_to_all.38.got_ref = f32[16,104,128]{2,1,0:T(8,128)S(1)} all-to-all(f32[16,104,128]{2,1,0:T(8,128)S(1)} %shard_map.39), channel_id=1, replica_groups=mesh['z'=8,'x'=4,'y'=4,'core'=2] {'x','y'}, dimensions={0} | all-to-all | bytes 1703936 | tf_op jit(solution)/shard_map/all_to_all | solution.py:333
  116.3 0.5 shard_map.40
  116.8 14.6 %all_to_all.39.got_ref = f32[16,24,128]{2,1,0:T(8,128)S(1)} all-to-all(f32[16,24,128]{2,1,0:T(8,128)S(1)} %get-tuple-element.35), channel_id=1, replica_groups=mesh['z'=8,'x'=4,'y'=4,'core'=2] {'z','core'}, dimensions={0} | all-to-all | bytes 393216 | tf_op jit(solution)/shard_map/all_to_all | solution.py:333
  131.4 10.8 %all_to_all.40.got_ref = f32[16,24,128]{2,1,0:T(8,128)S(1)} all-to-all(f32[16,24,128]{2,1,0:T(8,128)S(1)} %shard_map.41), channel_id=1, replica_groups=mesh['z'=8,'x'=4,'y'=4,'core'=2] {'x','y'}, dimensions={0} | all-to-all | bytes 393216 | tf_op jit(solution)/shard_map/all_to_all | solution.py:333
  142.2 2.7 %shard_map.42 = f32[64,192]{1,0:T(8,128)} custom-call(f32[16,24,128]{2,1,0:T(8,128)S(1)} %all_to_all.40.got_ref, f32[96,128]{1,0:T(8,128)S(1)} %get-tuple-element.36.vectors_ref), custom_call_target="tpu_custom_call" | custom-call | bytes 294912 | tf_op jit(solution)/shard_map/pallas_call | solution.py:47
  (11 shorter events, 0.1 us)
Async XLA Ops:
  1.1 14.7 %collective-permute-start = (bf16[192,384]{1,0:T(8,128)(2,1)S(1)}, bf16[192,384]{1,0:T(8,128)(2,1)S(1)}, u32[]{:S(2)}, u32[]{:S(2)}) collective-permute-start(bf16[192,384]{1,0:T(8,128)(2,1)S(1)} %shard_map.28.line_ref.refs_0_), channel_id=1, source_target_pairs={{0,224},{32,0},{64,32},{96,64},{128,96},{160,128},{192,160},{224,1... | collective-permute-start | bytes 442376 | tf_op jit(solution)/shard_map/ppermute | solution.py:341
  8.9 27.3 %all-to-all-start = ((bf16[16,192,256]{2,1,0:T(8,128)(2,1)}), bf16[16,192,256]{2,1,0:T(8,128)(2,1)S(1)}, u32[]{:S(2)}, u32[]{:S(2)}) async-start(bf16[16,192,256]{2,1,0:T(8,128)(2,1)} %shard_map.29), calls=%async_computation | async-start | bytes 3145728 | tf_op jit(solution)/shard_map/all_to_all | solution.py:333
  15.7 5.3 %collective-permute-start.4 = (bf16[192,384]{1,0:T(8,128)(2,1)S(1)}, bf16[192,384]{1,0:T(8,128)(2,1)S(1)}, u32[]{:S(2)}, u32[]{:S(2)}) collective-permute-start(bf16[192,384]{1,0:T(8,128)(2,1)S(1)} %shard_map.28.line_ref.refs_0_), channel_id=1, source_target_pairs={{0,32},{32,64},{64,96},{96,128},{128,160},{160,192},{192,224},{224... | collective-permute-start | bytes 442376 | tf_op jit(solution)/shard_map/ppermute | solution.py:341
  15.8 5.2 %collective-permute-start.1 = (bf16[192,384]{1,0:T(8,128)(2,1)S(1)}, bf16[192,384]{1,0:T(8,128)(2,1)S(1)}, u32[]{:S(2)}, u32[]{:S(2)}) collective-permute-start(bf16[192,384]{1,0:T(8,128)(2,1)S(1)} %collective-permute-done.refs_1_), channel_id=1, source_target_pairs={{0,224},{32,0},{64,32},{96,64},{128,96},{160,128},{192,160},{224,1... | collective-permute-start | bytes 442376 | tf_op jit(solution)/shard_map/ppermute | solution.py:341
  21.0 5.5 %collective-permute-start.5 = (bf16[192,384]{1,0:T(8,128)(2,1)S(1)}, bf16[192,384]{1,0:T(8,128)(2,1)S(1)}, u32[]{:S(2)}, u32[]{:S(2)}) collective-permute-start(bf16[192,384]{1,0:T(8,128)(2,1)S(1)} %collective-permute-done.4.refs_7_), channel_id=1, source_target_pairs={{0,32},{32,64},{64,96},{96,128},{128,160},{160,192},{192,224},{224... | collective-permute-start | bytes 442376 | tf_op jit(solution)/shard_map/ppermute | solution.py:341
  21.0 5.5 %collective-permute-start.2 = (bf16[192,384]{1,0:T(8,128)(2,1)S(1)}, bf16[192,384]{1,0:T(8,128)(2,1)S(1)}, u32[]{:S(2)}, u32[]{:S(2)}) collective-permute-start(bf16[192,384]{1,0:T(8,128)(2,1)S(1)} %collective-permute-done.1.refs_2_), channel_id=1, source_target_pairs={{0,224},{32,0},{64,32},{96,64},{128,96},{160,128},{192,160},{224,1... | collective-permute-start | bytes 442376 | tf_op jit(solution)/shard_map/ppermute | solution.py:341
  26.5 5.5 %collective-permute-start.6 = (bf16[192,384]{1,0:T(8,128)(2,1)S(1)}, bf16[192,384]{1,0:T(8,128)(2,1)S(1)}, u32[]{:S(2)}, u32[]{:S(2)}) collective-permute-start(bf16[192,384]{1,0:T(8,128)(2,1)S(1)} %collective-permute-done.5.refs_6_), channel_id=1, source_target_pairs={{0,32},{32,64},{64,96},{96,128},{128,160},{160,192},{192,224},{224... | collective-permute-start | bytes 442376 | tf_op jit(solution)/shard_map/ppermute | solution.py:341
  26.5 5.5 %collective-permute-start.3 = (bf16[192,384]{1,0:T(8,128)(2,1)S(1)}, bf16[192,384]{1,0:T(8,128)(2,1)S(1)}, u32[]{:S(2)}, u32[]{:S(2)}) collective-permute-start(bf16[192,384]{1,0:T(8,128)(2,1)S(1)} %collective-permute-done.2.refs_3_), channel_id=1, source_target_pairs={{0,224},{32,0},{64,32},{96,64},{128,96},{160,128},{192,160},{224,1... | collective-permute-start | bytes 442376 | tf_op jit(solution)/shard_map/ppermute | solution.py:341
  36.2 7.4 %collective-permute-start.7 = (bf16[3072,256]{1,0:T(8,128)(2,1)S(1)}, bf16[3072,256]{1,0:T(8,128)(2,1)S(1)}, u32[]{:S(2)}, u32[]{:S(2)}) collective-permute-start(bf16[3072,256]{1,0:T(8,128)(2,1)S(1)} %bitcast.3), channel_id=1, source_target_pairs={{0,1},{1,0},{2,3},{3,2},{4,5},{5,4},{6,7},{7,6},{8,9},{9,8},{10,11... | collective-permute-start | bytes 4718600 | tf_op jit(solution)/shard_map/ppermute | solution.py:337
  59.7 4.6 %collective-permute-start.8 = (f32[16,104,128]{2,1,0:T(8,128)S(1)}, f32[16,104,128]{2,1,0:T(8,128)S(1)}, u32[]{:S(2)}, u32[]{:S(2)}) collective-permute-start(f32[16,104,128]{2,1,0:T(8,128)S(1)} %get-tuple-element.28.other_ref), channel_id=1, source_target_pairs={{0,1},{1,0},{2,3},{3,2},{4,5},{5,4},{6,7},{7,6},{8,9},{9,8},{10,11... | collective-permute-start | bytes 2555912 | tf_op jit(solution)/shard_map/ppermute | solution.py:337
  92.5 5.9 %collective-permute-start.9 = (f32[16,104,128]{2,1,0:T(8,128)S(1)}, f32[16,104,128]{2,1,0:T(8,128)S(1)}, u32[]{:S(2)}, u32[]{:S(2)}) collective-permute-start(f32[16,104,128]{2,1,0:T(8,128)S(1)} %get-tuple-element.33.other_ref), channel_id=1, source_target_pairs={{0,1},{1,0},{2,3},{3,2},{4,5},{5,4},{6,7},{7,6},{8,9},{9,8},{10,11... | collective-permute-start | bytes 2555912 | tf_op jit(solution)/shard_map/ppermute | solution.py:337

commit v7 on v6

--- a/solution.py
+++ b/solution.py
@@ -29,6 +29,7 @@
 COLUMN_BLOCK = 256
 LANES = 128
 PIVOTS = 8
+SAMPLE = 24
 PACKED = 24
 MERGE_COST = 10_350_000_000
 
@@ -224,8 +225,35 @@
     out_ref[:, HALF:, :] = jnp.broadcast_to(terms[None], (PEERS, 16, LANES))
 
 
-def add_kernel(own_ref, other_ref, out_ref):
-    out_ref[...] = own_ref[...] + other_ref[...]
+def split_kernel(own_ref, other_ref, out_ref):
+    sums = own_ref[:, :HALF, :] + other_ref[:, :HALF, :]
+    sample = sums[:, :SAMPLE].reshape(PEERS * SAMPLE, LANES)
+    gram = lax.dot_general(sample, sample, (((0,), (0,)), ((), ())), preferred_element_type=f32)
+    gram = gram[:K] + swap_lanes(gram[K:])
+    gram = jnp.concatenate([jnp.where(left_lanes(gram), gram, 0.0), jnp.zeros_like(gram)], axis=0)
+    main = jnp.dot(gram[:8], gram, preferred_element_type=f32)[:1]
+    main = main * lax.rsqrt(jnp.sum(main * main) + 1e-30)
+    main = main.astype(bf16).astype(f32)
+    both = main + swap_lanes(main)
+    row = lax.broadcasted_iota(jnp.int32, (LANES, LANES), 0)
+    turned = jnp.where((row < K) == left_lanes(row), both, 0.0).astype(bf16)
+    wide = jnp.concatenate([sums, jnp.zeros((PEERS, LANES - HALF, LANES), f32)], axis=1)
+    wide = wide.reshape(PEERS * LANES, LANES).astype(bf16)
+    factor = lax.dot_general(
+        wide, turned, (((1,), (1,)), ((), ())), preferred_element_type=f32
+    ).astype(bf16)
+    known = (factor.astype(f32) * both).reshape(PEERS, LANES, LANES)
+    out_ref[:, :HALF, :] = (sums - known[:, :HALF]).astype(bf16)
+    index = lax.broadcasted_iota(jnp.int32, (8, LANES), 0)
+    lane = lax.broadcasted_iota(jnp.int32, (8, LANES), 1)
+    pick = jnp.where((lane == index * K) & (index < 2), 1.0, 0.0).astype(bf16)
+    rows = lax.dot_general(pick, factor, (((1,), (1,)), ((), ())), preferred_element_type=f32)
+    hi, mid = two_parts(own_ref[0, HALF : HALF + 1, :] + other_ref[0, HALF : HALF + 1, :])
+    low = jnp.where(index == 0, main, jnp.where(index == 1, swap_lanes(main), 0.0))
+    low = jnp.where(index == 2, hi, jnp.where(index == 3, mid, low))
+    for p in range(PEERS):
+        top = rows[:, p * LANES : (p + 1) * LANES]
+        out_ref[p, HALF:, :] = jnp.concatenate([top, low], axis=0).astype(bf16)
 
 
 def middle_kernel(got_ref, inv_ref, root_ref, out_ref, terms_ref):
@@ -246,9 +274,14 @@
 
 
 def gram_kernel(got_ref, inv_ref, root_ref, terms_ref, vectors_ref, out_ref):
-    sums = jnp.sum(got_ref[...], axis=0)
-    ratio = sums[HALF : HALF + 1] / terms_ref[1:2, :]
-    vectors = inv_ref[...] * sums[:HALF] - root_ref[...] * ratio
+    tail = got_ref[:, HALF:, :].astype(f32)
+    factors = tail[:, :8].reshape(PEERS * 8, LANES).astype(bf16)
+    mains = tail[:, 8:].reshape(PEERS * 8, LANES).astype(bf16)
+    known = lax.dot_general(factors, mains, (((0,), (0,)), ((), ())), preferred_element_type=f32)
+    sums = jnp.sum(got_ref[:, :HALF, :].astype(f32), axis=0) + known[:HALF]
+    terms = jnp.sum(tail[:, 8:], axis=0)
+    ratio = (terms[2:3] + terms[3:4]) / terms_ref[1:2, :]
+    vectors = inv_ref[...] * sums - root_ref[...] * ratio
     vectors_ref[...] = vectors
     tall = jnp.concatenate([vectors, jnp.zeros((LANES - HALF, LANES), f32)], axis=0)
     product = jnp.dot(tall.T, tall, precision=HIGHEST, preferred_element_type=f32)
@@ -405,7 +438,8 @@
     )
     theirs = swap_core(mine)
     (mine,) = call(again_kernel, [sent], [own_tile, packed, mine], (), flops)
-    (total,) = call(narrow_kernel, [shape(PEERS, HALF + 16, LANES, dtype=bf16)], [mine, theirs])
+    halved = shape(PEERS, HALF + 16, LANES, dtype=bf16)
+    (total,) = call(narrow_kernel, [halved], [mine, theirs])
     got = exchange(total, PLANE)
     total, terms = call(
         middle_kernel,
@@ -416,7 +450,7 @@
     mine, packed = call(second_kernel, [sent, weights], [other_tile, got], (), flops)
     theirs = swap_core(mine)
     (mine,) = call(again_kernel, [sent], [own_tile, packed, mine], (), flops)
-    (total,) = call(add_kernel, [sent], [mine, theirs])
+    (total,) = call(split_kernel, [halved], [mine, theirs])
     got = exchange(total, PLANE)
     gram = shape(PEERS, PACKED, LANES)
     vectors, total = call(gram_kernel, [own, gram], [got, inv, root, terms])

time: 145 us -> 142 us (0.979)
  blocking collectives: 78.2 us -> 74 us
    all_to_all x6, blocking collectives: 78.2 us -> 74 us  [exchange(): return lax.all_to_all(value, axes, 0, 0, tiled=True)]
where the time goes in v7:
time: 142 us
  blocking collectives  74 us (52%)
  starting transfers between devices  31.4 us (22%)
  Pallas kernels  24.6 us (17%)
  waiting for transfers between devices  11.7 us (8%)
    all_to_all x6, blocking collectives, exchange(): return lax.all_to_all(value, axes, 0, 0, tiled=True)  74 us
    pallas_call x15, Pallas kernels, call(): pl.pallas_call(kernel, out_shape=tuple(outs), in_specs=[pl.BlockSpec(memo...  24.6 us
    ppermute x7, starting transfers between devices, shift(): lax.ppermute(value, 'z', [(i, (i + step) % DEPTH) for i in range(DEPTH)])  15.2 us
    ppermute x3, starting transfers between devices, swap_core(): return lax.ppermute(value, 'core', [(0, 1), (1, 0)])  9.52 us
    ppermute x7, waiting for transfers between devices, shift(): lax.ppermute(value, 'z', [(i, (i + step) % DEPTH) for i in range(DEPTH)])  7.58 us
    all_to_all x1, starting transfers between devices, exchange(): return lax.all_to_all(value, axes, 0, 0, tiled=True)  6.75 us
    all_to_all x1, waiting for transfers between devices, exchange(): return lax.all_to_all(value, axes, 0, 0, tiled=True)  4.12 us
  transfers between devices with their start and end apart: 11, of which 4 were waited for; matrix products, arithmetic and copies ran while one was open for 0% of the time, Pallas kernels for 7%

profile of v7, /device:TPU:1, one launch (start us, length us, event | category | flops | bytes accessed | tf_op | source)
XLA Modules:
  0.0 141.9 jit_solution(1965310728109396571)
XLA Ops:
  0.0 1.1 shard_map.28.line_ref.refs_0_
  1.1 6.5 %collective-permute-start = (bf16[192,384]{1,0:T(8,128)(2,1)S(1)}, bf16[192,384]{1,0:T(8,128)(2,1)S(1)}, u32[]{:S(2)}, u32[]{:S(2)}) collective-permute-start(bf16[192,384]{1,0:T(8,128)(2,1)S(1)} %shard_map.28.line_ref.refs_0_), channel_id=1, source_target_pairs={{0,224},{32,0},{64,32},{96,64},{128,96},{160,128},{192,160},{224,1... | collective-permute-start | bytes 442376 | tf_op jit(solution)/shard_map/ppermute | solution.py:374
  7.6 1.3 shard_map.29
  8.9 6.8 %all-to-all-start = ((bf16[16,192,256]{2,1,0:T(8,128)(2,1)}), bf16[16,192,256]{2,1,0:T(8,128)(2,1)S(1)}, u32[]{:S(2)}, u32[]{:S(2)}) async-start(bf16[16,192,256]{2,1,0:T(8,128)(2,1)} %shard_map.29), calls=%async_computation | async-start | bytes 3145728 | tf_op jit(solution)/shard_map/all_to_all | solution.py:366
  15.7 0.1 collective-permute-start.4
  15.8 2.7 %collective-permute-start.1 = (bf16[192,384]{1,0:T(8,128)(2,1)S(1)}, bf16[192,384]{1,0:T(8,128)(2,1)S(1)}, u32[]{:S(2)}, u32[]{:S(2)}) collective-permute-start(bf16[192,384]{1,0:T(8,128)(2,1)S(1)} %collective-permute-done.refs_1_), channel_id=1, source_target_pairs={{0,224},{32,0},{64,32},{96,64},{128,96},{160,128},{192,160},{224,1... | collective-permute-start | bytes 442376 | tf_op jit(solution)/shard_map/ppermute | solution.py:374
  18.4 2.5 %collective-permute-done.4.refs_7_ = bf16[192,384]{1,0:T(8,128)(2,1)S(1)} collective-permute-done((bf16[192,384]{1,0:T(8,128)(2,1)S(1)}, bf16[192,384]{1,0:T(8,128)(2,1)S(1)}, u32[]{:S(2)}, u32[]{:S(2)}) %collective-permute-start.4) | collective-permute-done | bytes 147488 | tf_op jit(solution)/shard_map/ppermute | solution.py:374
  21.0 3.0 %collective-permute-start.2 = (bf16[192,384]{1,0:T(8,128)(2,1)S(1)}, bf16[192,384]{1,0:T(8,128)(2,1)S(1)}, u32[]{:S(2)}, u32[]{:S(2)}) collective-permute-start(bf16[192,384]{1,0:T(8,128)(2,1)S(1)} %collective-permute-done.1.refs_2_), channel_id=1, source_target_pairs={{0,224},{32,0},{64,32},{96,64},{128,96},{160,128},{192,160},{224,1... | collective-permute-start | bytes 442376 | tf_op jit(solution)/shard_map/ppermute | solution.py:374
  23.9 2.5 %collective-permute-done.5.refs_6_ = bf16[192,384]{1,0:T(8,128)(2,1)S(1)} collective-permute-done((bf16[192,384]{1,0:T(8,128)(2,1)S(1)}, bf16[192,384]{1,0:T(8,128)(2,1)S(1)}, u32[]{:S(2)}, u32[]{:S(2)}) %collective-permute-start.5) | collective-permute-done | bytes 147488 | tf_op jit(solution)/shard_map/ppermute | solution.py:374
  26.5 3.0 %collective-permute-start.3 = (bf16[192,384]{1,0:T(8,128)(2,1)S(1)}, bf16[192,384]{1,0:T(8,128)(2,1)S(1)}, u32[]{:S(2)}, u32[]{:S(2)}) collective-permute-start(bf16[192,384]{1,0:T(8,128)(2,1)S(1)} %collective-permute-done.2.refs_3_), channel_id=1, source_target_pairs={{0,224},{32,0},{64,32},{96,64},{128,96},{160,128},{192,160},{224,1... | collective-permute-start | bytes 442376 | tf_op jit(solution)/shard_map/ppermute | solution.py:374
  29.4 2.5 %collective-permute-done.6.refs_5_ = bf16[192,384]{1,0:T(8,128)(2,1)S(1)} collective-permute-done((bf16[192,384]{1,0:T(8,128)(2,1)S(1)}, bf16[192,384]{1,0:T(8,128)(2,1)S(1)}, u32[]{:S(2)}, u32[]{:S(2)}) %collective-permute-start.6) | collective-permute-done | bytes 147488 | tf_op jit(solution)/shard_map/ppermute | solution.py:374
  32.0 0.1 shard_map.30.refs_1_.cols_ref
  32.1 4.1 %all-to-all-done = bf16[16,192,256]{2,1,0:T(8,128)(2,1)S(1)} async-done(((bf16[16,192,256]{2,1,0:T(8,128)(2,1)}), bf16[16,192,256]{2,1,0:T(8,128)(2,1)S(1)}, u32[]{:S(2)}, u32[]{:S(2)}) %all-to-all-start) | async-done | bytes 1572896 | tf_op jit(solution)/shard_map/all_to_all | solution.py:366
  36.2 4.2 %collective-permute-start.7 = (bf16[3072,256]{1,0:T(8,128)(2,1)S(1)}, bf16[3072,256]{1,0:T(8,128)(2,1)S(1)}, u32[]{:S(2)}, u32[]{:S(2)}) collective-permute-start(bf16[3072,256]{1,0:T(8,128)(2,1)S(1)} %bitcast.3), channel_id=1, source_target_pairs={{0,1},{1,0},{2,3},{3,2},{4,5},{5,4},{6,7},{7,6},{8,9},{9,8},{10,11... | collective-permute-start | bytes 4718600 | tf_op jit(solution)/shard_map/ppermute | solution.py:370
  40.4 3.1 %shard_map.31 = (bf16[3072,1536]{1,0:T(8,128)(2,1)S(1)}, f32[8,1536]{1,0:T(8,128)S(1)}) custom-call(bf16[3072,256]{1,0:T(8,128)(2,1)S(1)} %bitcast.4, bf16[1536,384]{1,0:T(8,128)(2,1)S(1)} %shard_map.30.refs_1_.cols_ref), custom_call_target="tpu_custom_call" | custom-call | flops 2415919104 | bytes 12238848 | tf_op jit(solution)/shard_map/pallas_call | solution.py:48
  43.6 3.2 %shard_map.32 = (bf16[3072,1536]{1,0:T(8,128)(2,1)S(1)}, f32[8,16,128]{2,1,0:T(8,128)S(1)}) custom-call(bf16[3072,256]{1,0:T(8,128)(2,1)S(1)} %collective-permute-done.7.refs_0_, bf16[1536,384]{1,0:T(8,128)(2,1)S(1)} %shard_map.30.refs_1_.cols_ref, f32[8,1536]{1,0:T(8,128)S(1)} %get-tuple-element.24.refs_2_), custom_call_target="tpu_custom_call" | custom-call | flops 2415919104 | bytes 12304384 | tf_op jit(solution)/shard_map/pallas_call | solution.py:48
  46.8 9.9 %all_to_all.35.sums_ref = f32[8,16,128]{2,1,0:T(8,128)S(1)} all-to-all(f32[8,16,128]{2,1,0:T(8,128)S(1)} %get-tuple-element.26), channel_id=1, replica_groups=mesh['z'=8,'x'=4,'y'=4,'core'=2] {'z'}, dimensions={0} | all-to-all | bytes 131072 | tf_op jit(solution)/shard_map/all_to_all | solution.py:366
  56.7 3.0 %shard_map.33 = (f32[16,104,128]{2,1,0:T(8,128)S(1)}, bf16[1536,128]{1,0:T(8,128)(2,1)S(1)}, f32[96,128]{1,0:T(8,128)S(1)}, f32[96,128]{1,0:T(8,128)S(1)}) custom-call(bf16[3072,1536]{1,0:T(8,128)(2,1)S(1)} %get-tuple-element.25.tile_ref, f32[8,16,128]{2,1,0:T(8,128)S(1)} %all_to_all.35.sums_ref, bf16[1536,384]{1,0:T(8,128)(2,1)S(1)} %shard_map.30.refs_1_.cols_ref), custom_call_target="tpu_custom_call" | custom-call | flops 1207959552 | bytes 12025856 | tf_op jit(solution)/shard_map/pallas_call | solution.py:48
  59.7 2.0 %collective-permute-start.8 = (f32[16,104,128]{2,1,0:T(8,128)S(1)}, f32[16,104,128]{2,1,0:T(8,128)S(1)}, u32[]{:S(2)}, u32[]{:S(2)}) collective-permute-start(f32[16,104,128]{2,1,0:T(8,128)S(1)} %get-tuple-element.28.other_ref), channel_id=1, source_target_pairs={{0,1},{1,0},{2,3},{3,2},{4,5},{5,4},{6,7},{7,6},{8,9},{9,8},{10,11... | collective-permute-start | bytes 2555912 | tf_op jit(solution)/shard_map/ppermute | solution.py:370
  61.8 2.6 %shard_map.34.own_ref = f32[16,104,128]{2,1,0:T(8,128)S(1)} custom-call(bf16[3072,1536]{1,0:T(8,128)(2,1)S(1)} %get-tuple-element.23.tile_ref, bf16[1536,128]{1,0:T(8,128)(2,1)S(1)} %get-tuple-element.27.weights_ref, f32[16,104,128]{2,1,0:T(8,128)S(1)} %get-tuple-element.28.other_ref), custom_call_target="tpu_custom_call" | custom-call | flops 1207959552 | bytes 11534336 | tf_op jit(solution)/shard_map/pallas_call | solution.py:48
  64.5 13.6 %all_to_all.36.got_ref = bf16[16,112,128]{2,1,0:T(8,128)(2,1)S(1)} all-to-all(bf16[16,112,128]{2,1,0:T(8,128)(2,1)S(1)} %shard_map.35), channel_id=1, replica_groups=mesh['z'=8,'x'=4,'y'=4,'core'=2] {'x','y'}, dimensions={0} | all-to-all | bytes 917504 | tf_op jit(solution)/shard_map/all_to_all | solution.py:366
  78.1 0.2 shard_map.36
  78.3 11.5 %all_to_all.37.got_ref = bf16[8,112,128]{2,1,0:T(8,128)(2,1)S(1)} all-to-all(bf16[8,112,128]{2,1,0:T(8,128)(2,1)S(1)} %get-tuple-element.31), channel_id=1, replica_groups=mesh['z'=8,'x'=4,'y'=4,'core'=2] {'z'}, dimensions={0} | all-to-all | bytes 458752 | tf_op jit(solution)/shard_map/all_to_all | solution.py:366
  89.8 2.7 %shard_map.37 = (f32[16,104,128]{2,1,0:T(8,128)S(1)}, bf16[1536,128]{1,0:T(8,128)(2,1)S(1)}) custom-call(bf16[3072,1536]{1,0:T(8,128)(2,1)S(1)} %get-tuple-element.25.tile_ref, bf16[8,112,128]{2,1,0:T(8,128)(2,1)S(1)} %all_to_all.37.got_ref), custom_call_target="tpu_custom_call" | custom-call | flops 1207959552 | bytes 10911744 | tf_op jit(solution)/shard_map/pallas_call | solution.py:48
  92.5 3.3 %collective-permute-start.9 = (f32[16,104,128]{2,1,0:T(8,128)S(1)}, f32[16,104,128]{2,1,0:T(8,128)S(1)}, u32[]{:S(2)}, u32[]{:S(2)}) collective-permute-start(f32[16,104,128]{2,1,0:T(8,128)S(1)} %get-tuple-element.33.other_ref), channel_id=1, source_target_pairs={{0,1},{1,0},{2,3},{3,2},{4,5},{5,4},{6,7},{7,6},{8,9},{9,8},{10,11... | collective-permute-start | bytes 2555912 | tf_op jit(solution)/shard_map/ppermute | solution.py:370
  95.8 2.6 %shard_map.38.own_ref = f32[16,104,128]{2,1,0:T(8,128)S(1)} custom-call(bf16[3072,1536]{1,0:T(8,128)(2,1)S(1)} %get-tuple-element.23.tile_ref, bf16[1536,128]{1,0:T(8,128)(2,1)S(1)} %get-tuple-element.32.weights_ref, f32[16,104,128]{2,1,0:T(8,128)S(1)} %get-tuple-element.33.other_ref), custom_call_target="tpu_custom_call" | custom-call | flops 1207959552 | bytes 11534336 | tf_op jit(solution)/shard_map/pallas_call | solution.py:48
  98.4 1.2 shard_map.39
  99.6 13.5 %all_to_all.38.got_ref = bf16[16,112,128]{2,1,0:T(8,128)(2,1)S(1)} all-to-all(bf16[16,112,128]{2,1,0:T(8,128)(2,1)S(1)} %shard_map.39), channel_id=1, replica_groups=mesh['z'=8,'x'=4,'y'=4,'core'=2] {'x','y'}, dimensions={0} | all-to-all | bytes 917504 | tf_op jit(solution)/shard_map/all_to_all | solution.py:366
  113.0 0.7 shard_map.40
  113.7 14.9 %all_to_all.39.got_ref = f32[16,24,128]{2,1,0:T(8,128)S(1)} all-to-all(f32[16,24,128]{2,1,0:T(8,128)S(1)} %get-tuple-element.35), channel_id=1, replica_groups=mesh['z'=8,'x'=4,'y'=4,'core'=2] {'z','core'}, dimensions={0} | all-to-all | bytes 393216 | tf_op jit(solution)/shard_map/all_to_all | solution.py:366
  128.7 10.6 %all_to_all.40.got_ref = f32[16,24,128]{2,1,0:T(8,128)S(1)} all-to-all(f32[16,24,128]{2,1,0:T(8,128)S(1)} %shard_map.41), channel_id=1, replica_groups=mesh['z'=8,'x'=4,'y'=4,'core'=2] {'x','y'}, dimensions={0} | all-to-all | bytes 393216 | tf_op jit(solution)/shard_map/all_to_all | solution.py:366
  139.2 2.7 %shard_map.42 = f32[64,192]{1,0:T(8,128)} custom-call(f32[16,24,128]{2,1,0:T(8,128)S(1)} %all_to_all.40.got_ref, f32[96,128]{1,0:T(8,128)S(1)} %get-tuple-element.36.vectors_ref), custom_call_target="tpu_custom_call" | custom-call | bytes 294912 | tf_op jit(solution)/shard_map/pallas_call | solution.py:48
  (11 shorter events, 0.1 us)
Async XLA Ops:
  1.1 14.7 %collective-permute-start = (bf16[192,384]{1,0:T(8,128)(2,1)S(1)}, bf16[192,384]{1,0:T(8,128)(2,1)S(1)}, u32[]{:S(2)}, u32[]{:S(2)}) collective-permute-start(bf16[192,384]{1,0:T(8,128)(2,1)S(1)} %shard_map.28.line_ref.refs_0_), channel_id=1, source_target_pairs={{0,224},{32,0},{64,32},{96,64},{128,96},{160,128},{192,160},{224,1... | collective-permute-start | bytes 442376 | tf_op jit(solution)/shard_map/ppermute | solution.py:374
  8.9 27.3 %all-to-all-start = ((bf16[16,192,256]{2,1,0:T(8,128)(2,1)}), bf16[16,192,256]{2,1,0:T(8,128)(2,1)S(1)}, u32[]{:S(2)}, u32[]{:S(2)}) async-start(bf16[16,192,256]{2,1,0:T(8,128)(2,1)} %shard_map.29), calls=%async_computation | async-start | bytes 3145728 | tf_op jit(solution)/shard_map/all_to_all | solution.py:366
  15.7 5.3 %collective-permute-start.4 = (bf16[192,384]{1,0:T(8,128)(2,1)S(1)}, bf16[192,384]{1,0:T(8,128)(2,1)S(1)}, u32[]{:S(2)}, u32[]{:S(2)}) collective-permute-start(bf16[192,384]{1,0:T(8,128)(2,1)S(1)} %shard_map.28.line_ref.refs_0_), channel_id=1, source_target_pairs={{0,32},{32,64},{64,96},{96,128},{128,160},{160,192},{192,224},{224... | collective-permute-start | bytes 442376 | tf_op jit(solution)/shard_map/ppermute | solution.py:374
  15.8 5.2 %collective-permute-start.1 = (bf16[192,384]{1,0:T(8,128)(2,1)S(1)}, bf16[192,384]{1,0:T(8,128)(2,1)S(1)}, u32[]{:S(2)}, u32[]{:S(2)}) collective-permute-start(bf16[192,384]{1,0:T(8,128)(2,1)S(1)} %collective-permute-done.refs_1_), channel_id=1, source_target_pairs={{0,224},{32,0},{64,32},{96,64},{128,96},{160,128},{192,160},{224,1... | collective-permute-start | bytes 442376 | tf_op jit(solution)/shard_map/ppermute | solution.py:374
  21.0 5.5 %collective-permute-start.5 = (bf16[192,384]{1,0:T(8,128)(2,1)S(1)}, bf16[192,384]{1,0:T(8,128)(2,1)S(1)}, u32[]{:S(2)}, u32[]{:S(2)}) collective-permute-start(bf16[192,384]{1,0:T(8,128)(2,1)S(1)} %collective-permute-done.4.refs_7_), channel_id=1, source_target_pairs={{0,32},{32,64},{64,96},{96,128},{128,160},{160,192},{192,224},{224... | collective-permute-start | bytes 442376 | tf_op jit(solution)/shard_map/ppermute | solution.py:374
  21.0 5.5 %collective-permute-start.2 = (bf16[192,384]{1,0:T(8,128)(2,1)S(1)}, bf16[192,384]{1,0:T(8,128)(2,1)S(1)}, u32[]{:S(2)}, u32[]{:S(2)}) collective-permute-start(bf16[192,384]{1,0:T(8,128)(2,1)S(1)} %collective-permute-done.1.refs_2_), channel_id=1, source_target_pairs={{0,224},{32,0},{64,32},{96,64},{128,96},{160,128},{192,160},{224,1... | collective-permute-start | bytes 442376 | tf_op jit(solution)/shard_map/ppermute | solution.py:374
  26.5 5.5 %collective-permute-start.6 = (bf16[192,384]{1,0:T(8,128)(2,1)S(1)}, bf16[192,384]{1,0:T(8,128)(2,1)S(1)}, u32[]{:S(2)}, u32[]{:S(2)}) collective-permute-start(bf16[192,384]{1,0:T(8,128)(2,1)S(1)} %collective-permute-done.5.refs_6_), channel_id=1, source_target_pairs={{0,32},{32,64},{64,96},{96,128},{128,160},{160,192},{192,224},{224... | collective-permute-start | bytes 442376 | tf_op jit(solution)/shard_map/ppermute | solution.py:374
  26.5 5.5 %collective-permute-start.3 = (bf16[192,384]{1,0:T(8,128)(2,1)S(1)}, bf16[192,384]{1,0:T(8,128)(2,1)S(1)}, u32[]{:S(2)}, u32[]{:S(2)}) collective-permute-start(bf16[192,384]{1,0:T(8,128)(2,1)S(1)} %collective-permute-done.2.refs_3_), channel_id=1, source_target_pairs={{0,224},{32,0},{64,32},{96,64},{128,96},{160,128},{192,160},{224,1... | collective-permute-start | bytes 442376 | tf_op jit(solution)/shard_map/ppermute | solution.py:374
  36.2 7.4 %collective-permute-start.7 = (bf16[3072,256]{1,0:T(8,128)(2,1)S(1)}, bf16[3072,256]{1,0:T(8,128)(2,1)S(1)}, u32[]{:S(2)}, u32[]{:S(2)}) collective-permute-start(bf16[3072,256]{1,0:T(8,128)(2,1)S(1)} %bitcast.3), channel_id=1, source_target_pairs={{0,1},{1,0},{2,3},{3,2},{4,5},{5,4},{6,7},{7,6},{8,9},{9,8},{10,11... | collective-permute-start | bytes 4718600 | tf_op jit(solution)/shard_map/ppermute | solution.py:370
  59.7 4.6 %collective-permute-start.8 = (f32[16,104,128]{2,1,0:T(8,128)S(1)}, f32[16,104,128]{2,1,0:T(8,128)S(1)}, u32[]{:S(2)}, u32[]{:S(2)}) collective-permute-start(f32[16,104,128]{2,1,0:T(8,128)S(1)} %get-tuple-element.28.other_ref), channel_id=1, source_target_pairs={{0,1},{1,0},{2,3},{3,2},{4,5},{5,4},{6,7},{7,6},{8,9},{9,8},{10,11... | collective-permute-start | bytes 2555912 | tf_op jit(solution)/shard_map/ppermute | solution.py:370
  92.5 5.9 %collective-permute-start.9 = (f32[16,104,128]{2,1,0:T(8,128)S(1)}, f32[16,104,128]{2,1,0:T(8,128)S(1)}, u32[]{:S(2)}, u32[]{:S(2)}) collective-permute-start(f32[16,104,128]{2,1,0:T(8,128)S(1)} %get-tuple-element.33.other_ref), channel_id=1, source_target_pairs={{0,1},{1,0},{2,3},{3,2},{4,5},{5,4},{6,7},{7,6},{8,9},{9,8},{10,11... | collective-permute-start | bytes 2555912 | tf_op jit(solution)/shard_map/ppermute | solution.py:370

commit v8 on v7

--- a/solution.py
+++ b/solution.py
@@ -26,10 +26,10 @@
 COLUMNS = DEPTH * DOCS
 ROWS = PEERS * DOCS
 ROW_BLOCK = 3072
-COLUMN_BLOCK = 256
+COLUMN_BLOCK = 768
 LANES = 128
 PIVOTS = 8
-SAMPLE = 24
+SAMPLE = 8
 PACKED = 24
 MERGE_COST = 10_350_000_000
 
@@ -42,14 +42,14 @@
     return jax.ShapeDtypeStruct(dims, dtype)
 
 
-def call(kernel, outs, args, scratch=(), flops=0, space=pltpu.VMEM):
-    vmem = pl.BlockSpec(memory_space=pltpu.VMEM)
+def call(kernel, outs, args, scratch=(), flops=0, space=pltpu.VMEM, spaces=None):
+    spaces = spaces or [pltpu.VMEM] * len(outs)
     moved = sum(math.prod(a.shape) * a.dtype.itemsize for a in (*args, *outs))
     return pl.pallas_call(
         kernel,
         out_shape=tuple(outs),
         in_specs=[pl.BlockSpec(memory_space=space)] * len(args),
-        out_specs=tuple(vmem for _ in outs),
+        out_specs=tuple(pl.BlockSpec(memory_space=out) for out in spaces),
         scratch_shapes=list(scratch),
         cost_estimate=pl.CostEstimate(flops=flops, bytes_accessed=moved, transcendentals=0),
         compiler_params=pltpu.CompilerParams(vmem_limit_bytes=8 * 2**20),
@@ -75,27 +75,29 @@
     return hi, (value - hi).astype(bf16).astype(f32)
 
 
-def unit_kernel(emb_hbm, start_hbm, line_ref, emb_ref, start_ref, done):
+def unit_kernel(emb_hbm, start_hbm, line_ref, plane_hbm, emb_ref, start_ref, row_ref, done, sent):
     copies = [
         pltpu.make_async_copy(emb_hbm, emb_ref, done.at[0]),
         pltpu.make_async_copy(start_hbm, start_ref, done.at[1]),
     ]
     for copy in copies:
         copy.start()
-    for copy in copies:
-        copy.wait()
+    copies[0].wait()
     wide = emb_ref[...].astype(f32)
     unit = wide * lax.rsqrt(jnp.sum(wide * wide, axis=1, keepdims=True) + 1e-06)
-    line_ref[:, :E] = unit.astype(bf16)
+    unit = unit.astype(bf16)
+    line_ref[:, :E] = unit
+    row_ref[...] = unit * (sharpness / 2)
+    outs = [pltpu.make_async_copy(row_ref, plane_hbm.at[p], sent.at[p]) for p in range(PEERS)]
+    for copy in outs:
+        copy.start()
+    copies[1].wait()
     start = jnp.concatenate([start_ref[...], jnp.zeros((K, 2 * LANES - DOCS), f32)], axis=1)
     start = jnp.concatenate([start, jnp.zeros_like(start)], axis=0).T[:DOCS]
     hi, mid = two_parts(start)
     line_ref[:, E:] = jnp.where(left_lanes(hi), hi, swap_lanes(mid)).astype(bf16)
-
-
-def plane_kernel(line_ref, plane_ref):
-    unit = line_ref[:, :E] * (sharpness / 2)
-    plane_ref[...] = jnp.broadcast_to(unit[None], plane_ref.shape)
+    for copy in outs:
+        copy.wait()
 
 
 def merge_kernel(*refs):
@@ -377,9 +379,9 @@
 def local(embeddings, start_vectors):
     all_docs = embeddings.shape[0] * lax.axis_size(AXES)
     width = E + 2 * K
-    (line,) = call(
+    line, plane = call(
         unit_kernel,
-        [shape(DOCS, width, dtype=bf16)],
+        [shape(DOCS, width, dtype=bf16), shape(PEERS, DOCS, E, dtype=bf16)],
         [
             pltpu.with_memory_space_constraint(value, pltpu.HBM)
             for value in (embeddings, start_vectors.T)
@@ -387,11 +389,13 @@
         [
             pltpu.VMEM((DOCS, E), bf16),
             pltpu.VMEM((K, DOCS), f32),
+            pltpu.VMEM((DOCS, E), bf16),
             pltpu.SemaphoreType.DMA((2,)),
+            pltpu.SemaphoreType.DMA((PEERS,)),
         ],
         space=pltpu.HBM,
-    )
-    (plane,) = call(plane_kernel, [shape(PEERS, DOCS, E, dtype=bf16)], [line])
+        spaces=[pltpu.VMEM, pltpu.HBM],
+    )
     pieces = [line] + [None] * (DEPTH - 1)
     behind = ahead = line
     for i in range(1, DEPTH // 2):

time: 142 us -> 142 us (level)
    pallas_call x15 -> x14, Pallas kernels: 24.6 us -> 24.6 us  [call(): pl.pallas_call(kernel, out_shape=tuple(outs), in_specs=[pl.BlockSpec(memo...]
  transfers between devices with their start and end apart: 11 -> 11, of which waited for: 4 -> 4; matrix products, arithmetic and copies ran while one was open for 0% -> 0% of each run, Pallas kernels for 7% -> 6%
where the time goes in v8:
time: 142 us
  blocking collectives  74 us (52%)
  starting transfers between devices  31.4 us (22%)
  Pallas kernels  24.6 us (17%)
  waiting for transfers between devices  11.7 us (8%)
    all_to_all x6, blocking collectives, exchange(): return lax.all_to_all(value, axes, 0, 0, tiled=True)  74 us
    pallas_call x14, Pallas kernels, call(): pl.pallas_call(kernel, out_shape=tuple(outs), in_specs=[pl.BlockSpec(memo...  24.6 us
    ppermute x7, starting transfers between devices, shift(): lax.ppermute(value, 'z', [(i, (i + step) % DEPTH) for i in range(DEPTH)])  15.2 us
    ppermute x3, starting transfers between devices, swap_core(): return lax.ppermute(value, 'core', [(0, 1), (1, 0)])  9.49 us
    ppermute x7, waiting for transfers between devices, shift(): lax.ppermute(value, 'z', [(i, (i + step) % DEPTH) for i in range(DEPTH)])  7.58 us
    all_to_all x1, starting transfers between devices, exchange(): return lax.all_to_all(value, axes, 0, 0, tiled=True)  6.75 us
    all_to_all x1, waiting for transfers between devices, exchange(): return lax.all_to_all(value, axes, 0, 0, tiled=True)  4.12 us
  transfers between devices with their start and end apart: 11, of which 4 were waited for; matrix products, arithmetic and copies ran while one was open for 0% of the time, Pallas kernels for 6%

profile of v8, /device:TPU:1, one launch (start us, length us, event | category | flops | bytes accessed | tf_op | source)
XLA Modules:
  0.0 141.8 jit_solution(6059021135217652368)
XLA Ops:
  0.0 2.3 %shard_map.28 = (bf16[192,384]{1,0:T(8,128)(2,1)S(1)}, bf16[16,192,256]{2,1,0:T(8,128)(2,1)}) custom-call(bf16[192,256]{1,0:T(8,128)(2,1)} %emb_hbm.1, f32[64,192]{1,0:T(8,128)} %bitcast.5), custom_call_target="tpu_custom_call" | custom-call | bytes 1867776 | tf_op jit(solution)/shard_map/pallas_call | solution.py:48
  2.3 6.5 %collective-permute-start = (bf16[192,384]{1,0:T(8,128)(2,1)S(1)}, bf16[192,384]{1,0:T(8,128)(2,1)S(1)}, u32[]{:S(2)}, u32[]{:S(2)}) collective-permute-start(bf16[192,384]{1,0:T(8,128)(2,1)S(1)} %get-tuple-element.24.refs_0_), channel_id=1, source_target_pairs={{0,224},{32,0},{64,32},{96,64},{128,96},{160,128},{192,160},{224,1... | collective-permute-start | bytes 442376 | tf_op jit(solution)/shard_map/ppermute | solution.py:376
  8.8 6.8 %all-to-all-start = ((bf16[16,192,256]{2,1,0:T(8,128)(2,1)}), bf16[16,192,256]{2,1,0:T(8,128)(2,1)S(1)}, u32[]{:S(2)}, u32[]{:S(2)}) async-start(bf16[16,192,256]{2,1,0:T(8,128)(2,1)} %get-tuple-element.23), calls=%async_computation | async-start | bytes 3145728 | tf_op jit(solution)/shard_map/all_to_all | solution.py:368
  15.6 0.1 collective-permute-start.4
  15.7 2.7 %collective-permute-start.1 = (bf16[192,384]{1,0:T(8,128)(2,1)S(1)}, bf16[192,384]{1,0:T(8,128)(2,1)S(1)}, u32[]{:S(2)}, u32[]{:S(2)}) collective-permute-start(bf16[192,384]{1,0:T(8,128)(2,1)S(1)} %collective-permute-done.refs_1_), channel_id=1, source_target_pairs={{0,224},{32,0},{64,32},{96,64},{128,96},{160,128},{192,160},{224,1... | collective-permute-start | bytes 442376 | tf_op jit(solution)/shard_map/ppermute | solution.py:376
  18.4 2.5 %collective-permute-done.4.refs_7_ = bf16[192,384]{1,0:T(8,128)(2,1)S(1)} collective-permute-done((bf16[192,384]{1,0:T(8,128)(2,1)S(1)}, bf16[192,384]{1,0:T(8,128)(2,1)S(1)}, u32[]{:S(2)}, u32[]{:S(2)}) %collective-permute-start.4) | collective-permute-done | bytes 147488 | tf_op jit(solution)/shard_map/ppermute | solution.py:376
  20.9 3.0 %collective-permute-start.2 = (bf16[192,384]{1,0:T(8,128)(2,1)S(1)}, bf16[192,384]{1,0:T(8,128)(2,1)S(1)}, u32[]{:S(2)}, u32[]{:S(2)}) collective-permute-start(bf16[192,384]{1,0:T(8,128)(2,1)S(1)} %collective-permute-done.1.refs_2_), channel_id=1, source_target_pairs={{0,224},{32,0},{64,32},{96,64},{128,96},{160,128},{192,160},{224,1... | collective-permute-start | bytes 442376 | tf_op jit(solution)/shard_map/ppermute | solution.py:376
  23.9 2.5 %collective-permute-done.5.refs_6_ = bf16[192,384]{1,0:T(8,128)(2,1)S(1)} collective-permute-done((bf16[192,384]{1,0:T(8,128)(2,1)S(1)}, bf16[192,384]{1,0:T(8,128)(2,1)S(1)}, u32[]{:S(2)}, u32[]{:S(2)}) %collective-permute-start.5) | collective-permute-done | bytes 147488 | tf_op jit(solution)/shard_map/ppermute | solution.py:376
  26.4 3.0 %collective-permute-start.3 = (bf16[192,384]{1,0:T(8,128)(2,1)S(1)}, bf16[192,384]{1,0:T(8,128)(2,1)S(1)}, u32[]{:S(2)}, u32[]{:S(2)}) collective-permute-start(bf16[192,384]{1,0:T(8,128)(2,1)S(1)} %collective-permute-done.2.refs_3_), channel_id=1, source_target_pairs={{0,224},{32,0},{64,32},{96,64},{128,96},{160,128},{192,160},{224,1... | collective-permute-start | bytes 442376 | tf_op jit(solution)/shard_map/ppermute | solution.py:376
  29.4 2.5 %collective-permute-done.6.refs_5_ = bf16[192,384]{1,0:T(8,128)(2,1)S(1)} collective-permute-done((bf16[192,384]{1,0:T(8,128)(2,1)S(1)}, bf16[192,384]{1,0:T(8,128)(2,1)S(1)}, u32[]{:S(2)}, u32[]{:S(2)}) %collective-permute-start.6) | collective-permute-done | bytes 147488 | tf_op jit(solution)/shard_map/ppermute | solution.py:376
  31.9 0.1 shard_map.29.refs_1_.cols_ref
  32.0 4.1 %all-to-all-done = bf16[16,192,256]{2,1,0:T(8,128)(2,1)S(1)} async-done(((bf16[16,192,256]{2,1,0:T(8,128)(2,1)}), bf16[16,192,256]{2,1,0:T(8,128)(2,1)S(1)}, u32[]{:S(2)}, u32[]{:S(2)}) %all-to-all-start) | async-done | bytes 1572896 | tf_op jit(solution)/shard_map/all_to_all | solution.py:368
  36.1 4.2 %collective-permute-start.7 = (bf16[3072,256]{1,0:T(8,128)(2,1)S(1)}, bf16[3072,256]{1,0:T(8,128)(2,1)S(1)}, u32[]{:S(2)}, u32[]{:S(2)}) collective-permute-start(bf16[3072,256]{1,0:T(8,128)(2,1)S(1)} %bitcast.3), channel_id=1, source_target_pairs={{0,1},{1,0},{2,3},{3,2},{4,5},{5,4},{6,7},{7,6},{8,9},{9,8},{10,11... | collective-permute-start | bytes 4718600 | tf_op jit(solution)/shard_map/ppermute | solution.py:372
  40.3 3.1 %shard_map.30 = (bf16[3072,1536]{1,0:T(8,128)(2,1)S(1)}, f32[8,1536]{1,0:T(8,128)S(1)}) custom-call(bf16[3072,256]{1,0:T(8,128)(2,1)S(1)} %bitcast.4, bf16[1536,384]{1,0:T(8,128)(2,1)S(1)} %shard_map.29.refs_1_.cols_ref), custom_call_target="tpu_custom_call" | custom-call | flops 2415919104 | bytes 12238848 | tf_op jit(solution)/shard_map/pallas_call | solution.py:48
  43.5 3.3 %shard_map.31 = (bf16[3072,1536]{1,0:T(8,128)(2,1)S(1)}, f32[8,16,128]{2,1,0:T(8,128)S(1)}) custom-call(bf16[3072,256]{1,0:T(8,128)(2,1)S(1)} %collective-permute-done.7.refs_0_, bf16[1536,384]{1,0:T(8,128)(2,1)S(1)} %shard_map.29.refs_1_.cols_ref, f32[8,1536]{1,0:T(8,128)S(1)} %get-tuple-element.28.refs_2_), custom_call_target="tpu_custom_call" | custom-call | flops 2415919104 | bytes 12304384 | tf_op jit(solution)/shard_map/pallas_call | solution.py:48
  46.8 9.9 %all_to_all.35.sums_ref = f32[8,16,128]{2,1,0:T(8,128)S(1)} all-to-all(f32[8,16,128]{2,1,0:T(8,128)S(1)} %get-tuple-element.30), channel_id=1, replica_groups=mesh['z'=8,'x'=4,'y'=4,'core'=2] {'z'}, dimensions={0} | all-to-all | bytes 131072 | tf_op jit(solution)/shard_map/all_to_all | solution.py:368
  56.7 3.0 %shard_map.32 = (f32[16,104,128]{2,1,0:T(8,128)S(1)}, bf16[1536,128]{1,0:T(8,128)(2,1)S(1)}, f32[96,128]{1,0:T(8,128)S(1)}, f32[96,128]{1,0:T(8,128)S(1)}) custom-call(bf16[3072,1536]{1,0:T(8,128)(2,1)S(1)} %get-tuple-element.29.tile_ref, f32[8,16,128]{2,1,0:T(8,128)S(1)} %all_to_all.35.sums_ref, bf16[1536,384]{1,0:T(8,128)(2,1)S(1)} %shard_map.29.refs_1_.cols_ref), custom_call_target="tpu_custom_call" | custom-call | flops 1207959552 | bytes 12025856 | tf_op jit(solution)/shard_map/pallas_call | solution.py:48
  59.7 2.0 %collective-permute-start.8 = (f32[16,104,128]{2,1,0:T(8,128)S(1)}, f32[16,104,128]{2,1,0:T(8,128)S(1)}, u32[]{:S(2)}, u32[]{:S(2)}) collective-permute-start(f32[16,104,128]{2,1,0:T(8,128)S(1)} %get-tuple-element.32.other_ref), channel_id=1, source_target_pairs={{0,1},{1,0},{2,3},{3,2},{4,5},{5,4},{6,7},{7,6},{8,9},{9,8},{10,11... | collective-permute-start | bytes 2555912 | tf_op jit(solution)/shard_map/ppermute | solution.py:372
  61.7 2.6 %shard_map.33.own_ref = f32[16,104,128]{2,1,0:T(8,128)S(1)} custom-call(bf16[3072,1536]{1,0:T(8,128)(2,1)S(1)} %get-tuple-element.27.tile_ref, bf16[1536,128]{1,0:T(8,128)(2,1)S(1)} %get-tuple-element.31.weights_ref, f32[16,104,128]{2,1,0:T(8,128)S(1)} %get-tuple-element.32.other_ref), custom_call_target="tpu_custom_call" | custom-call | flops 1207959552 | bytes 11534336 | tf_op jit(solution)/shard_map/pallas_call | solution.py:48
  64.3 0.1 shard_map.34
  64.4 13.6 %all_to_all.36.got_ref = bf16[16,112,128]{2,1,0:T(8,128)(2,1)S(1)} all-to-all(bf16[16,112,128]{2,1,0:T(8,128)(2,1)S(1)} %shard_map.34), channel_id=1, replica_groups=mesh['z'=8,'x'=4,'y'=4,'core'=2] {'x','y'}, dimensions={0} | all-to-all | bytes 917504 | tf_op jit(solution)/shard_map/all_to_all | solution.py:368
  78.0 0.2 shard_map.35
  78.2 11.5 %all_to_all.37.got_ref = bf16[8,112,128]{2,1,0:T(8,128)(2,1)S(1)} all-to-all(bf16[8,112,128]{2,1,0:T(8,128)(2,1)S(1)} %get-tuple-element.35), channel_id=1, replica_groups=mesh['z'=8,'x'=4,'y'=4,'core'=2] {'z'}, dimensions={0} | all-to-all | bytes 458752 | tf_op jit(solution)/shard_map/all_to_all | solution.py:368
  89.7 2.7 %shard_map.36 = (f32[16,104,128]{2,1,0:T(8,128)S(1)}, bf16[1536,128]{1,0:T(8,128)(2,1)S(1)}) custom-call(bf16[3072,1536]{1,0:T(8,128)(2,1)S(1)} %get-tuple-element.29.tile_ref, bf16[8,112,128]{2,1,0:T(8,128)(2,1)S(1)} %all_to_all.37.got_ref), custom_call_target="tpu_custom_call" | custom-call | flops 1207959552 | bytes 10911744 | tf_op jit(solution)/shard_map/pallas_call | solution.py:48
  92.4 3.3 %collective-permute-start.9 = (f32[16,104,128]{2,1,0:T(8,128)S(1)}, f32[16,104,128]{2,1,0:T(8,128)S(1)}, u32[]{:S(2)}, u32[]{:S(2)}) collective-permute-start(f32[16,104,128]{2,1,0:T(8,128)S(1)} %get-tuple-element.37.other_ref), channel_id=1, source_target_pairs={{0,1},{1,0},{2,3},{3,2},{4,5},{5,4},{6,7},{7,6},{8,9},{9,8},{10,11... | collective-permute-start | bytes 2555912 | tf_op jit(solution)/shard_map/ppermute | solution.py:372
  95.7 2.6 %shard_map.37.own_ref = f32[16,104,128]{2,1,0:T(8,128)S(1)} custom-call(bf16[3072,1536]{1,0:T(8,128)(2,1)S(1)} %get-tuple-element.27.tile_ref, bf16[1536,128]{1,0:T(8,128)(2,1)S(1)} %get-tuple-element.36.weights_ref, f32[16,104,128]{2,1,0:T(8,128)S(1)} %get-tuple-element.37.other_ref), custom_call_target="tpu_custom_call" | custom-call | flops 1207959552 | bytes 11534336 | tf_op jit(solution)/shard_map/pallas_call | solution.py:48
  98.3 1.2 shard_map.38
  99.5 13.5 %all_to_all.38.got_ref = bf16[16,112,128]{2,1,0:T(8,128)(2,1)S(1)} all-to-all(bf16[16,112,128]{2,1,0:T(8,128)(2,1)S(1)} %shard_map.38), channel_id=1, replica_groups=mesh['z'=8,'x'=4,'y'=4,'core'=2] {'x','y'}, dimensions={0} | all-to-all | bytes 917504 | tf_op jit(solution)/shard_map/all_to_all | solution.py:368
  112.9 0.7 shard_map.39
  113.6 14.9 %all_to_all.39.got_ref = f32[16,24,128]{2,1,0:T(8,128)S(1)} all-to-all(f32[16,24,128]{2,1,0:T(8,128)S(1)} %get-tuple-element.39), channel_id=1, replica_groups=mesh['z'=8,'x'=4,'y'=4,'core'=2] {'z','core'}, dimensions={0} | all-to-all | bytes 393216 | tf_op jit(solution)/shard_map/all_to_all | solution.py:368
  128.6 10.6 %all_to_all.40.got_ref = f32[16,24,128]{2,1,0:T(8,128)S(1)} all-to-all(f32[16,24,128]{2,1,0:T(8,128)S(1)} %shard_map.40), channel_id=1, replica_groups=mesh['z'=8,'x'=4,'y'=4,'core'=2] {'x','y'}, dimensions={0} | all-to-all | bytes 393216 | tf_op jit(solution)/shard_map/all_to_all | solution.py:368
  139.1 2.7 %shard_map.41 = f32[64,192]{1,0:T(8,128)} custom-call(f32[16,24,128]{2,1,0:T(8,128)S(1)} %all_to_all.40.got_ref, f32[96,128]{1,0:T(8,128)S(1)} %get-tuple-element.40.vectors_ref), custom_call_target="tpu_custom_call" | custom-call | bytes 294912 | tf_op jit(solution)/shard_map/pallas_call | solution.py:48
  (10 shorter events, 0.1 us)
Async XLA Ops:
  2.3 13.3 %collective-permute-start = (bf16[192,384]{1,0:T(8,128)(2,1)S(1)}, bf16[192,384]{1,0:T(8,128)(2,1)S(1)}, u32[]{:S(2)}, u32[]{:S(2)}) collective-permute-start(bf16[192,384]{1,0:T(8,128)(2,1)S(1)} %get-tuple-element.24.refs_0_), channel_id=1, source_target_pairs={{0,224},{32,0},{64,32},{96,64},{128,96},{160,128},{192,160},{224,1... | collective-permute-start | bytes 442376 | tf_op jit(solution)/shard_map/ppermute | solution.py:376
  8.8 27.3 %all-to-all-start = ((bf16[16,192,256]{2,1,0:T(8,128)(2,1)}), bf16[16,192,256]{2,1,0:T(8,128)(2,1)S(1)}, u32[]{:S(2)}, u32[]{:S(2)}) async-start(bf16[16,192,256]{2,1,0:T(8,128)(2,1)} %get-tuple-element.23), calls=%async_computation | async-start | bytes 3145728 | tf_op jit(solution)/shard_map/all_to_all | solution.py:368
  15.6 5.3 %collective-permute-start.4 = (bf16[192,384]{1,0:T(8,128)(2,1)S(1)}, bf16[192,384]{1,0:T(8,128)(2,1)S(1)}, u32[]{:S(2)}, u32[]{:S(2)}) collective-permute-start(bf16[192,384]{1,0:T(8,128)(2,1)S(1)} %get-tuple-element.24.refs_0_), channel_id=1, source_target_pairs={{0,32},{32,64},{64,96},{96,128},{128,160},{160,192},{192,224},{224... | collective-permute-start | bytes 442376 | tf_op jit(solution)/shard_map/ppermute | solution.py:376
  15.7 5.2 %collective-permute-start.1 = (bf16[192,384]{1,0:T(8,128)(2,1)S(1)}, bf16[192,384]{1,0:T(8,128)(2,1)S(1)}, u32[]{:S(2)}, u32[]{:S(2)}) collective-permute-start(bf16[192,384]{1,0:T(8,128)(2,1)S(1)} %collective-permute-done.refs_1_), channel_id=1, source_target_pairs={{0,224},{32,0},{64,32},{96,64},{128,96},{160,128},{192,160},{224,1... | collective-permute-start | bytes 442376 | tf_op jit(solution)/shard_map/ppermute | solution.py:376
  20.9 5.5 %collective-permute-start.5 = (bf16[192,384]{1,0:T(8,128)(2,1)S(1)}, bf16[192,384]{1,0:T(8,128)(2,1)S(1)}, u32[]{:S(2)}, u32[]{:S(2)}) collective-permute-start(bf16[192,384]{1,0:T(8,128)(2,1)S(1)} %collective-permute-done.4.refs_7_), channel_id=1, source_target_pairs={{0,32},{32,64},{64,96},{96,128},{128,160},{160,192},{192,224},{224... | collective-permute-start | bytes 442376 | tf_op jit(solution)/shard_map/ppermute | solution.py:376
  20.9 5.5 %collective-permute-start.2 = (bf16[192,384]{1,0:T(8,128)(2,1)S(1)}, bf16[192,384]{1,0:T(8,128)(2,1)S(1)}, u32[]{:S(2)}, u32[]{:S(2)}) collective-permute-start(bf16[192,384]{1,0:T(8,128)(2,1)S(1)} %collective-permute-done.1.refs_2_), channel_id=1, source_target_pairs={{0,224},{32,0},{64,32},{96,64},{128,96},{160,128},{192,160},{224,1... | collective-permute-start | bytes 442376 | tf_op jit(solution)/shard_map/ppermute | solution.py:376
  26.4 5.5 %collective-permute-start.6 = (bf16[192,384]{1,0:T(8,128)(2,1)S(1)}, bf16[192,384]{1,0:T(8,128)(2,1)S(1)}, u32[]{:S(2)}, u32[]{:S(2)}) collective-permute-start(bf16[192,384]{1,0:T(8,128)(2,1)S(1)} %collective-permute-done.5.refs_6_), channel_id=1, source_target_pairs={{0,32},{32,64},{64,96},{96,128},{128,160},{160,192},{192,224},{224... | collective-permute-start | bytes 442376 | tf_op jit(solution)/shard_map/ppermute | solution.py:376
  26.4 5.5 %collective-permute-start.3 = (bf16[192,384]{1,0:T(8,128)(2,1)S(1)}, bf16[192,384]{1,0:T(8,128)(2,1)S(1)}, u32[]{:S(2)}, u32[]{:S(2)}) collective-permute-start(bf16[192,384]{1,0:T(8,128)(2,1)S(1)} %collective-permute-done.2.refs_3_), channel_id=1, source_target_pairs={{0,224},{32,0},{64,32},{96,64},{128,96},{160,128},{192,160},{224,1... | collective-permute-start | bytes 442376 | tf_op jit(solution)/shard_map/ppermute | solution.py:376
  36.1 7.4 %collective-permute-start.7 = (bf16[3072,256]{1,0:T(8,128)(2,1)S(1)}, bf16[3072,256]{1,0:T(8,128)(2,1)S(1)}, u32[]{:S(2)}, u32[]{:S(2)}) collective-permute-start(bf16[3072,256]{1,0:T(8,128)(2,1)S(1)} %bitcast.3), channel_id=1, source_target_pairs={{0,1},{1,0},{2,3},{3,2},{4,5},{5,4},{6,7},{7,6},{8,9},{9,8},{10,11... | collective-permute-start | bytes 4718600 | tf_op jit(solution)/shard_map/ppermute | solution.py:372
  59.7 4.6 %collective-permute-start.8 = (f32[16,104,128]{2,1,0:T(8,128)S(1)}, f32[16,104,128]{2,1,0:T(8,128)S(1)}, u32[]{:S(2)}, u32[]{:S(2)}) collective-permute-start(f32[16,104,128]{2,1,0:T(8,128)S(1)} %get-tuple-element.32.other_ref), channel_id=1, source_target_pairs={{0,1},{1,0},{2,3},{3,2},{4,5},{5,4},{6,7},{7,6},{8,9},{9,8},{10,11... | collective-permute-start | bytes 2555912 | tf_op jit(solution)/shard_map/ppermute | solution.py:372
  92.4 5.9 %collective-permute-start.9 = (f32[16,104,128]{2,1,0:T(8,128)S(1)}, f32[16,104,128]{2,1,0:T(8,128)S(1)}, u32[]{:S(2)}, u32[]{:S(2)}) collective-permute-start(f32[16,104,128]{2,1,0:T(8,128)S(1)} %get-tuple-element.37.other_ref), channel_id=1, source_target_pairs={{0,1},{1,0},{2,3},{3,2},{4,5},{5,4},{6,7},{7,6},{8,9},{9,8},{10,11... | collective-permute-start | bytes 2555912 | tf_op jit(solution)/shard_map/ppermute | solution.py:372

commit v9 on v8

--- a/solution.py
+++ b/solution.py
@@ -25,8 +25,8 @@
 K = 64
 COLUMNS = DEPTH * DOCS
 ROWS = PEERS * DOCS
-ROW_BLOCK = 3072
-COLUMN_BLOCK = 768
+ROW_BLOCK = 768
+COLUMN_BLOCK = 256
 LANES = 128
 PIVOTS = 8
 SAMPLE = 8
@@ -115,20 +115,22 @@
         rows_ref, cols_ref, tile_ref, sums_ref, acc = refs
         acc[...] = jnp.zeros_like(acc)
 
-    def block(i, _):
-        at = pl.ds(pl.multiple_of(i * ROW_BLOCK, ROW_BLOCK), ROW_BLOCK)
-        rows = rows_ref[at, :]
-        for c in range(COLUMNS // COLUMN_BLOCK):
-            where = slice(c * COLUMN_BLOCK, (c + 1) * COLUMN_BLOCK)
+    for c in range(COLUMNS // COLUMN_BLOCK):
+        where = slice(c * COLUMN_BLOCK, (c + 1) * COLUMN_BLOCK)
+        sums = jnp.zeros((8, COLUMN_BLOCK), f32)
+        for r in range(ROWS // ROW_BLOCK):
+            at = slice(r * ROW_BLOCK, (r + 1) * ROW_BLOCK)
             scores = lax.dot_general(
-                rows, cols_ref[where, :E], (((1,), (1,)), ((), ())), preferred_element_type=f32
+                rows_ref[at, :],
+                cols_ref[where, :E],
+                (((1,), (1,)), ((), ())),
+                preferred_element_type=f32,
             )
             entry = jnp.tanh(scores - sharpness * threshold / 2) + 1.0
             tile_ref[at, where] = entry.astype(bf16)
-            acc[:, where] += jnp.sum(entry.reshape(ROW_BLOCK // 8, 8, COLUMN_BLOCK), axis=0)
-        return 0
-
-    lax.fori_loop(0, ROWS // ROW_BLOCK, block, 0)
+            sums += jnp.sum(entry.reshape(ROW_BLOCK // 8, 8, COLUMN_BLOCK), axis=0)
+        acc[:, where] += sums
+
     if last:
         total = 0.5 * jnp.sum(acc[...], axis=0, keepdims=True)
         sums_ref[...] = jnp.zeros_like(sums_ref)

time: 142 us -> 142 us (level)
  no operation moved by 1% of the time
where the time goes in v9:
time: 142 us
  blocking collectives  74 us (52%)
  starting transfers between devices  31.4 us (22%)
  Pallas kernels  24.6 us (17%)
  waiting for transfers between devices  11.7 us (8%)
    all_to_all x6, blocking collectives, exchange(): return lax.all_to_all(value, axes, 0, 0, tiled=True)  74 us
    pallas_call x14, Pallas kernels, call(): pl.pallas_call(kernel, out_shape=tuple(outs), in_specs=[pl.BlockSpec(memo...  24.6 us
    ppermute x7, starting transfers between devices, shift(): lax.ppermute(value, 'z', [(i, (i + step) % DEPTH) for i in range(DEPTH)])  15.2 us
    ppermute x3, starting transfers between devices, swap_core(): return lax.ppermute(value, 'core', [(0, 1), (1, 0)])  9.47 us
    ppermute x7, waiting for transfers between devices, shift(): lax.ppermute(value, 'z', [(i, (i + step) % DEPTH) for i in range(DEPTH)])  7.58 us
    all_to_all x1, starting transfers between devices, exchange(): return lax.all_to_all(value, axes, 0, 0, tiled=True)  6.75 us
    all_to_all x1, waiting for transfers between devices, exchange(): return lax.all_to_all(value, axes, 0, 0, tiled=True)  4.12 us
  transfers between devices with their start and end apart: 11, of which 4 were waited for; matrix products, arithmetic and copies ran while one was open for 0% of the time, Pallas kernels for 6%

profile of v9, /device:TPU:1, one launch (start us, length us, event | category | flops | bytes accessed | tf_op | source)
XLA Modules:
  0.0 141.8 jit_solution(2028519323966689958)
XLA Ops:
  0.0 2.3 %shard_map.28 = (bf16[192,384]{1,0:T(8,128)(2,1)S(1)}, bf16[16,192,256]{2,1,0:T(8,128)(2,1)}) custom-call(bf16[192,256]{1,0:T(8,128)(2,1)} %emb_hbm.1, f32[64,192]{1,0:T(8,128)} %bitcast.5), custom_call_target="tpu_custom_call" | custom-call | bytes 1867776 | tf_op jit(solution)/shard_map/pallas_call | solution.py:48
  2.3 6.5 %collective-permute-start = (bf16[192,384]{1,0:T(8,128)(2,1)S(1)}, bf16[192,384]{1,0:T(8,128)(2,1)S(1)}, u32[]{:S(2)}, u32[]{:S(2)}) collective-permute-start(bf16[192,384]{1,0:T(8,128)(2,1)S(1)} %get-tuple-element.24.refs_0_), channel_id=1, source_target_pairs={{0,224},{32,0},{64,32},{96,64},{128,96},{160,128},{192,160},{224,1... | collective-permute-start | bytes 442376 | tf_op jit(solution)/shard_map/ppermute | solution.py:378
  8.8 6.8 %all-to-all-start = ((bf16[16,192,256]{2,1,0:T(8,128)(2,1)}), bf16[16,192,256]{2,1,0:T(8,128)(2,1)S(1)}, u32[]{:S(2)}, u32[]{:S(2)}) async-start(bf16[16,192,256]{2,1,0:T(8,128)(2,1)} %get-tuple-element.23), calls=%async_computation | async-start | bytes 3145728 | tf_op jit(solution)/shard_map/all_to_all | solution.py:370
  15.6 0.1 collective-permute-start.4
  15.7 2.7 %collective-permute-start.1 = (bf16[192,384]{1,0:T(8,128)(2,1)S(1)}, bf16[192,384]{1,0:T(8,128)(2,1)S(1)}, u32[]{:S(2)}, u32[]{:S(2)}) collective-permute-start(bf16[192,384]{1,0:T(8,128)(2,1)S(1)} %collective-permute-done.refs_1_), channel_id=1, source_target_pairs={{0,224},{32,0},{64,32},{96,64},{128,96},{160,128},{192,160},{224,1... | collective-permute-start | bytes 442376 | tf_op jit(solution)/shard_map/ppermute | solution.py:378
  18.4 2.5 %collective-permute-done.4.refs_7_ = bf16[192,384]{1,0:T(8,128)(2,1)S(1)} collective-permute-done((bf16[192,384]{1,0:T(8,128)(2,1)S(1)}, bf16[192,384]{1,0:T(8,128)(2,1)S(1)}, u32[]{:S(2)}, u32[]{:S(2)}) %collective-permute-start.4) | collective-permute-done | bytes 147488 | tf_op jit(solution)/shard_map/ppermute | solution.py:378
  20.9 3.0 %collective-permute-start.2 = (bf16[192,384]{1,0:T(8,128)(2,1)S(1)}, bf16[192,384]{1,0:T(8,128)(2,1)S(1)}, u32[]{:S(2)}, u32[]{:S(2)}) collective-permute-start(bf16[192,384]{1,0:T(8,128)(2,1)S(1)} %collective-permute-done.1.refs_2_), channel_id=1, source_target_pairs={{0,224},{32,0},{64,32},{96,64},{128,96},{160,128},{192,160},{224,1... | collective-permute-start | bytes 442376 | tf_op jit(solution)/shard_map/ppermute | solution.py:378
  23.9 2.5 %collective-permute-done.5.refs_6_ = bf16[192,384]{1,0:T(8,128)(2,1)S(1)} collective-permute-done((bf16[192,384]{1,0:T(8,128)(2,1)S(1)}, bf16[192,384]{1,0:T(8,128)(2,1)S(1)}, u32[]{:S(2)}, u32[]{:S(2)}) %collective-permute-start.5) | collective-permute-done | bytes 147488 | tf_op jit(solution)/shard_map/ppermute | solution.py:378
  26.4 3.0 %collective-permute-start.3 = (bf16[192,384]{1,0:T(8,128)(2,1)S(1)}, bf16[192,384]{1,0:T(8,128)(2,1)S(1)}, u32[]{:S(2)}, u32[]{:S(2)}) collective-permute-start(bf16[192,384]{1,0:T(8,128)(2,1)S(1)} %collective-permute-done.2.refs_3_), channel_id=1, source_target_pairs={{0,224},{32,0},{64,32},{96,64},{128,96},{160,128},{192,160},{224,1... | collective-permute-start | bytes 442376 | tf_op jit(solution)/shard_map/ppermute | solution.py:378
  29.4 2.5 %collective-permute-done.6.refs_5_ = bf16[192,384]{1,0:T(8,128)(2,1)S(1)} collective-permute-done((bf16[192,384]{1,0:T(8,128)(2,1)S(1)}, bf16[192,384]{1,0:T(8,128)(2,1)S(1)}, u32[]{:S(2)}, u32[]{:S(2)}) %collective-permute-start.6) | collective-permute-done | bytes 147488 | tf_op jit(solution)/shard_map/ppermute | solution.py:378
  31.9 0.1 shard_map.29.refs_1_.cols_ref
  32.0 4.1 %all-to-all-done = bf16[16,192,256]{2,1,0:T(8,128)(2,1)S(1)} async-done(((bf16[16,192,256]{2,1,0:T(8,128)(2,1)}), bf16[16,192,256]{2,1,0:T(8,128)(2,1)S(1)}, u32[]{:S(2)}, u32[]{:S(2)}) %all-to-all-start) | async-done | bytes 1572896 | tf_op jit(solution)/shard_map/all_to_all | solution.py:370
  36.1 4.2 %collective-permute-start.7 = (bf16[3072,256]{1,0:T(8,128)(2,1)S(1)}, bf16[3072,256]{1,0:T(8,128)(2,1)S(1)}, u32[]{:S(2)}, u32[]{:S(2)}) collective-permute-start(bf16[3072,256]{1,0:T(8,128)(2,1)S(1)} %bitcast.3), channel_id=1, source_target_pairs={{0,1},{1,0},{2,3},{3,2},{4,5},{5,4},{6,7},{7,6},{8,9},{9,8},{10,11... | collective-permute-start | bytes 4718600 | tf_op jit(solution)/shard_map/ppermute | solution.py:374
  40.3 3.2 %shard_map.30 = (bf16[3072,1536]{1,0:T(8,128)(2,1)S(1)}, f32[8,1536]{1,0:T(8,128)S(1)}) custom-call(bf16[3072,256]{1,0:T(8,128)(2,1)S(1)} %bitcast.4, bf16[1536,384]{1,0:T(8,128)(2,1)S(1)} %shard_map.29.refs_1_.cols_ref), custom_call_target="tpu_custom_call" | custom-call | flops 2415919104 | bytes 12238848 | tf_op jit(solution)/shard_map/pallas_call | solution.py:48
  43.5 3.2 %shard_map.31 = (bf16[3072,1536]{1,0:T(8,128)(2,1)S(1)}, f32[8,16,128]{2,1,0:T(8,128)S(1)}) custom-call(bf16[3072,256]{1,0:T(8,128)(2,1)S(1)} %collective-permute-done.7.refs_0_, bf16[1536,384]{1,0:T(8,128)(2,1)S(1)} %shard_map.29.refs_1_.cols_ref, f32[8,1536]{1,0:T(8,128)S(1)} %get-tuple-element.28.refs_2_), custom_call_target="tpu_custom_call" | custom-call | flops 2415919104 | bytes 12304384 | tf_op jit(solution)/shard_map/pallas_call | solution.py:48
  46.8 9.9 %all_to_all.35.sums_ref = f32[8,16,128]{2,1,0:T(8,128)S(1)} all-to-all(f32[8,16,128]{2,1,0:T(8,128)S(1)} %get-tuple-element.30), channel_id=1, replica_groups=mesh['z'=8,'x'=4,'y'=4,'core'=2] {'z'}, dimensions={0} | all-to-all | bytes 131072 | tf_op jit(solution)/shard_map/all_to_all | solution.py:370
  56.7 3.0 %shard_map.32 = (f32[16,104,128]{2,1,0:T(8,128)S(1)}, bf16[1536,128]{1,0:T(8,128)(2,1)S(1)}, f32[96,128]{1,0:T(8,128)S(1)}, f32[96,128]{1,0:T(8,128)S(1)}) custom-call(bf16[3072,1536]{1,0:T(8,128)(2,1)S(1)} %get-tuple-element.29.tile_ref, f32[8,16,128]{2,1,0:T(8,128)S(1)} %all_to_all.35.sums_ref, bf16[1536,384]{1,0:T(8,128)(2,1)S(1)} %shard_map.29.refs_1_.cols_ref), custom_call_target="tpu_custom_call" | custom-call | flops 1207959552 | bytes 12025856 | tf_op jit(solution)/shard_map/pallas_call | solution.py:48
  59.7 2.0 %collective-permute-start.8 = (f32[16,104,128]{2,1,0:T(8,128)S(1)}, f32[16,104,128]{2,1,0:T(8,128)S(1)}, u32[]{:S(2)}, u32[]{:S(2)}) collective-permute-start(f32[16,104,128]{2,1,0:T(8,128)S(1)} %get-tuple-element.32.other_ref), channel_id=1, source_target_pairs={{0,1},{1,0},{2,3},{3,2},{4,5},{5,4},{6,7},{7,6},{8,9},{9,8},{10,11... | collective-permute-start | bytes 2555912 | tf_op jit(solution)/shard_map/ppermute | solution.py:374
  61.6 2.6 %shard_map.33.own_ref = f32[16,104,128]{2,1,0:T(8,128)S(1)} custom-call(bf16[3072,1536]{1,0:T(8,128)(2,1)S(1)} %get-tuple-element.27.tile_ref, bf16[1536,128]{1,0:T(8,128)(2,1)S(1)} %get-tuple-element.31.weights_ref, f32[16,104,128]{2,1,0:T(8,128)S(1)} %get-tuple-element.32.other_ref), custom_call_target="tpu_custom_call" | custom-call | flops 1207959552 | bytes 11534336 | tf_op jit(solution)/shard_map/pallas_call | solution.py:48
  64.3 0.1 shard_map.34
  64.4 13.7 %all_to_all.36.got_ref = bf16[16,112,128]{2,1,0:T(8,128)(2,1)S(1)} all-to-all(bf16[16,112,128]{2,1,0:T(8,128)(2,1)S(1)} %shard_map.34), channel_id=1, replica_groups=mesh['z'=8,'x'=4,'y'=4,'core'=2] {'x','y'}, dimensions={0} | all-to-all | bytes 917504 | tf_op jit(solution)/shard_map/all_to_all | solution.py:370
  78.0 0.2 shard_map.35
  78.2 11.5 %all_to_all.37.got_ref = bf16[8,112,128]{2,1,0:T(8,128)(2,1)S(1)} all-to-all(bf16[8,112,128]{2,1,0:T(8,128)(2,1)S(1)} %get-tuple-element.35), channel_id=1, replica_groups=mesh['z'=8,'x'=4,'y'=4,'core'=2] {'z'}, dimensions={0} | all-to-all | bytes 458752 | tf_op jit(solution)/shard_map/all_to_all | solution.py:370
  89.7 2.7 %shard_map.36 = (f32[16,104,128]{2,1,0:T(8,128)S(1)}, bf16[1536,128]{1,0:T(8,128)(2,1)S(1)}) custom-call(bf16[3072,1536]{1,0:T(8,128)(2,1)S(1)} %get-tuple-element.29.tile_ref, bf16[8,112,128]{2,1,0:T(8,128)(2,1)S(1)} %all_to_all.37.got_ref), custom_call_target="tpu_custom_call" | custom-call | flops 1207959552 | bytes 10911744 | tf_op jit(solution)/shard_map/pallas_call | solution.py:48
  92.4 3.3 %collective-permute-start.9 = (f32[16,104,128]{2,1,0:T(8,128)S(1)}, f32[16,104,128]{2,1,0:T(8,128)S(1)}, u32[]{:S(2)}, u32[]{:S(2)}) collective-permute-start(f32[16,104,128]{2,1,0:T(8,128)S(1)} %get-tuple-element.37.other_ref), channel_id=1, source_target_pairs={{0,1},{1,0},{2,3},{3,2},{4,5},{5,4},{6,7},{7,6},{8,9},{9,8},{10,11... | collective-permute-start | bytes 2555912 | tf_op jit(solution)/shard_map/ppermute | solution.py:374
  95.7 2.6 %shard_map.37.own_ref = f32[16,104,128]{2,1,0:T(8,128)S(1)} custom-call(bf16[3072,1536]{1,0:T(8,128)(2,1)S(1)} %get-tuple-element.27.tile_ref, bf16[1536,128]{1,0:T(8,128)(2,1)S(1)} %get-tuple-element.36.weights_ref, f32[16,104,128]{2,1,0:T(8,128)S(1)} %get-tuple-element.37.other_ref), custom_call_target="tpu_custom_call" | custom-call | flops 1207959552 | bytes 11534336 | tf_op jit(solution)/shard_map/pallas_call | solution.py:48
  98.3 1.2 shard_map.38
  99.5 13.5 %all_to_all.38.got_ref = bf16[16,112,128]{2,1,0:T(8,128)(2,1)S(1)} all-to-all(bf16[16,112,128]{2,1,0:T(8,128)(2,1)S(1)} %shard_map.38), channel_id=1, replica_groups=mesh['z'=8,'x'=4,'y'=4,'core'=2] {'x','y'}, dimensions={0} | all-to-all | bytes 917504 | tf_op jit(solution)/shard_map/all_to_all | solution.py:370
  112.9 0.6 shard_map.39
  113.6 14.9 %all_to_all.39.got_ref = f32[16,24,128]{2,1,0:T(8,128)S(1)} all-to-all(f32[16,24,128]{2,1,0:T(8,128)S(1)} %get-tuple-element.39), channel_id=1, replica_groups=mesh['z'=8,'x'=4,'y'=4,'core'=2] {'z','core'}, dimensions={0} | all-to-all | bytes 393216 | tf_op jit(solution)/shard_map/all_to_all | solution.py:370
  128.5 10.5 %all_to_all.40.got_ref = f32[16,24,128]{2,1,0:T(8,128)S(1)} all-to-all(f32[16,24,128]{2,1,0:T(8,128)S(1)} %shard_map.40), channel_id=1, replica_groups=mesh['z'=8,'x'=4,'y'=4,'core'=2] {'x','y'}, dimensions={0} | all-to-all | bytes 393216 | tf_op jit(solution)/shard_map/all_to_all | solution.py:370
  139.1 2.7 %shard_map.41 = f32[64,192]{1,0:T(8,128)} custom-call(f32[16,24,128]{2,1,0:T(8,128)S(1)} %all_to_all.40.got_ref, f32[96,128]{1,0:T(8,128)S(1)} %get-tuple-element.40.vectors_ref), custom_call_target="tpu_custom_call" | custom-call | bytes 294912 | tf_op jit(solution)/shard_map/pallas_call | solution.py:48
  (10 shorter events, 0.1 us)
Async XLA Ops:
  2.3 13.3 %collective-permute-start = (bf16[192,384]{1,0:T(8,128)(2,1)S(1)}, bf16[192,384]{1,0:T(8,128)(2,1)S(1)}, u32[]{:S(2)}, u32[]{:S(2)}) collective-permute-start(bf16[192,384]{1,0:T(8,128)(2,1)S(1)} %get-tuple-element.24.refs_0_), channel_id=1, source_target_pairs={{0,224},{32,0},{64,32},{96,64},{128,96},{160,128},{192,160},{224,1... | collective-permute-start | bytes 442376 | tf_op jit(solution)/shard_map/ppermute | solution.py:378
  8.8 27.3 %all-to-all-start = ((bf16[16,192,256]{2,1,0:T(8,128)(2,1)}), bf16[16,192,256]{2,1,0:T(8,128)(2,1)S(1)}, u32[]{:S(2)}, u32[]{:S(2)}) async-start(bf16[16,192,256]{2,1,0:T(8,128)(2,1)} %get-tuple-element.23), calls=%async_computation | async-start | bytes 3145728 | tf_op jit(solution)/shard_map/all_to_all | solution.py:370
  15.6 5.3 %collective-permute-start.4 = (bf16[192,384]{1,0:T(8,128)(2,1)S(1)}, bf16[192,384]{1,0:T(8,128)(2,1)S(1)}, u32[]{:S(2)}, u32[]{:S(2)}) collective-permute-start(bf16[192,384]{1,0:T(8,128)(2,1)S(1)} %get-tuple-element.24.refs_0_), channel_id=1, source_target_pairs={{0,32},{32,64},{64,96},{96,128},{128,160},{160,192},{192,224},{224... | collective-permute-start | bytes 442376 | tf_op jit(solution)/shard_map/ppermute | solution.py:378
  15.7 5.2 %collective-permute-start.1 = (bf16[192,384]{1,0:T(8,128)(2,1)S(1)}, bf16[192,384]{1,0:T(8,128)(2,1)S(1)}, u32[]{:S(2)}, u32[]{:S(2)}) collective-permute-start(bf16[192,384]{1,0:T(8,128)(2,1)S(1)} %collective-permute-done.refs_1_), channel_id=1, source_target_pairs={{0,224},{32,0},{64,32},{96,64},{128,96},{160,128},{192,160},{224,1... | collective-permute-start | bytes 442376 | tf_op jit(solution)/shard_map/ppermute | solution.py:378
  20.9 5.5 %collective-permute-start.5 = (bf16[192,384]{1,0:T(8,128)(2,1)S(1)}, bf16[192,384]{1,0:T(8,128)(2,1)S(1)}, u32[]{:S(2)}, u32[]{:S(2)}) collective-permute-start(bf16[192,384]{1,0:T(8,128)(2,1)S(1)} %collective-permute-done.4.refs_7_), channel_id=1, source_target_pairs={{0,32},{32,64},{64,96},{96,128},{128,160},{160,192},{192,224},{224... | collective-permute-start | bytes 442376 | tf_op jit(solution)/shard_map/ppermute | solution.py:378
  20.9 5.5 %collective-permute-start.2 = (bf16[192,384]{1,0:T(8,128)(2,1)S(1)}, bf16[192,384]{1,0:T(8,128)(2,1)S(1)}, u32[]{:S(2)}, u32[]{:S(2)}) collective-permute-start(bf16[192,384]{1,0:T(8,128)(2,1)S(1)} %collective-permute-done.1.refs_2_), channel_id=1, source_target_pairs={{0,224},{32,0},{64,32},{96,64},{128,96},{160,128},{192,160},{224,1... | collective-permute-start | bytes 442376 | tf_op jit(solution)/shard_map/ppermute | solution.py:378
  26.4 5.5 %collective-permute-start.6 = (bf16[192,384]{1,0:T(8,128)(2,1)S(1)}, bf16[192,384]{1,0:T(8,128)(2,1)S(1)}, u32[]{:S(2)}, u32[]{:S(2)}) collective-permute-start(bf16[192,384]{1,0:T(8,128)(2,1)S(1)} %collective-permute-done.5.refs_6_), channel_id=1, source_target_pairs={{0,32},{32,64},{64,96},{96,128},{128,160},{160,192},{192,224},{224... | collective-permute-start | bytes 442376 | tf_op jit(solution)/shard_map/ppermute | solution.py:378
  26.4 5.5 %collective-permute-start.3 = (bf16[192,384]{1,0:T(8,128)(2,1)S(1)}, bf16[192,384]{1,0:T(8,128)(2,1)S(1)}, u32[]{:S(2)}, u32[]{:S(2)}) collective-permute-start(bf16[192,384]{1,0:T(8,128)(2,1)S(1)} %collective-permute-done.2.refs_3_), channel_id=1, source_target_pairs={{0,224},{32,0},{64,32},{96,64},{128,96},{160,128},{192,160},{224,1... | collective-permute-start | bytes 442376 | tf_op jit(solution)/shard_map/ppermute | solution.py:378
  36.1 7.4 %collective-permute-start.7 = (bf16[3072,256]{1,0:T(8,128)(2,1)S(1)}, bf16[3072,256]{1,0:T(8,128)(2,1)S(1)}, u32[]{:S(2)}, u32[]{:S(2)}) collective-permute-start(bf16[3072,256]{1,0:T(8,128)(2,1)S(1)} %bitcast.3), channel_id=1, source_target_pairs={{0,1},{1,0},{2,3},{3,2},{4,5},{5,4},{6,7},{7,6},{8,9},{9,8},{10,11... | collective-permute-start | bytes 4718600 | tf_op jit(solution)/shard_map/ppermute | solution.py:374
  59.7 4.6 %collective-permute-start.8 = (f32[16,104,128]{2,1,0:T(8,128)S(1)}, f32[16,104,128]{2,1,0:T(8,128)S(1)}, u32[]{:S(2)}, u32[]{:S(2)}) collective-permute-start(f32[16,104,128]{2,1,0:T(8,128)S(1)} %get-tuple-element.32.other_ref), channel_id=1, source_target_pairs={{0,1},{1,0},{2,3},{3,2},{4,5},{5,4},{6,7},{7,6},{8,9},{9,8},{10,11... | collective-permute-start | bytes 2555912 | tf_op jit(solution)/shard_map/ppermute | solution.py:374
  92.4 5.9 %collective-permute-start.9 = (f32[16,104,128]{2,1,0:T(8,128)S(1)}, f32[16,104,128]{2,1,0:T(8,128)S(1)}, u32[]{:S(2)}, u32[]{:S(2)}) collective-permute-start(f32[16,104,128]{2,1,0:T(8,128)S(1)} %get-tuple-element.37.other_ref), channel_id=1, source_target_pairs={{0,1},{1,0},{2,3},{3,2},{4,5},{5,4},{6,7},{7,6},{8,9},{9,8},{10,11... | collective-permute-start | bytes 2555912 | tf_op jit(solution)/shard_map/ppermute | solution.py:374
